TPU v7x, 32 devices: a whole 2x2x4 slice. The times are simulated.
32 devices in a mesh: zslab: 4 (over y, x), xband: 8 (over z, core).
Axes of the slice: x: 2, y: 2, z: 4, core: 2. Of those that a mesh axis runs over, the one named last changes fastest.
Arguments:
- volume: float32 [8, 128, 512], P('xband', 'zslab'), may hold values from 0.2 to 1.8
- measured: float32 [8, 128, 512], P('xband', 'zslab'), may hold values from 1.6 to 14.4
- magnification: float32 [8, 8], P(None, 'xband'), may hold values from 1.25 to 2
- shift_y: int32 [8, 8], P(None, 'xband'), may hold values from -32 to 32
- shift_z: int32 [8, 8], P(None, 'xband'), may hold values from -4 to 4
Outputs:
- residual: float32 [8, 128, 512], P('xband', 'zslab')
- correction: float32 [8, 128, 512], P('xband', 'zslab')
All inputs are finite; a program needn't handle non-finite values.
Results may differ from a plain program's by a relative error of at most 0.0003.
Values sent between devices are 32-bit elements; how exact they have to be, the bound alone decides.
No kernel may reach another device: no remote copies, remote signals or barrier semaphores. Data moves between devices by JAX's collectives and lax.ppermute only.
A program may use at most 64 MiB of HBM per device.

v0:
```python
import math

import jax
import jax.numpy as jnp
from jax import lax
from jax.sharding import PartitionSpec as P

HALO = 4


def passed_along(x, axis, by):
    devices = lax.axis_size(axis)
    pairs = [(i, i + by) for i in range(devices) if 0 <= i + by < devices]
    return lax.ppermute(x, axis, pairs)


def extended_2(x, sides, width):
    for axis, dim in sides:
        devices, length = (lax.axis_size(axis), x.shape[dim])
        up = [(i, (i + 1) % devices) for i in range(devices - 1)]
        down = [(j, i) for i, j in up]
        last = lax.slice_in_dim(x, length - width, length, axis=dim)
        first = lax.slice_in_dim(x, 0, width, axis=dim)
        before = lax.ppermute(last, axis, up)
        after = lax.ppermute(first, axis, down)
        x = jnp.concatenate([before, x, after], axis=dim)
    return x


def hat_tables(magnification, shift_y, width):
    columns = jnp.arange(width, dtype=jnp.float32)
    centre = (width - 1) / 2.0
    target = (
        (columns[None, None, :] - centre) / magnification[:, :, None]
        + centre
        + shift_y.astype(jnp.float32)[:, :, None]
    )
    return jnp.maximum(0.0, 1.0 - jnp.abs(columns[None, None, None, :] - target[:, :, :, None]))


def split_rims(blocks, depth):
    return (blocks[:, :HALO], blocks[:, HALO : HALO + depth], blocks[:, HALO + depth :])


def shards(volume, measured, magnification, shift_y, shift_z):
    bands, depth, width = volume.shape
    total_x = bands * lax.axis_size("xband")
    total_angles = magnification.shape[0]
    hats = hat_tables(magnification, shift_y, width)

    def forward_rows():
        images = jnp.einsum(
            "izy,aiuy->aizu",
            volume,
            hats,
            precision=lax.Precision.HIGHEST,
            preferred_element_type=jnp.float32,
        )
        padded = jnp.pad(images, ((0, 0), (0, 0), (2 * HALO, 2 * HALO), (0, 0)))

        def place(plane, offset):
            return lax.dynamic_slice_in_dim(plane, HALO - offset, depth + 2 * HALO, 0)

        placed = jax.vmap(jax.vmap(place))(padded, shift_z)
        return jnp.sum(placed, axis=1)

    summed = lax.psum_scatter(forward_rows(), "xband", scatter_dimension=0, tiled=True)
    lower_rim, middle, upper_rim = split_rims(summed, depth)
    from_above = passed_along(lower_rim, "zslab", -1)
    from_below = passed_along(upper_rim, "zslab", 1)
    proj = middle.at[:, depth - HALO :].add(from_above).at[:, :HALO].add(from_below)
    measured_sum, proj_sum = lax.psum((jnp.sum(measured, axis=1), jnp.sum(proj, axis=1)), "zslab")
    gain = measured_sum / proj_sum
    residual = (measured - gain[:, None, :] * proj) / total_x
    extended = extended_2(residual, (("zslab", 1),), HALO)

    def pick(plane, band_offsets):
        return jax.vmap(lambda offset: lax.dynamic_slice_in_dim(plane, HALO + offset, depth, 0))(
            band_offsets
        )

    rows = jax.vmap(pick)(lax.all_gather(extended, "xband", axis=0, tiled=True), shift_z)
    images = jnp.einsum(
        "aizu,aiuy->izy",
        rows,
        hats,
        precision=lax.Precision.HIGHEST,
        preferred_element_type=jnp.float32,
    )
    correction = images / math.sqrt(total_angles)
    return (residual, correction)


def solution(mesh):
    return jax.shard_map(
        shards,
        mesh=mesh,
        in_specs=(
            P("xband", "zslab", None),
            P("xband", "zslab", None),
            P(None, "xband"),
            P(None, "xband"),
            P(None, "xband"),
        ),
        out_specs=(P("xband", "zslab", None), P("xband", "zslab", None)),
        check_vma=False,
    )
```

profile of v0, /device:TPU:0, one launch (start us, length us, event | category | flops | bytes accessed | tf_op | source)
XLA Modules:
  0.0 114.1 jit_solution(9756427483090364221)
XLA Ops:
  7.2 0.0 copy-start
  7.2 0.0 reduce-scatter.2.cloned.1.call-start
  7.2 0.7 convert_bitcast_fusion
  7.9 0.7 fusion.14
  8.6 8.9 %fusion.8 = f32[8,1,32,512]{3,2,0,1:T(8,128)S(1)} fusion(f32[8,512]{1,0:T(8,128)S(1)} %fusion.14, f32[1,32,512]{2,1,0:T(8,128)S(1)} %copy-done), kind=kOutput, calls=%fused_computation.11 | convolution fusion | flops 813694976 | bytes 606208 | tf_op jit(solution)/shard_map/izy,aiuy->aizu/dot_general | solution.py:52
  17.5 0.0 copy-start.3
  17.5 0.5 copy.15
  18.1 0.1 copy-done.3
  18.2 0.1 pad.17.clone
  18.3 0.1 fusion.18
  18.4 0.6 pad.10.clone
  19.0 1.2 %gather_fusion = f32[8,40,512]{2,0,1:T(8,128)S(1)} fusion(f32[8,1,48,512]{3,1,0,2:T(1,128)S(1)} %pad.10.clone, s32[8]{0:T(128)S(1)} %or_bitcast_fusion.1), kind=kCustom, calls=%fused_computation | custom fusion | bytes 1310848 | tf_op jit(solution)/shard_map/vmap(vmap())/gather | solution.py:62
  20.1 0.0 copy-start.2
  20.2 1.2 %copy.12 = f32[8,40,512]{2,1,0:T(8,128)} copy(f32[8,40,512]{2,0,1:T(8,128)S(1)} %gather_fusion) | data formatting | bytes 1310720 | tf_op jit(solution)/shard_map/vmap(vmap())/gather | solution.py:62
  21.4 0.0 reduce-scatter.2.cloned.1.call-update
  21.4 34.2 %reduce-scatter.2.cloned.1.call-done = f32[1,40,512]{2,1,0:T(8,128)} async-done(((f32[8,40,512]{2,1,0:T(8,128)}), f32[1,40,512]{2,1,0:T(8,128)}) %reduce-scatter.2.cloned.1.call-update) | async-done | bytes 81936 | tf_op jit(solution)/shard_map/reduce_scatter | solution.py:67
  55.6 0.7 fusion.25
  56.3 1.3 %collective-permute-start = (f32[1,4,512]{2,1,0:T(4,128)S(1)}, f32[1,4,512]{2,1,0:T(4,128)S(1)}, u32[]{:S(2)}, u32[]{:S(2)}) collective-permute-start(f32[1,4,512]{2,1,0:T(4,128)S(1)} %get-tuple-element.31), channel_id=1, source_target_pairs={{8,0},{16,8},{24,16},{9,1},{17,9},{25,17},{10,2},{18,10},{26,18},{... | collective-permute-start | bytes 24584 | tf_op jit(solution)/shard_map/ppermute | solution.py:14
  57.7 4.5 %collective-permute-start.1 = (f32[1,4,512]{2,1,0:T(4,128)S(1)}, f32[1,4,512]{2,1,0:T(4,128)S(1)}, u32[]{:S(2)}, u32[]{:S(2)}) collective-permute-start(f32[1,4,512]{2,1,0:T(4,128)S(1)} %get-tuple-element.30), channel_id=1, source_target_pairs={{0,8},{8,16},{16,24},{1,9},{9,17},{17,25},{2,10},{10,18},{18,26},{... | collective-permute-start | bytes 24584 | tf_op jit(solution)/shard_map/ppermute | solution.py:14
  62.2 0.9 slice.78
  63.1 0.0 collective-permute-done
  63.1 0.7 fusion.16
  63.9 10.3 %all-reduce.3 = (f32[1,512]{1,0:T(1,128)S(1)}, f32[1,512]{1,0:T(1,128)S(1)}) all-reduce(f32[1,512]{1,0:T(1,128)S(1)} %bitcast.36, f32[1,512]{1,0:T(1,128)S(1)} %bitcast.37), channel_id=1, replica_groups=mesh['zslab'=4,'xband'=8] {'zslab'}, use_global_device_ids=true, to_apply=%region_1.2 | all-reduce | flops 1024 | bytes 8192 | tf_op jit(solution)/shard_map/psum | solution.py:72
  74.2 0.0 copy-start.1
  74.3 3.3 %collective-permute-start.2 = (f32[1,4,512]{2,1,0:T(4,128)S(1)}, f32[1,4,512]{2,1,0:T(4,128)S(1)}, u32[]{:S(2)}, u32[]{:S(2)}) collective-permute-start(f32[1,4,512]{2,1,0:T(4,128)S(1)} %get-tuple-element.32), channel_id=1, source_target_pairs={{0,8},{8,16},{16,24},{1,9},{9,17},{17,25},{2,10},{10,18},{18,26},{... | collective-permute-start | bytes 24584 | tf_op jit(solution)/shard_map/ppermute | solution.py:24
  77.6 1.3 %collective-permute-start.3 = (f32[1,4,512]{2,1,0:T(4,128)S(1)}, f32[1,4,512]{2,1,0:T(4,128)S(1)}, u32[]{:S(2)}, u32[]{:S(2)}) collective-permute-start(f32[1,4,512]{2,1,0:T(4,128)S(1)} %get-tuple-element.33), channel_id=1, source_target_pairs={{8,0},{16,8},{24,16},{9,1},{17,9},{25,17},{10,2},{18,10},{26,18},{... | collective-permute-start | bytes 24584 | tf_op jit(solution)/shard_map/ppermute | solution.py:25
  78.9 0.0 collective-permute-done.2
  79.0 4.2 %collective-permute-done.3 = f32[1,4,512]{2,1,0:T(4,128)S(1)} collective-permute-done((f32[1,4,512]{2,1,0:T(4,128)S(1)}, f32[1,4,512]{2,1,0:T(4,128)S(1)}, u32[]{:S(2)}, u32[]{:S(2)}) %collective-permute-start.3) | collective-permute-done | bytes 8224 | tf_op jit(solution)/shard_map/ppermute | solution.py:25
  83.2 15.6 %all_gather.3 = f32[8,40,512]{2,1,0:T(8,128)S(1)} all-gather(f32[1,40,512]{2,1,0:T(8,128)S(1)} %pad_maximum_fusion), channel_id=1, replica_groups=mesh['zslab'=4,'xband'=8] {'xband'}, dimensions={0}, use_global_device_ids=true | all-gather | bytes 737280 | tf_op jit(solution)/shard_map/all_gather | solution.py:82
  98.8 0.4 copy.13
  99.2 1.3 %gather_fusion.1 = f32[8,32,512]{2,0,1:T(8,128)S(1)} fusion(f32[8,40,512]{2,0,1:T(8,128)S(1)} %copy.13, s32[8]{0:T(128)S(1)} %or_bitcast_fusion), kind=kCustom, calls=%fused_computation.1 | custom fusion | bytes 1048672 | tf_op jit(solution)/shard_map/vmap(vmap())/gather | solution.py:78
  100.5 6.8 %fusion.11 = f32[1,32,512]{2,1,0:T(8,128)} fusion(f32[8,512]{1,0:T(8,128)S(1)} %fusion.14, f32[8,32,512]{2,0,1:T(8,128)S(1)} %gather_fusion.1), kind=kOutput, calls=%fused_computation.14 | convolution fusion | flops 813711360 | bytes 606208 | tf_op jit(solution)/shard_map/aizu,aiuy->izy/dot_general | solution.py:83
  (18 shorter events, 0.2 us)
Async XLA Ops:
  7.2 1.5 %copy-start = (f32[1,32,512]{2,1,0:T(8,128)S(1)}, f32[1,32,512]{2,1,0:T(8,128)}, u32[]{:S(2)}) copy-start(f32[1,32,512]{2,1,0:T(8,128)} %param.9) | copy-start | bytes 196612
  7.2 48.4 %reduce-scatter.2.cloned.1.call-start = ((), (), s32[]{:S(2)}) async-start(), calls=%async_computation.1 | async-start | bytes 737280 | tf_op jit(solution)/shard_map/reduce_scatter | solution.py:67
  17.5 0.7 copy-start.3
  20.1 37.5 %copy-start.2 = (f32[1,32,512]{2,1,0:T(8,128)S(1)}, f32[1,32,512]{2,1,0:T(8,128)}, u32[]{:S(2)}) copy-start(f32[1,32,512]{2,1,0:T(8,128)} %param.10) | copy-start | bytes 196612
  56.3 6.8 %collective-permute-start = (f32[1,4,512]{2,1,0:T(4,128)S(1)}, f32[1,4,512]{2,1,0:T(4,128)S(1)}, u32[]{:S(2)}, u32[]{:S(2)}) collective-permute-start(f32[1,4,512]{2,1,0:T(4,128)S(1)} %get-tuple-element.31), channel_id=1, source_target_pairs={{8,0},{16,8},{24,16},{9,1},{17,9},{25,17},{10,2},{18,10},{26,18},{... | collective-permute-start | bytes 24584 | tf_op jit(solution)/shard_map/ppermute | solution.py:14
  57.7 6.2 %collective-permute-start.1 = (f32[1,4,512]{2,1,0:T(4,128)S(1)}, f32[1,4,512]{2,1,0:T(4,128)S(1)}, u32[]{:S(2)}, u32[]{:S(2)}) collective-permute-start(f32[1,4,512]{2,1,0:T(4,128)S(1)} %get-tuple-element.30), channel_id=1, source_target_pairs={{0,8},{8,16},{16,24},{1,9},{9,17},{17,25},{2,10},{10,18},{18,26},{... | collective-permute-start | bytes 24584 | tf_op jit(solution)/shard_map/ppermute | solution.py:14
  74.2 24.9 %copy-start.1 = (f32[1,32,512]{2,1,0:T(8,128)}, f32[1,32,512]{2,1,0:T(8,128)S(1)}, u32[]{:S(2)}) copy-start(f32[1,32,512]{2,1,0:T(8,128)S(1)} %subtract_multiply_fusion) | copy-start | bytes 196612
  74.3 4.7 %collective-permute-start.2 = (f32[1,4,512]{2,1,0:T(4,128)S(1)}, f32[1,4,512]{2,1,0:T(4,128)S(1)}, u32[]{:S(2)}, u32[]{:S(2)}) collective-permute-start(f32[1,4,512]{2,1,0:T(4,128)S(1)} %get-tuple-element.32), channel_id=1, source_target_pairs={{0,8},{8,16},{16,24},{1,9},{9,17},{17,25},{2,10},{10,18},{18,26},{... | collective-permute-start | bytes 24584 | tf_op jit(solution)/shard_map/ppermute | solution.py:24
  77.6 5.5 %collective-permute-start.3 = (f32[1,4,512]{2,1,0:T(4,128)S(1)}, f32[1,4,512]{2,1,0:T(4,128)S(1)}, u32[]{:S(2)}, u32[]{:S(2)}) collective-permute-start(f32[1,4,512]{2,1,0:T(4,128)S(1)} %get-tuple-element.33), channel_id=1, source_target_pairs={{8,0},{16,8},{24,16},{9,1},{17,9},{25,17},{10,2},{18,10},{26,18},{... | collective-permute-start | bytes 24584 | tf_op jit(solution)/shard_map/ppermute | solution.py:25
Sparse Core Ops, SparseCore 0:
  21.5 34.0 reduce-scatter.1
where the time goes:
time: 115 us; the launch traced here: 114 us
  waiting for transfers between devices  38.4 us (33%)
  blocking collectives  25.9 us (23%)
  matrix products  15.7 us (14%)
  between operations  14.2 us (12%)
  starting transfers between devices  10.5 us (9%)
  local copies, waits for them, and re-layouts  7.08 us (6%)
  other arithmetic  2.33 us (2%)
    reduce_scatter x1, waiting for transfers between devices, shards(): lax.psum_scatter(forward_rows(), 'xband', scatter_dimension=0, tiled=True)  34.2 us
    all_gather x1, blocking collectives, shards(): lax.all_gather(extended, 'xband', axis=0, tiled=True)  15.6 us
    psum x1, blocking collectives, shards(): lax.psum((jnp.sum(measured, axis=1), jnp.sum(proj, axis=1)), 'zslab')  10.3 us
    dot_general x1, matrix products, forward_rows(): jnp.einsum('izy,aiuy->aizu', volume, hats, precision=lax.Precision.HIGHES...  8.9 us
    dot_general x1, matrix products, shards(): jnp.einsum('aizu,aiuy->izy', rows, hats, precision=lax.Precision.HIGHEST,...  6.77 us
    ppermute x2, starting transfers between devices, passed_along(): return lax.ppermute(x, axis, pairs)  5.83 us
    ppermute x1, waiting for transfers between devices, extended_2(): after = lax.ppermute(first, axis, down)  4.2 us
    ppermute x1, starting transfers between devices, extended_2(): before = lax.ppermute(last, axis, up)  3.34 us
  transfers between devices with their start and end apart: 5, of which 2 were waited for; matrix products, arithmetic and copies ran while one was open for 1% of the time, Pallas kernels for 0%

commit v1 on v0

v1 whole, which is shorter than its diff:
```python
import functools
import math

import jax
import jax.numpy as jnp
from jax import lax
from jax.experimental import pallas as pl
from jax.experimental.pallas import tpu as pltpu
from jax.sharding import PartitionSpec as P

HALO = 4
LANES = 128
VMEM_LIMIT = 48 * 1024 * 1024
NT = (((1,), (1,)), ((), ()))


def rows_at(tile, index):
    return jnp.take_along_axis(tile, index, axis=0, mode="promise_in_bounds")


def by_lane(lane, depth, values):
    out = jnp.full(lane.shape, values[0])
    for q in range(1, len(values)):
        out = jnp.where(lane >= q * depth, values[q], out)
    return out


def two_parts(x):
    high = x.astype(jnp.bfloat16)
    return high, (x - high.astype(jnp.float32)).astype(jnp.bfloat16)


def copy_tables(sources, start, table, sem):
    copies = [
        pltpu.make_async_copy(source.at[pl.ds(start, 8)], table.at[k], sem.at[k])
        for k, source in enumerate(sources)
    ]
    for copy in copies:
        copy.start()
    return copies


def forward_kernel(n, depth, width, slabs, *refs):
    half = n // 2
    info, volumes, measured = refs[0], refs[1 : 1 + n], refs[1 + n : 1 + n + half]
    proj, up, down, sums = refs[1 + n + half : 5 + n + half]
    turned, high, low, table, sem = refs[5 + n + half :]
    tiles = width // LANES
    per = LANES // depth
    groups = n // per
    rows = depth + 2 * HALO
    centre = (width - 1) / 2.0
    band, slab = info[0], info[1]
    copies = copy_tables(volumes, tiles * depth, table, sem)
    for g in range(groups):
        for tile in range(tiles):
            part = pl.ds(tile * depth, depth)
            block = jnp.concatenate([volumes[g * per + q][part, :] for q in range(per)], axis=0)
            turned[g, tile * LANES : (tile + 1) * LANES, :] = block.T
    for copy in copies:
        copy.wait()

    lane = lax.broadcasted_iota(jnp.int32, (8, LANES), 1)
    step = lax.broadcasted_iota(jnp.int32, (8, LANES), 0).astype(jnp.float32)
    place = lax.broadcasted_iota(jnp.int32, (rows, LANES), 0)
    wide_lane = lax.broadcasted_iota(jnp.int32, (rows, LANES), 1)
    keep = (place >= HALO) | (slab > 0)
    keep = keep & ((place < HALO + depth) | (slab < slabs - 1))

    def angle(j, carry):
        a = band ^ (2 * j)
        total = jnp.zeros((rows, width), jnp.float32)
        for g in range(groups):
            inverse = [table[g * per + q, 0, a] for q in range(per)]
            offset = [table[g * per + q, 1, a] for q in range(per)]
            shift = [table[g * per + q, 2, a].astype(jnp.int32) for q in range(per)]
            inverse_l = by_lane(lane, depth, inverse)
            offset_l = by_lane(lane, depth, offset)
            fine = step * inverse_l

            def eight(block):
                first = (block * 8).astype(jnp.float32) - centre
                base = [(first * inverse[q] + offset[q]).astype(jnp.int32) for q in range(per)]
                window = turned[g, pl.ds(base[0], 8), :]
                for q in range(1, per):
                    window = jnp.where(lane >= q * depth, turned[g, pl.ds(base[q], 8), :], window)
                base_l = by_lane(lane, depth, [b.astype(jnp.float32) for b in base])
                target = (first * inverse_l + offset_l) - base_l + fine
                lower = target.astype(jnp.int32)
                frac = target - lower.astype(jnp.float32)
                left = rows_at(window, lower)
                return left + frac * (rows_at(window, lower + 1) - left)

            def sixteen(i, carry):
                pair = jnp.concatenate([eight(2 * i), eight(2 * i + 1)], axis=0)
                at = pl.ds(pl.multiple_of(16 * i, 16), 16)
                high[at, :], low[at, :] = two_parts(pair)
                return carry

            lax.fori_loop(0, width // 16, sixteen, 0, unroll=4)
            shift_l = by_lane(wide_lane, depth, shift)
            hits = (place - HALO - shift_l == (wide_lane & (depth - 1))) & keep
            select = jnp.where(hits, 1.0, 0.0).astype(jnp.bfloat16)
            total += lax.dot_general(select, high[...], NT, preferred_element_type=jnp.float32)
            total += lax.dot_general(select, low[...], NT, preferred_element_type=jnp.float32)
        proj[j] = total
        return carry

    lax.fori_loop(0, half, angle, 0)
    for j in range(half):
        up[8 * j : 8 * j + 8, :] = proj[j, depth : depth + 8, :]
        down[8 * j : 8 * j + 8, :] = proj[j, :8, :]
        at = 8 * half + HALO * j
        up[at : at + HALO, :] = measured[j][depth - HALO :, :]
        down[at : at + HALO, :] = measured[j][:HALO, :]
        sums[j : j + 1, :] = jnp.sum(proj[j], axis=0, keepdims=True)
        sums[half + j : half + j + 1, :] = jnp.sum(measured[j][...], axis=0, keepdims=True)
    at = (8 + HALO) * half
    up[at:, :] = sums[...]
    down[at:, :] = sums[...]


def backward_kernel(n, depth, width, slabs, *refs):
    half = n // 2
    info, own_table, other_table, proj, sums, from_below, from_above = refs[:7]
    others, measured = refs[7 : 7 + slabs - 3], refs[7 + slabs - 3 : 7 + slabs - 3 + half]
    residual, own, other = refs[7 + slabs - 3 + half : 10 + slabs - 3 + half]
    held, stack, turned, high, low, table, sem = refs[10 + slabs - 3 + half :]
    tiles = width // LANES
    per = LANES // depth
    groups = half // per
    rows = depth + 2 * HALO
    centre = (width - 1) / 2.0
    pad = 24
    band, slab = info[0], info[1]
    copies = copy_tables((own_table, other_table), tiles * depth, table, sem)
    edge = (8 + HALO) * half
    column = sums[...] + from_below[edge:, :] + from_above[edge:, :]
    for ref in others:
        column += ref[...]
    place = lax.broadcasted_iota(jnp.int32, (rows, width), 0)
    keep = (place >= HALO) | (slab > 0)
    keep = keep & ((place < HALO + depth) | (slab < slabs - 1))
    for j in range(half):
        gain = column[half + j : half + j + 1, :] / column[j : j + 1, :]
        at = 8 * half + HALO * j
        wanted = jnp.concatenate(
            [from_below[at : at + HALO, :], measured[j][...], from_above[at : at + HALO, :]], axis=0
        )
        image = jnp.concatenate(
            [
                proj[j, :8, :] + from_below[8 * j : 8 * j + 8, :],
                proj[j, 8:depth, :],
                proj[j, depth:, :] + from_above[8 * j : 8 * j + 8, :],
            ],
            axis=0,
        )
        value = jnp.where(keep, (wanted - gain * image) * (1.0 / n), 0.0)
        if j == 0:
            residual[...] = value[HALO : HALO + depth, :]
        for tile in range(tiles):
            held[j, tile] = value[:, tile * LANES : (tile + 1) * LANES]
    for copy in copies:
        copy.wait()

    lane = lax.broadcasted_iota(jnp.int32, (8, LANES), 1)
    step = lax.broadcasted_iota(jnp.int32, (8, LANES), 0).astype(jnp.float32)
    place = lax.broadcasted_iota(jnp.int32, (depth, LANES), 0)
    wide_lane = lax.broadcasted_iota(jnp.int32, (depth, LANES), 1)
    select = jnp.where(place == (wide_lane & (depth - 1)), 1.0, 0.0).astype(jnp.bfloat16)
    turned[:pad, :] = jnp.zeros((pad, LANES), jnp.float32)
    turned[pad + width :, :] = jnp.zeros((pad, LANES), jnp.float32)

    for cell, out in enumerate((own, other)):
        total = jnp.zeros((depth, width), jnp.float32)
        for g in range(groups):
            angles = [band ^ (2 * (g * per + q)) for q in range(per)]
            inverse = [table[cell, 0, a] for a in angles]
            offset = [table[cell, 1, a] for a in angles]
            shift = [table[cell, 2, a].astype(jnp.int32) + HALO for a in angles]
            magnification = [table[cell, 3, a] for a in angles]
            for tile in range(tiles):
                for q in range(per):
                    stack[q * depth : (q + 1) * depth, :] = held[g * per + q, tile, pl.ds(shift[q], depth), :]
                turned[pad + tile * LANES : pad + (tile + 1) * LANES, :] = stack[...].T
            inverse_l = by_lane(lane, depth, inverse)
            offset_l = by_lane(lane, depth, offset)
            magnification_l = by_lane(lane, depth, magnification)
            fine = step * magnification_l

            def eight(block):
                first = (block * 8).astype(jnp.float32)
                base = [
                    jnp.clip(
                        ((first - offset[q]) * magnification[q] + (centre + 1024.0)).astype(jnp.int32) - 1025,
                        -pad,
                        width,
                    )
                    for q in range(per)
                ]
                windows = [turned[pl.ds(base[0] + (pad + 8 * r), 8), :] for r in range(3)]
                for q in range(1, per):
                    here = lane >= q * depth
                    windows = [
                        jnp.where(here, turned[pl.ds(base[q] + (pad + 8 * r), 8), :], windows[r]) for r in range(3)
                    ]
                base_l = by_lane(lane, depth, [b.astype(jnp.float32) for b in base])
                target = ((first - offset_l) * magnification_l + centre) - base_l + fine
                lower = target.astype(jnp.int32)
                frac = target - lower.astype(jnp.float32)
                out = jnp.zeros((8, LANES), jnp.float32)
                for tap in range(4):
                    index = lower + (tap - 1)
                    within = index & 7
                    value = jnp.where(index < 8, rows_at(windows[0], within), rows_at(windows[1], within))
                    if tap >= 2:
                        value = jnp.where(index < 16, value, rows_at(windows[2], within))
                    weight = jnp.maximum(0.0, 1.0 - jnp.abs((frac + (1.0 - tap)) * inverse_l))
                    out += weight * value
                return out

            def sixteen(i, carry):
                pair = jnp.concatenate([eight(2 * i), eight(2 * i + 1)], axis=0)
                at = pl.ds(pl.multiple_of(16 * i, 16), 16)
                high[at, :], low[at, :] = two_parts(pair)
                return carry

            lax.fori_loop(0, width // 16, sixteen, 0, unroll=2)
            total += lax.dot_general(select, high[...], NT, preferred_element_type=jnp.float32)
            total += lax.dot_general(select, low[...], NT, preferred_element_type=jnp.float32)
        out[...] = total * (1.0 / math.sqrt(n))


def swapped(x, by):
    n = lax.axis_size("xband")
    return lax.ppermute(x, "xband", [(i, i ^ by) for i in range(n)])


def from_slab(x, by):
    n = lax.axis_size("zslab")
    return lax.ppermute(x, "zslab", [(i, (i + by) % n) for i in range(n)])


def shards(volume, measured, magnification, shift_y, shift_z):
    _, depth, width = volume.shape
    n, slabs = lax.axis_size("xband"), lax.axis_size("zslab")
    half = n // 2
    rows = depth + 2 * HALO
    centre = (width - 1) / 2.0
    f32 = jnp.float32
    info = jnp.stack([lax.axis_index("xband"), lax.axis_index("zslab")]).astype(jnp.int32)

    mag = magnification[:, 0]
    entries = jnp.stack(
        [1.0 / mag, centre + shift_y[:, 0].astype(f32), shift_z[:, 0].astype(f32), mag], axis=0
    )
    entries = jnp.pad(entries, ((0, 4), (0, LANES - n)))
    packed = volume[0].reshape(depth, width // LANES, LANES).transpose(1, 0, 2).reshape(-1, LANES)
    packed = jnp.concatenate([packed, entries], axis=0)

    mine = [packed] + [swapped(packed, 2 * k) for k in range(1, half)]
    views = [measured[0]] + [swapped(measured[0], 2 * k) for k in range(1, half)]
    theirs = [swapped(x, 1) for x in mine]

    smem = pl.BlockSpec(memory_space=pltpu.SMEM)
    vmem = pl.BlockSpec(memory_space=pltpu.VMEM)
    edge_rows = (8 + HALO + 2) * half
    params = pltpu.CompilerParams(vmem_limit_bytes=VMEM_LIMIT)
    proj, up, down, sums = pl.pallas_call(
        functools.partial(forward_kernel, n, depth, width, slabs),
        out_shape=[
            jax.ShapeDtypeStruct((half, rows, width), f32),
            jax.ShapeDtypeStruct((edge_rows, width), f32),
            jax.ShapeDtypeStruct((edge_rows, width), f32),
            jax.ShapeDtypeStruct((2 * half, width), f32),
        ],
        in_specs=[smem] + [vmem] * (n + half),
        out_specs=[vmem] * 4,
        scratch_shapes=[
            pltpu.VMEM((n * depth // LANES, width, LANES), f32),
            pltpu.VMEM((width, LANES), jnp.bfloat16),
            pltpu.VMEM((width, LANES), jnp.bfloat16),
            pltpu.SMEM((n, 8, LANES), f32),
            pltpu.SemaphoreType.DMA((n,)),
        ],
        compiler_params=params,
    )(info, *mine, *theirs, *views)

    from_below, from_above = from_slab(up, 1), from_slab(down, -1)
    others = [from_slab(sums, k) for k in range(2, slabs - 1)]

    residual, own, other = pl.pallas_call(
        functools.partial(backward_kernel, n, depth, width, slabs),
        out_shape=[jax.ShapeDtypeStruct((depth, width), f32)] * 3,
        in_specs=[smem] + [vmem] * (6 + len(others) + half),
        out_specs=[vmem] * 3,
        scratch_shapes=[
            pltpu.VMEM((half, width // LANES, rows, LANES), f32),
            pltpu.VMEM((LANES, LANES), f32),
            pltpu.VMEM((width + 48, LANES), f32),
            pltpu.VMEM((width, LANES), jnp.bfloat16),
            pltpu.VMEM((width, LANES), jnp.bfloat16),
            pltpu.SMEM((2, 8, LANES), f32),
            pltpu.SemaphoreType.DMA((2,)),
        ],
        compiler_params=params,
    )(info, mine[0], theirs[0], proj, sums, from_below, from_above, *others, *views)

    correction = own + swapped(other, 1)
    return residual[None], correction[None]


def solution(mesh):
    return jax.shard_map(
        shards,
        mesh=mesh,
        in_specs=(
            P("xband", "zslab", None),
            P("xband", "zslab", None),
            P(None, "xband"),
            P(None, "xband"),
            P(None, "xband"),
        ),
        out_specs=(P("xband", "zslab", None), P("xband", "zslab", None)),
        check_vma=False,
    )
```

time: 115 us -> 47.5 us (0.41)
  waiting for transfers between devices: 38.4 us -> 10.2 us
  blocking collectives: 25.9 us -> 0 us
  matrix products: 15.7 us -> 0 us
  Pallas kernels: 0 us -> 15 us
  between operations: 14.2 us -> 0.72 us
  starting transfers between devices: 10.5 us -> 18.4 us
  local copies, waits for them, and re-layouts: 7.08 us -> 1.53 us
    reduce_scatter x1 -> x0, waiting for transfers between devices: 34.2 us -> none  [shards(): lax.psum_scatter(forward_rows(), 'xband', scatter_dimension=0, tiled=True)]
    dot_general x2 -> x0, matrix products: 15.7 us -> none  [the longest x1 8.9 us: forward_rows(): jnp.einsum('izy,aiuy->aizu', volume, hats, precision=lax.Precision.HIGHES...]
    all_gather x1 -> x0, blocking collectives: 15.6 us -> none  [shards(): lax.all_gather(extended, 'xband', axis=0, tiled=True)]
    pallas_call x0 -> x2, Pallas kernels: none -> 15 us  [the longest x1 9.83 us: shards(): pl.pallas_call(functools.partial(forward_kernel, n, depth, width, slabs),...]
    psum x1 -> x0, blocking collectives: 10.3 us -> none  [shards(): lax.psum((jnp.sum(measured, axis=1), jnp.sum(proj, axis=1)), 'zslab')]
    ppermute x4 -> x14, starting transfers between devices: 10.5 us -> 18.4 us  [the longest x11 14 us: swapped(): return lax.ppermute(x, 'xband', [(i, i ^ by) for i in range(n)])]
    ppermute x4 -> x14, waiting for transfers between devices: 4.23 us -> 10.2 us  [the longest x11 5.87 us: swapped(): return lax.ppermute(x, 'xband', [(i, i ^ by) for i in range(n)])]
    gather x4 -> x0, local copies, waits for them, and re-layouts: 3.8 us -> none  [the longest x3 2.48 us: place(): return lax.dynamic_slice_in_dim(plane, HALO - offset, depth + 2 * HALO, 0)]
  transfers between devices with their start and end apart: 5 -> 14, of which waited for: 2 -> 6; matrix products, arithmetic and copies ran while one was open for 1% -> 0% of each run, Pallas kernels for 0% -> 0%
where the time goes in v1:
time: 47.5 us; the launch traced here: 47.3 us
  starting transfers between devices  18.4 us (39%)
  Pallas kernels  15 us (32%)
  waiting for transfers between devices  10.2 us (21%)
  local copies, waits for them, and re-layouts  1.53 us (3%)
  other arithmetic  1.41 us (3%)
  between operations  0.72 us (2%)
    ppermute x11, starting transfers between devices, swapped(): return lax.ppermute(x, 'xband', [(i, i ^ by) for i in range(n)])  14 us
    pallas_call x1, Pallas kernels, shards(): pl.pallas_call(functools.partial(forward_kernel, n, depth, width, slabs),...  9.83 us
    ppermute x11, waiting for transfers between devices, swapped(): return lax.ppermute(x, 'xband', [(i, i ^ by) for i in range(n)])  5.87 us
    pallas_call x1, Pallas kernels, shards(): pl.pallas_call(functools.partial(backward_kernel, n, depth, width, slabs)...  5.15 us
    ppermute x3, starting transfers between devices, from_slab(): return lax.ppermute(x, 'zslab', [(i, (i + by) % n) for i in range(n)])  4.43 us
    ppermute x3, waiting for transfers between devices, from_slab(): return lax.ppermute(x, 'zslab', [(i, (i + by) % n) for i in range(n)])  4.37 us
  transfers between devices with their start and end apart: 14, of which 6 were waited for; matrix products, arithmetic and copies ran while one was open for 0% of the time, Pallas kernels for 0%

profile of v1, /device:TPU:0, one launch (start us, length us, event | category | flops | bytes accessed | tf_op | source)
XLA Modules:
  0.0 47.3 jit_solution(6843795117271111222)
XLA Ops:
  0.6 0.7 %add_bitcast_fusion.1 = f32[1,8]{1,0:T(1,128)S(1)} fusion(s32[8,1]{0,1:T(1,128)} %param.8), kind=kLoop, calls=%fused_computation.9 | loop fusion | flops 16 | bytes 64 | tf_op jit(solution)/shard_map/add | solution.py:255
  1.3 0.6 %copy-done.1 = f32[8,1]{0,1:T(1,128)S(1)} copy-done((f32[8,1]{0,1:T(1,128)S(1)}, f32[8,1]{0,1:T(1,128)}, u32[]{:S(2)}) %copy-start.1) | copy-done | bytes 56
  2.0 0.9 %reshape_squeeze.3 = f32[32,4,128]{2,1,0:T(4,128)S(1)} reshape(f32[1,32,512]{2,1,0:T(8,128)} %param.5) | data formatting | bytes 131072 | tf_op jit(solution)/shard_map/reshape;squeeze | solution.py:258
  2.9 0.0 copy-start
  2.9 5.1 %collective-permute-start.3 = (f32[136,128]{1,0:T(8,128)S(1)}, f32[136,128]{1,0:T(8,128)S(1)}, u32[]{:S(2)}, u32[]{:S(2)}) collective-permute-start(f32[136,128]{1,0:T(8,128)S(1)} %pad_maximum_fusion.refs_1_), channel_id=1, source_target_pairs={{0,6},{1,7},{2,4},{3,5},{4,2},{5,3},{6,0},{7,1},{8,14},{9,15},{10,... | collective-permute-start | bytes 208904 | tf_op jit(solution)/shard_map/ppermute | solution.py:236
  8.0 0.0 collective-permute-start.2
  8.0 0.6 %collective-permute-start.1 = (f32[136,128]{1,0:T(8,128)S(1)}, f32[136,128]{1,0:T(8,128)S(1)}, u32[]{:S(2)}, u32[]{:S(2)}) collective-permute-start(f32[136,128]{1,0:T(8,128)S(1)} %pad_maximum_fusion.refs_1_), channel_id=1, source_target_pairs={{0,2},{1,3},{2,0},{3,1},{4,6},{5,7},{6,4},{7,5},{8,10},{9,11},{10,... | collective-permute-start | bytes 208904 | tf_op jit(solution)/shard_map/ppermute | solution.py:236
  8.7 3.7 %collective-permute-start.9 = (f32[32,512]{1,0:T(8,128)S(1)}, f32[32,512]{1,0:T(8,128)S(1)}, u32[]{:S(2)}, u32[]{:S(2)}) collective-permute-start(f32[32,512]{1,0:T(8,128)S(1)} %bitcast.15), channel_id=1, source_target_pairs={{0,6},{1,7},{2,4},{3,5},{4,2},{5,3},{6,0},{7,1},{8,14},{9,15},{10,... | collective-permute-start | bytes 196616 | tf_op jit(solution)/shard_map/ppermute | solution.py:236
  12.4 0.0 collective-permute-start.8
  12.4 3.5 %collective-permute-done.9.refs_12_.refs_11_ = f32[32,512]{1,0:T(8,128)S(1)} collective-permute-done((f32[32,512]{1,0:T(8,128)S(1)}, f32[32,512]{1,0:T(8,128)S(1)}, u32[]{:S(2)}, u32[]{:S(2)}) %collective-permute-start.9) | collective-permute-done | bytes 65568 | tf_op jit(solution)/shard_map/ppermute | solution.py:236
  15.9 3.4 %collective-permute-start.7 = (f32[32,512]{1,0:T(8,128)S(1)}, f32[32,512]{1,0:T(8,128)S(1)}, u32[]{:S(2)}, u32[]{:S(2)}) collective-permute-start(f32[32,512]{1,0:T(8,128)S(1)} %bitcast.17), channel_id=1, source_target_pairs={{0,2},{1,3},{2,0},{3,1},{4,6},{5,7},{6,4},{7,5},{8,10},{9,11},{10,... | collective-permute-start | bytes 196616 | tf_op jit(solution)/shard_map/ppermute | solution.py:236
  19.3 0.3 collective-permute-done.8.refs_11_.refs_10_
  19.6 0.0 collective-permute-start
  19.6 0.5 %collective-permute-start.6 = (f32[136,128]{1,0:T(8,128)S(1)}, f32[136,128]{1,0:T(8,128)S(1)}, u32[]{:S(2)}, u32[]{:S(2)}) collective-permute-start(f32[136,128]{1,0:T(8,128)S(1)} %collective-permute-done.3.refs_4_), channel_id=1, source_target_pairs={{0,1},{1,0},{2,3},{3,2},{4,5},{5,4},{6,7},{7,6},{8,9},{9,8},{10,11... | collective-permute-start | bytes 208904 | tf_op jit(solution)/shard_map/ppermute | solution.py:236
  20.1 0.1 collective-permute-start.5
  20.2 0.4 collective-permute-start.4
  20.6 0.1 pad_add_fusion.refs_0_
  20.7 0.8 %collective-permute-done.7.refs_10_.refs_9_ = f32[32,512]{1,0:T(8,128)S(1)} collective-permute-done((f32[32,512]{1,0:T(8,128)S(1)}, f32[32,512]{1,0:T(8,128)S(1)}, u32[]{:S(2)}, u32[]{:S(2)}) %collective-permute-start.7) | collective-permute-done | bytes 65568 | tf_op jit(solution)/shard_map/ppermute | solution.py:236
  21.5 0.0 collective-permute-done.refs_5_.refs_2_
  21.5 0.0 collective-permute-done.6.refs_8_
  21.5 0.0 collective-permute-done.5.refs_7_
  21.6 9.8 %shard_map.68 = (f32[4,40,512]{2,1,0:T(8,128)S(1)}, f32[56,512]{1,0:T(8,128)S(1)}, f32[56,512]{1,0:T(8,128)S(1)}, f32[8,512]{1,0:T(8,128)S(1)}) custom-call(s32[2]{0:T(128)S(1)} %pad_add_fusion.refs_0_, f32[136,128]{1,0:T(8,128)S(1)} %pad_maximum_fusion.refs_1_, f32[136,128]{1,0:T(8,128)S(1)} %collective-permute-done.1.refs_2_, ...), custom_call_target="tpu_custom_call" | custom-call | tf_op jit(solution)/shard_map/pallas_call | solution.py:269
  31.4 1.5 %collective-permute-start.10 = (f32[56,512]{1,0:T(8,128)S(1)}, f32[56,512]{1,0:T(8,128)S(1)}, u32[]{:S(2)}, u32[]{:S(2)}) collective-permute-start(f32[56,512]{1,0:T(8,128)S(1)} %get-tuple-element.11), channel_id=1, source_target_pairs={{0,8},{8,16},{16,24},{24,0},{1,9},{9,17},{17,25},{25,1},{2,10},{10... | collective-permute-start | bytes 344072 | tf_op jit(solution)/shard_map/ppermute | solution.py:241
  32.9 1.5 %collective-permute-start.11 = (f32[56,512]{1,0:T(8,128)S(1)}, f32[56,512]{1,0:T(8,128)S(1)}, u32[]{:S(2)}, u32[]{:S(2)}) collective-permute-start(f32[56,512]{1,0:T(8,128)S(1)} %get-tuple-element.12), channel_id=1, source_target_pairs={{0,24},{8,0},{16,8},{24,16},{1,25},{9,1},{17,9},{25,17},{2,26},{10... | collective-permute-start | bytes 344072 | tf_op jit(solution)/shard_map/ppermute | solution.py:241
  34.4 1.5 %collective-permute-start.12 = (f32[8,512]{1,0:T(8,128)S(1)}, f32[8,512]{1,0:T(8,128)S(1)}, u32[]{:S(2)}, u32[]{:S(2)}) collective-permute-start(f32[8,512]{1,0:T(8,128)S(1)} %get-tuple-element.10.refs_4_), channel_id=1, source_target_pairs={{0,16},{8,24},{16,0},{24,8},{1,17},{9,25},{17,1},{25,9},{2,18},{10... | collective-permute-start | bytes 49160 | tf_op jit(solution)/shard_map/ppermute | solution.py:241
  35.8 2.5 %collective-permute-done.12.refs_7_ = f32[8,512]{1,0:T(8,128)S(1)} collective-permute-done((f32[8,512]{1,0:T(8,128)S(1)}, f32[8,512]{1,0:T(8,128)S(1)}, u32[]{:S(2)}, u32[]{:S(2)}) %collective-permute-start.12) | collective-permute-done | bytes 16416 | tf_op jit(solution)/shard_map/ppermute | solution.py:241
  38.3 0.0 collective-permute-done.10.refs_5_
  38.3 1.9 %collective-permute-done.11.refs_6_ = f32[56,512]{1,0:T(8,128)S(1)} collective-permute-done((f32[56,512]{1,0:T(8,128)S(1)}, f32[56,512]{1,0:T(8,128)S(1)}, u32[]{:S(2)}, u32[]{:S(2)}) %collective-permute-start.11) | collective-permute-done | bytes 114720 | tf_op jit(solution)/shard_map/ppermute | solution.py:241
  40.2 5.2 %shard_map.69 = (f32[32,512]{1,0:T(8,128)}, f32[32,512]{1,0:T(8,128)S(1)}, f32[32,512]{1,0:T(8,128)S(1)}) custom-call(s32[2]{0:T(128)S(1)} %pad_add_fusion.refs_0_, f32[136,128]{1,0:T(8,128)S(1)} %pad_maximum_fusion.refs_1_, f32[136,128]{1,0:T(8,128)S(1)} %collective-permute-done.refs_5_.refs_2_, f32[4,40,512]{2,1,0:T(8,128)S(1)} %get-tuple-element.9.refs_3_, ...), custom_call_target="tpu_custom_call" | custom-call | tf_op jit(solution)/shard_map/pallas_call | solution.py:292
  45.4 0.1 collective-permute-start.13
  45.4 1.2 %collective-permute-done.13 = f32[32,512]{1,0:T(8,128)S(1)} collective-permute-done((f32[32,512]{1,0:T(8,128)S(1)}, f32[32,512]{1,0:T(8,128)S(1)}, u32[]{:S(2)}, u32[]{:S(2)}) %collective-permute-start.13) | collective-permute-done | bytes 65568 | tf_op jit(solution)/shard_map/ppermute | solution.py:236
  46.7 0.6 %add_bitcast_fusion = f32[1,32,512]{2,1,0:T(8,128)} fusion(f32[32,512]{1,0:T(8,128)S(1)} %get-tuple-element.14, f32[32,512]{1,0:T(8,128)S(1)} %collective-permute-done.13), kind=kLoop, calls=%fused_computation.1 | loop fusion | flops 16384 | bytes 196608 | tf_op jit(solution)/shard_map/broadcast_in_dim | solution.py:310
  (13 shorter events, 0.1 us)
Async XLA Ops:
  0.6 0.7 %copy-start.2 = (s32[8,1]{0,1:T(1,128)S(1)}, s32[8,1]{0,1:T(1,128)}, u32[]{:S(2)}) copy-start(s32[8,1]{0,1:T(1,128)} %param.9) | copy-start | bytes 100
  1.3 0.7 %copy-start.1 = (f32[8,1]{0,1:T(1,128)S(1)}, f32[8,1]{0,1:T(1,128)}, u32[]{:S(2)}) copy-start(f32[8,1]{0,1:T(1,128)} %param.7) | copy-start | bytes 100
  2.9 5.8 %copy-start = (f32[1,32,512]{2,1,0:T(8,128)S(1)}, f32[1,32,512]{2,1,0:T(8,128)}, u32[]{:S(2)}) copy-start(f32[1,32,512]{2,1,0:T(8,128)} %param.6) | copy-start | bytes 196612
  2.9 16.7 %collective-permute-start.3 = (f32[136,128]{1,0:T(8,128)S(1)}, f32[136,128]{1,0:T(8,128)S(1)}, u32[]{:S(2)}, u32[]{:S(2)}) collective-permute-start(f32[136,128]{1,0:T(8,128)S(1)} %pad_maximum_fusion.refs_1_), channel_id=1, source_target_pairs={{0,6},{1,7},{2,4},{3,5},{4,2},{5,3},{6,0},{7,1},{8,14},{9,15},{10,... | collective-permute-start | bytes 208904 | tf_op jit(solution)/shard_map/ppermute | solution.py:236
  8.0 12.1 %collective-permute-start.2 = (f32[136,128]{1,0:T(8,128)S(1)}, f32[136,128]{1,0:T(8,128)S(1)}, u32[]{:S(2)}, u32[]{:S(2)}) collective-permute-start(f32[136,128]{1,0:T(8,128)S(1)} %pad_maximum_fusion.refs_1_), channel_id=1, source_target_pairs={{0,4},{1,5},{2,6},{3,7},{4,0},{5,1},{6,2},{7,3},{8,12},{9,13},{10,... | collective-permute-start | bytes 208904 | tf_op jit(solution)/shard_map/ppermute | solution.py:236
  8.0 12.2 %collective-permute-start.1 = (f32[136,128]{1,0:T(8,128)S(1)}, f32[136,128]{1,0:T(8,128)S(1)}, u32[]{:S(2)}, u32[]{:S(2)}) collective-permute-start(f32[136,128]{1,0:T(8,128)S(1)} %pad_maximum_fusion.refs_1_), channel_id=1, source_target_pairs={{0,2},{1,3},{2,0},{3,1},{4,6},{5,7},{6,4},{7,5},{8,10},{9,11},{10,... | collective-permute-start | bytes 208904 | tf_op jit(solution)/shard_map/ppermute | solution.py:236
  8.7 7.2 %collective-permute-start.9 = (f32[32,512]{1,0:T(8,128)S(1)}, f32[32,512]{1,0:T(8,128)S(1)}, u32[]{:S(2)}, u32[]{:S(2)}) collective-permute-start(f32[32,512]{1,0:T(8,128)S(1)} %bitcast.15), channel_id=1, source_target_pairs={{0,6},{1,7},{2,4},{3,5},{4,2},{5,3},{6,0},{7,1},{8,14},{9,15},{10,... | collective-permute-start | bytes 196616 | tf_op jit(solution)/shard_map/ppermute | solution.py:236
  12.4 7.2 %collective-permute-start.8 = (f32[32,512]{1,0:T(8,128)S(1)}, f32[32,512]{1,0:T(8,128)S(1)}, u32[]{:S(2)}, u32[]{:S(2)}) collective-permute-start(f32[32,512]{1,0:T(8,128)S(1)} %bitcast.16), channel_id=1, source_target_pairs={{0,4},{1,5},{2,6},{3,7},{4,0},{5,1},{6,2},{7,3},{8,12},{9,13},{10,... | collective-permute-start | bytes 196616 | tf_op jit(solution)/shard_map/ppermute | solution.py:236
  15.9 5.6 %collective-permute-start.7 = (f32[32,512]{1,0:T(8,128)S(1)}, f32[32,512]{1,0:T(8,128)S(1)}, u32[]{:S(2)}, u32[]{:S(2)}) collective-permute-start(f32[32,512]{1,0:T(8,128)S(1)} %bitcast.17), channel_id=1, source_target_pairs={{0,2},{1,3},{2,0},{3,1},{4,6},{5,7},{6,4},{7,5},{8,10},{9,11},{10,... | collective-permute-start | bytes 196616 | tf_op jit(solution)/shard_map/ppermute | solution.py:236
  19.6 1.9 %collective-permute-start = (f32[136,128]{1,0:T(8,128)S(1)}, f32[136,128]{1,0:T(8,128)S(1)}, u32[]{:S(2)}, u32[]{:S(2)}) collective-permute-start(f32[136,128]{1,0:T(8,128)S(1)} %pad_maximum_fusion.refs_1_), channel_id=1, source_target_pairs={{0,1},{1,0},{2,3},{3,2},{4,5},{5,4},{6,7},{7,6},{8,9},{9,8},{10,11... | collective-permute-start | bytes 208904 | tf_op jit(solution)/shard_map/ppermute | solution.py:236
  19.6 1.9 %collective-permute-start.6 = (f32[136,128]{1,0:T(8,128)S(1)}, f32[136,128]{1,0:T(8,128)S(1)}, u32[]{:S(2)}, u32[]{:S(2)}) collective-permute-start(f32[136,128]{1,0:T(8,128)S(1)} %collective-permute-done.3.refs_4_), channel_id=1, source_target_pairs={{0,1},{1,0},{2,3},{3,2},{4,5},{5,4},{6,7},{7,6},{8,9},{9,8},{10,11... | collective-permute-start | bytes 208904 | tf_op jit(solution)/shard_map/ppermute | solution.py:236
  20.1 1.4 %collective-permute-start.5 = (f32[136,128]{1,0:T(8,128)S(1)}, f32[136,128]{1,0:T(8,128)S(1)}, u32[]{:S(2)}, u32[]{:S(2)}) collective-permute-start(f32[136,128]{1,0:T(8,128)S(1)} %collective-permute-done.2.refs_3_), channel_id=1, source_target_pairs={{0,1},{1,0},{2,3},{3,2},{4,5},{5,4},{6,7},{7,6},{8,9},{9,8},{10,11... | collective-permute-start | bytes 208904 | tf_op jit(solution)/shard_map/ppermute | solution.py:236
  20.2 1.4 %collective-permute-start.4 = (f32[136,128]{1,0:T(8,128)S(1)}, f32[136,128]{1,0:T(8,128)S(1)}, u32[]{:S(2)}, u32[]{:S(2)}) collective-permute-start(f32[136,128]{1,0:T(8,128)S(1)} %collective-permute-done.1.refs_2_), channel_id=1, source_target_pairs={{0,1},{1,0},{2,3},{3,2},{4,5},{5,4},{6,7},{7,6},{8,9},{9,8},{10,11... | collective-permute-start | bytes 208904 | tf_op jit(solution)/shard_map/ppermute | solution.py:236
  31.4 6.9 %collective-permute-start.10 = (f32[56,512]{1,0:T(8,128)S(1)}, f32[56,512]{1,0:T(8,128)S(1)}, u32[]{:S(2)}, u32[]{:S(2)}) collective-permute-start(f32[56,512]{1,0:T(8,128)S(1)} %get-tuple-element.11), channel_id=1, source_target_pairs={{0,8},{8,16},{16,24},{24,0},{1,9},{9,17},{17,25},{25,1},{2,10},{10... | collective-permute-start | bytes 344072 | tf_op jit(solution)/shard_map/ppermute | solution.py:241
  32.9 7.3 %collective-permute-start.11 = (f32[56,512]{1,0:T(8,128)S(1)}, f32[56,512]{1,0:T(8,128)S(1)}, u32[]{:S(2)}, u32[]{:S(2)}) collective-permute-start(f32[56,512]{1,0:T(8,128)S(1)} %get-tuple-element.12), channel_id=1, source_target_pairs={{0,24},{8,0},{16,8},{24,16},{1,25},{9,1},{17,9},{25,17},{2,26},{10... | collective-permute-start | bytes 344072 | tf_op jit(solution)/shard_map/ppermute | solution.py:241
  34.4 3.9 %collective-permute-start.12 = (f32[8,512]{1,0:T(8,128)S(1)}, f32[8,512]{1,0:T(8,128)S(1)}, u32[]{:S(2)}, u32[]{:S(2)}) collective-permute-start(f32[8,512]{1,0:T(8,128)S(1)} %get-tuple-element.10.refs_4_), channel_id=1, source_target_pairs={{0,16},{8,24},{16,0},{24,8},{1,17},{9,25},{17,1},{25,9},{2,18},{10... | collective-permute-start | bytes 49160 | tf_op jit(solution)/shard_map/ppermute | solution.py:241
  45.4 1.3 %collective-permute-start.13 = (f32[32,512]{1,0:T(8,128)S(1)}, f32[32,512]{1,0:T(8,128)S(1)}, u32[]{:S(2)}, u32[]{:S(2)}) collective-permute-start(f32[32,512]{1,0:T(8,128)S(1)} %get-tuple-element.15), channel_id=1, source_target_pairs={{0,1},{1,0},{2,3},{3,2},{4,5},{5,4},{6,7},{7,6},{8,9},{9,8},{10,11... | collective-permute-start | bytes 196616 | tf_op jit(solution)/shard_map/ppermute | solution.py:236

commit v2 on v0

v2 whole, which is shorter than its diff:
```python
import functools
import math

import jax
import jax.numpy as jnp
from jax import lax
from jax.experimental import pallas as pl
from jax.experimental.pallas import tpu as pltpu
from jax.sharding import PartitionSpec as P

HALO = 4
LANES = 128
PAD = 24
Y_BITS = 21
U_BITS = 20
INVERSE, SHIFT, Y_STRIDE, Y_MIDDLE, U_STRIDE, U_MIDDLE, MAGNIFICATION = range(7)
VMEM_LIMIT = 48 * 1024 * 1024
NT = (((1,), (1,)), ((), ()))


def rows_at(tile, index):
    return jnp.take_along_axis(tile, index, axis=0, mode="promise_in_bounds")


def by_lane(lane, depth, values):
    out = jnp.full(lane.shape, values[0])
    for q in range(1, len(values)):
        out = jnp.where(lane >= q * depth, values[q], out)
    return out


def lanes_turned(tile, by):
    lane = lax.broadcasted_iota(jnp.int32, tile.shape, 1)
    return jnp.take_along_axis(tile, lane ^ by, axis=1, mode="promise_in_bounds")


def two_parts(x):
    high = x.astype(jnp.bfloat16)
    return high, (x - high.astype(jnp.float32)).astype(jnp.bfloat16)


def inside(shape, depth, slab, slabs):
    place = lax.broadcasted_iota(jnp.int32, shape, 0)
    return ((place >= HALO) | (slab > 0)) & ((place < HALO + depth) | (slab < slabs - 1))


def pack_kernel(depth, width, volume, magnification, shift_y, shift_z, place, packed, sem):
    tiles = width // LANES
    copies = [
        pltpu.make_async_copy(
            volume.at[:, pl.ds(tile * LANES, LANES)], packed.at[pl.ds(tile * depth, depth)], sem.at[tile]
        )
        for tile in range(tiles)
    ]
    for copy in copies:
        copy.start()
    mag = magnification[...]
    n = mag.shape[1]
    offset = (width - 1) / 2.0 + shift_y[...].astype(jnp.float32)
    rows = [
        1.0 / mag,
        shift_z[...].astype(jnp.float32),
        jnp.round(8.0 * 2.0**Y_BITS / mag),
        jnp.round((0.5 / mag + offset) * 2.0**Y_BITS),
        jnp.round(8.0 * 2.0**U_BITS * mag),
        jnp.round(((width // 2 - offset) * mag + (width - 1) / 2.0) * 2.0**U_BITS),
        mag,
        mag,
    ]
    table = jnp.concatenate([jnp.concatenate(rows, axis=0), jnp.zeros((8, LANES - n), jnp.float32)], axis=1)
    packed[tiles * depth :, :] = lanes_turned(table, place[...])
    for copy in copies:
        copy.wait()


def edges_kernel(half, depth, *refs):
    proj, measured, (up, down, sums) = refs[0], refs[1 : 1 + half], refs[1 + half :]
    for j in range(half):
        up[8 * j : 8 * j + 8, :] = proj[j, depth : depth + 8, :]
        down[8 * j : 8 * j + 8, :] = proj[j, :8, :]
        at = 8 * half + HALO * j
        up[at : at + HALO, :] = measured[j][depth - HALO :, :]
        down[at : at + HALO, :] = measured[j][:HALO, :]
        sums[j : j + 1, :] = jnp.sum(proj[j], axis=0, keepdims=True)
        sums[half + j : half + j + 1, :] = jnp.sum(measured[j][...], axis=0, keepdims=True)
    at = (8 + HALO) * half
    up[at:, :] = sums[...]
    down[at:, :] = sums[...]


def forward_kernel(half, depth, width, slabs, bands, swap, added, *refs):
    info, volumes = refs[0], refs[1 : 1 + bands]
    before = refs[1 + bands] if added else None
    proj, turned, images = refs[1 + bands + added :]
    tiles = width // LANES
    per = LANES // depth
    groups = bands // per
    rows = depth + 2 * HALO
    slab = info[1]
    for g in range(groups):
        for tile in range(tiles):
            part = slice(tile * depth, (tile + 1) * depth)
            block = jnp.concatenate([volumes[g * per + q][part, :] for q in range(per)], axis=0)
            turned[g, tile * LANES : (tile + 1) * LANES, :] = block.T

    lane = lax.broadcasted_iota(jnp.int32, (8, LANES), 1)
    step = lax.broadcasted_iota(jnp.int32, (8, LANES), 0).astype(jnp.float32)
    place = lax.broadcasted_iota(jnp.int32, (rows, LANES), 0)
    wide_lane = lax.broadcasted_iota(jnp.int32, (rows, LANES), 1)
    keep = inside((rows, LANES), depth, slab, slabs)
    together = images.shape[0]

    def gather(i, g, inverse, stride, start):
        fine = step * by_lane(lane, depth, inverse)
        stride_l = by_lane(lane, depth, stride)
        start_l = by_lane(lane, depth, start)

        def eight(point, point_l):
            window = turned[g, pl.ds(point[0] >> Y_BITS, 8), :]
            for q in range(1, per):
                window = jnp.where(lane >= q * depth, turned[g, pl.ds(point[q] >> Y_BITS, 8), :], window)
            target = (point_l & (2**Y_BITS - 1)).astype(jnp.float32) * 2.0**-Y_BITS + fine
            lower = target.astype(jnp.int32)
            frac = target - lower.astype(jnp.float32)
            left = rows_at(window, lower)
            return left + frac * (rows_at(window, lower + 1) - left)

        def sixteen(block, carry):
            point, point_l = carry
            first = eight(point, point_l)
            point, point_l = [p + d for p, d in zip(point, stride)], point_l + stride_l
            pair = jnp.concatenate([first, eight(point, point_l)], axis=0)
            point, point_l = [p + d for p, d in zip(point, stride)], point_l + stride_l
            at = pl.ds(pl.multiple_of(16 * block, 16), 16)
            images[i, g, at, :LANES], images[i, g, at, LANES:] = two_parts(pair)
            return point, point_l

        lax.fori_loop(0, width // 16, sixteen, (start, start_l), unroll=8)

    def some_angles(first, carry):
        tables, whole = [], []
        for k in range(bands):
            table = volumes[k][tiles * depth :, :]
            if together < half:
                table = lanes_turned(table, first * (2 * together))
            tables.append(table)
            numbers = table.astype(jnp.int32)
            ahead = pltpu.roll(numbers, Y_MIDDLE - Y_STRIDE, 0)
            here = lax.broadcasted_iota(jnp.int32, (8, LANES), 0)
            whole.append(jnp.where(here == Y_MIDDLE, numbers - (width // 16) * ahead, numbers))

        def value(source, row, i):
            return [[source[g * per + q][row, 2 * ((g * per + q) ^ i) + swap] for q in range(per)] for g in range(groups)]

        scalars = [
            [value(tables, INVERSE, i), value(whole, Y_STRIDE, i), value(whole, Y_MIDDLE, i), value(whole, SHIFT, i)]
            for i in range(together)
        ]
        for i in range(together):
            for g in range(groups):
                gather(i, g, *[entry[g] for entry in scalars[i][:3]])
        for i in range(together):
            j = first * together + i
            total = before[j] if added else None
            for g in range(groups):
                shift_l = by_lane(wide_lane, depth, scalars[i][3][g])
                hits = (place - HALO - shift_l == (wide_lane & (depth - 1))) & keep
                select = jnp.where(hits, 1.0, 0.0).astype(jnp.bfloat16)
                select = jnp.concatenate([select, select], axis=1)
                image = lax.dot_general(select, images[i, g], NT, preferred_element_type=jnp.float32)
                total = image if total is None else total + image
            proj[j] = total
        return carry

    if together == half:
        some_angles(0, 0)
    else:
        lax.fori_loop(0, half // together, some_angles, 0)


def project_back(half, depth, width, swap, entries, held, out, stack, turned, images):
    tiles = width // LANES
    per = LANES // depth
    groups = half // per
    lane = lax.broadcasted_iota(jnp.int32, (8, LANES), 1)
    step = lax.broadcasted_iota(jnp.int32, (8, LANES), 0).astype(jnp.float32)
    place = lax.broadcasted_iota(jnp.int32, (depth, LANES), 0)
    wide_lane = lax.broadcasted_iota(jnp.int32, (depth, LANES), 1)
    select = jnp.where(place == (wide_lane & (depth - 1)), 1.0, 0.0).astype(jnp.bfloat16)
    select = jnp.concatenate([select, select], axis=1)
    turned[:PAD, :] = jnp.zeros((PAD, LANES), jnp.float32)
    turned[PAD + width :, :] = jnp.zeros((PAD, LANES), jnp.float32)
    table = entries[tiles * depth :, :]
    numbers = table.astype(jnp.int32)
    ahead = pltpu.roll(numbers, U_MIDDLE - U_STRIDE, 0)
    here = lax.broadcasted_iota(jnp.int32, (8, LANES), 0)
    numbers = jnp.where(here == U_MIDDLE, numbers - (width // 16) * ahead, numbers)

    def value(source, row, g):
        return [source[row, 2 * (g * per + q) + swap] for q in range(per)]

    total = jnp.zeros((depth, width), jnp.float32)
    for g in range(groups):
        shift = [d + HALO for d in value(numbers, SHIFT, g)]
        stride, start = value(numbers, U_STRIDE, g), value(numbers, U_MIDDLE, g)
        for tile in range(tiles):
            for q in range(per):
                stack[tile, q * depth : (q + 1) * depth, :] = held[g * per + q, tile, pl.ds(shift[q], depth), :]
            turned[PAD + tile * LANES : PAD + (tile + 1) * LANES, :] = stack[tile].T
        inverse_l = by_lane(lane, depth, value(table, INVERSE, g))
        fine = step * by_lane(lane, depth, value(table, MAGNIFICATION, g))
        stride_l = by_lane(lane, depth, stride)
        start_l = by_lane(lane, depth, start)

        def eight(point, point_l):
            base = [jnp.clip((p >> U_BITS) - 1, -PAD, width) + PAD for p in point]
            windows = [turned[pl.ds(base[0] + 8 * r, 8), :] for r in range(3)]
            for q in range(1, per):
                here = lane >= q * depth
                windows = [jnp.where(here, turned[pl.ds(base[q] + 8 * r, 8), :], windows[r]) for r in range(3)]
            target = (point_l & (2**U_BITS - 1)).astype(jnp.float32) * 2.0**-U_BITS + fine
            lower = target.astype(jnp.int32)
            frac = (target - lower.astype(jnp.float32)) * inverse_l
            out = jnp.zeros((8, LANES), jnp.float32)
            for tap in range(4):
                index = lower + tap
                within = index & 7
                value = jnp.where(index < 8, rows_at(windows[0], within), rows_at(windows[1], within))
                if tap >= 2:
                    value = jnp.where(index < 16, value, rows_at(windows[2], within))
                weight = jnp.maximum(0.0, 1.0 - jnp.abs(frac + (1.0 - tap) * inverse_l))
                out += weight * value
            return out

        def sixteen(i, carry):
            point, point_l = carry
            first = eight(point, point_l)
            point, point_l = [p + d for p, d in zip(point, stride)], point_l + stride_l
            pair = jnp.concatenate([first, eight(point, point_l)], axis=0)
            point, point_l = [p + d for p, d in zip(point, stride)], point_l + stride_l
            at = pl.ds(pl.multiple_of(16 * i, 16), 16)
            images[at, :LANES], images[at, LANES:] = two_parts(pair)
            return point, point_l

        lax.fori_loop(0, width // 16, sixteen, (start, start_l), unroll=4)
        total += lax.dot_general(select, images[...], NT, preferred_element_type=jnp.float32)
    out[...] = total * (1.0 / math.sqrt(2 * half))


def residual_kernel(half, depth, width, slabs, *refs):
    info, entries, proj, sums, from_below, from_above = refs[:6]
    others, measured = refs[6 : 6 + slabs - 3], refs[6 + slabs - 3 : 6 + slabs - 3 + half]
    residual, held, other, stack, turned, images = refs[6 + slabs - 3 + half :]
    rows = depth + 2 * HALO
    tiles = width // LANES
    edge = (8 + HALO) * half
    column = sums[...] + from_below[edge:, :] + from_above[edge:, :]
    for ref in others:
        column += ref[...]
    keep = inside((rows, LANES), depth, info[1], slabs)
    for j in range(half):
        at = 8 * half + HALO * j
        for tile in range(tiles):
            part = slice(tile * LANES, (tile + 1) * LANES)
            image = jnp.concatenate(
                [
                    proj[j, :8, part] + from_below[8 * j : 8 * j + 8, part],
                    proj[j, 8:depth, part],
                    proj[j, depth:, part] + from_above[8 * j : 8 * j + 8, part],
                ],
                axis=0,
            )
            wanted = jnp.concatenate(
                [from_below[at : at + HALO, part], measured[j][:, part], from_above[at : at + HALO, part]], axis=0
            )
            gain = column[half + j : half + j + 1, part] / column[j : j + 1, part]
            value = jnp.where(keep, (wanted - gain * image) * (1.0 / (2 * half)), 0.0)
            if j == 0:
                residual[:, part] = value[HALO : HALO + depth, :]
            held[j, tile] = value
    project_back(half, depth, width, 1, entries, held, other, stack, turned, images)


def own_kernel(half, depth, width, entries, held, out, stack, turned, images):
    project_back(half, depth, width, 0, entries, held, out, stack, turned, images)


def swapped(x, by):
    n = lax.axis_size("xband")
    return lax.ppermute(x, "xband", [(i, i ^ by) for i in range(n)])


def from_slab(x, by):
    n = lax.axis_size("zslab")
    return lax.ppermute(x, "zslab", [(i, (i + by) % n) for i in range(n)])


def shards(volume, measured, magnification, shift_y, shift_z):
    _, depth, width = volume.shape
    n, slabs = lax.axis_size("xband"), lax.axis_size("zslab")
    half = n // 2
    rows = depth + 2 * HALO
    tiles = width // LANES
    f32, bf16 = jnp.float32, jnp.bfloat16
    info = jnp.stack([lax.axis_index("xband"), lax.axis_index("zslab")]).astype(jnp.int32)

    smem = pl.BlockSpec(memory_space=pltpu.SMEM)
    vmem = pl.BlockSpec(memory_space=pltpu.VMEM)
    params = pltpu.CompilerParams(vmem_limit_bytes=VMEM_LIMIT)

    def on_core(body, shapes, operands, scratch=(), spaces={}):
        out = pl.pallas_call(
            body,
            out_shape=[jax.ShapeDtypeStruct(shape, f32) for shape in shapes],
            in_specs=[spaces.get(i, smem if x is info else vmem) for i, x in enumerate(operands)],
            out_specs=[vmem] * len(shapes),
            scratch_shapes=scratch,
            compiler_params=params,
        )(*operands)
        return out if len(shapes) > 1 else out[0]

    place = jnp.full((1, 1), lax.axis_index("xband"), jnp.int32)
    packed = on_core(
        functools.partial(pack_kernel, depth, width),
        [(tiles * depth + 8, LANES)],
        [volume[0]] + [x.reshape(1, n) for x in (magnification, shift_y, shift_z)] + [place],
        [pltpu.SemaphoreType.DMA((tiles,))],
        {0: pl.BlockSpec(memory_space=pl.ANY)},
    )
    far_first = range(half - 1, 0, -1)
    moved = {k: swapped(packed, 2 * k) for k in far_first}
    mine = [packed] + [moved[k] for k in range(1, half)]
    first_swap = swapped(packed, 1)

    view, first_swap = lax.optimization_barrier((measured[0], first_swap))
    moved = {k: swapped(view, 2 * k) for k in far_first}
    views = [view] + [moved[k] for k in range(1, half)]
    theirs = [first_swap] + [swapped(x, 1) for x in mine[1:]]

    def forward(volumes, swap, before):
        bands = len(volumes)
        return on_core(
            functools.partial(forward_kernel, half, depth, width, slabs, bands, swap, len(before)),
            [(half, rows, width)],
            [info] + volumes + before,
            [
                pltpu.VMEM((bands * depth // LANES, width, LANES), f32),
                pltpu.VMEM((min(half, 4), bands * depth // LANES, width, 2 * LANES), bf16),
            ],
        )

    proj = forward(theirs, 1, [forward(mine, 0, [])])
    edge_rows = (8 + HALO + 2) * half
    up, down, sums = on_core(
        functools.partial(edges_kernel, half, depth),
        [(edge_rows, width), (edge_rows, width), (2 * half, width)],
        [proj] + views,
    )
    below, above = from_slab(up, 1), from_slab(down, -1)
    others = [from_slab(sums, k) for k in range(2, slabs - 1)]

    scratch = [
        pltpu.VMEM((tiles, LANES, LANES), f32),
        pltpu.VMEM((width + 2 * PAD, LANES), f32),
        pltpu.VMEM((width, 2 * LANES), bf16),
    ]
    residual, held, other = on_core(
        functools.partial(residual_kernel, half, depth, width, slabs),
        [(depth, width), (half, tiles, rows, LANES), (depth, width)],
        [info, theirs[0], proj, sums, below, above] + others + views,
        scratch,
    )
    from_other = swapped(other, 1)
    own = on_core(
        functools.partial(own_kernel, half, depth, width), [(depth, width)], [mine[0], held], scratch
    )
    return residual[None], (own + from_other)[None]


def solution(mesh):
    return jax.shard_map(
        shards,
        mesh=mesh,
        in_specs=(
            P("xband", "zslab", None),
            P("xband", "zslab", None),
            P(None, "xband"),
            P(None, "xband"),
            P(None, "xband"),
        ),
        out_specs=(P("xband", "zslab", None), P("xband", "zslab", None)),
        check_vma=False,
    )
```

time: 115 us -> 33.8 us (0.29)
  waiting for transfers between devices: 38.4 us -> 5.98 us
  blocking collectives: 25.9 us -> 0 us
  matrix products: 15.7 us -> 0 us
  between operations: 14.2 us -> 0.76 us
  Pallas kernels: 0 us -> 8.66 us
  local copies, waits for them, and re-layouts: 7.08 us -> 1.51 us
  starting transfers between devices: 10.5 us -> 15.9 us
  other arithmetic: 2.33 us -> 0.72 us
    reduce_scatter x1 -> x0, waiting for transfers between devices: 34.2 us -> none  [shards(): lax.psum_scatter(forward_rows(), 'xband', scatter_dimension=0, tiled=True)]
    dot_general x2 -> x0, matrix products: 15.7 us -> none  [the longest x1 8.9 us: forward_rows(): jnp.einsum('izy,aiuy->aizu', volume, hats, precision=lax.Precision.HIGHES...]
    all_gather x1 -> x0, blocking collectives: 15.6 us -> none  [shards(): lax.all_gather(extended, 'xband', axis=0, tiled=True)]
    psum x1 -> x0, blocking collectives: 10.3 us -> none  [shards(): lax.psum((jnp.sum(measured, axis=1), jnp.sum(proj, axis=1)), 'zslab')]
    pallas_call x0 -> x6, Pallas kernels: none -> 8.66 us  [on_core(): pl.pallas_call(body, out_shape=[jax.ShapeDtypeStruct(shape, f32) for shap...]
    ppermute x4 -> x14, starting transfers between devices: 10.5 us -> 15.9 us  [the longest x11 11.4 us: swapped(): return lax.ppermute(x, 'xband', [(i, i ^ by) for i in range(n)])]
    gather x4 -> x0, local copies, waits for them, and re-layouts: 3.8 us -> none  [the longest x3 2.48 us: place(): return lax.dynamic_slice_in_dim(plane, HALO - offset, depth + 2 * HALO, 0)]
    ppermute x4 -> x14, waiting for transfers between devices: 4.23 us -> 5.98 us  [the longest x3 4.08 us: from_slab(): return lax.ppermute(x, 'zslab', [(i, (i + by) % n) for i in range(n)])]
  transfers between devices with their start and end apart: 5 -> 14, of which waited for: 2 -> 4; matrix products, arithmetic and copies ran while one was open for 1% -> 0% of each run, Pallas kernels for 0% -> 18%
where the time goes in v2:
time: 33.8 us; the launch traced here: 33.5 us
  starting transfers between devices  15.9 us (47%)
  Pallas kernels  8.66 us (26%)
  waiting for transfers between devices  5.98 us (18%)
  local copies, waits for them, and re-layouts  1.51 us (4%)
  between operations  0.76 us (2%)
  other arithmetic  0.72 us (2%)
    ppermute x11, starting transfers between devices, swapped(): return lax.ppermute(x, 'xband', [(i, i ^ by) for i in range(n)])  11.4 us
    pallas_call x6, Pallas kernels, on_core(): pl.pallas_call(body, out_shape=[jax.ShapeDtypeStruct(shape, f32) for shap...  8.66 us
    ppermute x3, starting transfers between devices, from_slab(): return lax.ppermute(x, 'zslab', [(i, (i + by) % n) for i in range(n)])  4.49 us
    ppermute x3, waiting for transfers between devices, from_slab(): return lax.ppermute(x, 'zslab', [(i, (i + by) % n) for i in range(n)])  4.08 us
    ppermute x11, waiting for transfers between devices, swapped(): return lax.ppermute(x, 'xband', [(i, i ^ by) for i in range(n)])  1.89 us
    unnamed x10, local copies, waits for them, and re-layouts  1.51 us
  transfers between devices with their start and end apart: 14, of which 4 were waited for; matrix products, arithmetic and copies ran while one was open for 0% of the time, Pallas kernels for 18%

profile of v2, /device:TPU:0, one launch (start us, length us, event | category | flops | bytes accessed | tf_op | source)
XLA Modules:
  0.0 33.5 jit_solution(6916674296151096397)
XLA Ops:
  0.7 0.6 %copy-done.2 = f32[8,1]{0,1:T(1,128)S(1)} copy-done((f32[8,1]{0,1:T(1,128)S(1)}, f32[8,1]{0,1:T(1,128)}, u32[]{:S(2)}) %copy-start.2) | copy-done | bytes 56
  1.3 0.0 copy-done.3
  1.3 0.0 copy-done.4
  1.3 0.8 %copy-done.1 = f32[1,32,512]{2,1,0:T(8,128)S(1)} copy-done((f32[1,32,512]{2,1,0:T(8,128)S(1)}, f32[1,32,512]{2,1,0:T(8,128)}, u32[]{:S(2)}) %copy-start.1) | copy-done | bytes 65560
  2.2 0.2 shard_map.68.refs_1_.entries
  2.4 5.1 %collective-permute-start.5 = (f32[136,128]{1,0:T(8,128)S(1)}, f32[136,128]{1,0:T(8,128)S(1)}, u32[]{:S(2)}, u32[]{:S(2)}) collective-permute-start(f32[136,128]{1,0:T(8,128)S(1)} %shard_map.68.refs_1_.entries), channel_id=1, source_target_pairs={{0,6},{1,7},{2,4},{3,5},{4,2},{5,3},{6,0},{7,1},{8,14},{9,15},{10,... | collective-permute-start | bytes 208904 | tf_op jit(solution)/shard_map/ppermute | solution.py:290
  7.5 0.0 collective-permute-start
  7.5 0.0 collective-permute-start.3
  7.5 0.7 %collective-permute-start.1 = (f32[136,128]{1,0:T(8,128)S(1)}, f32[136,128]{1,0:T(8,128)S(1)}, u32[]{:S(2)}, u32[]{:S(2)}) collective-permute-start(f32[136,128]{1,0:T(8,128)S(1)} %shard_map.68.refs_1_.entries), channel_id=1, source_target_pairs={{0,2},{1,3},{2,0},{3,1},{4,6},{5,7},{6,4},{7,5},{8,10},{9,11},{10,... | collective-permute-start | bytes 208904 | tf_op jit(solution)/shard_map/ppermute | solution.py:290
  8.2 1.9 %collective-permute-done.5.refs_4_ = f32[136,128]{1,0:T(8,128)S(1)} collective-permute-done((f32[136,128]{1,0:T(8,128)S(1)}, f32[136,128]{1,0:T(8,128)S(1)}, u32[]{:S(2)}, u32[]{:S(2)}) %collective-permute-start.5) | collective-permute-done | bytes 69664 | tf_op jit(solution)/shard_map/ppermute | solution.py:290
  10.1 0.0 collective-permute-done.refs_1_
  10.1 4.4 %collective-permute-start.9 = (f32[32,512]{1,0:T(8,128)S(1)}, f32[32,512]{1,0:T(8,128)S(1)}, u32[]{:S(2)}, u32[]{:S(2)}) collective-permute-start(f32[32,512]{1,0:T(8,128)S(1)} %bitcast.11), channel_id=1, source_target_pairs={{0,6},{1,7},{2,4},{3,5},{4,2},{5,3},{6,0},{7,1},{8,14},{9,15},{10,... | collective-permute-start | bytes 196616 | tf_op jit(solution)/shard_map/ppermute | solution.py:290
  14.5 0.0 collective-permute-start.8
  14.5 0.0 collective-permute-done.3.refs_3_
  14.5 0.6 %collective-permute-start.7 = (f32[32,512]{1,0:T(8,128)S(1)}, f32[32,512]{1,0:T(8,128)S(1)}, u32[]{:S(2)}, u32[]{:S(2)}) collective-permute-start(f32[32,512]{1,0:T(8,128)S(1)} %bitcast.13), channel_id=1, source_target_pairs={{0,2},{1,3},{2,0},{3,1},{4,6},{5,7},{6,4},{7,5},{8,10},{9,11},{10,... | collective-permute-start | bytes 196616 | tf_op jit(solution)/shard_map/ppermute | solution.py:290
  15.2 0.0 collective-permute-done.1.refs_2_
  15.2 0.5 %collective-permute-start.2 = (f32[136,128]{1,0:T(8,128)S(1)}, f32[136,128]{1,0:T(8,128)S(1)}, u32[]{:S(2)}, u32[]{:S(2)}) collective-permute-start(f32[136,128]{1,0:T(8,128)S(1)} %collective-permute-done.1.refs_2_), channel_id=1, source_target_pairs={{0,1},{1,0},{2,3},{3,2},{4,5},{5,4},{6,7},{7,6},{8,9},{9,8},{10,11... | collective-permute-start | bytes 208904 | tf_op jit(solution)/shard_map/ppermute | solution.py:290
  15.7 0.1 pad_add_fusion.refs_0_
  15.8 2.4 %shard_map.69.refs_5_ = f32[4,40,512]{2,1,0:T(8,128)S(1)} custom-call(s32[2]{0:T(128)S(1)} %pad_add_fusion.refs_0_, f32[136,128]{1,0:T(8,128)S(1)} %shard_map.68.refs_1_.entries, f32[136,128]{1,0:T(8,128)S(1)} %collective-permute-done.1.refs_2_, f32[136,128]{1,0:T(8,128)S(1)} %collective-permute-done.3.refs_3_, f32[136,128]{1,0:T(8,128)S(1)} %collective-permute-done.5.refs_4_), custom_call_target="tpu_custom_call" | custom-call | tf_op jit(solution)/shard_map/pallas_call | solution.py:312
  18.1 0.0 collective-permute-done.4.refs_3_
  18.2 2.4 %shard_map.70.refs_0_.refs_2_ = f32[4,40,512]{2,1,0:T(8,128)S(1)} custom-call(s32[2]{0:T(128)S(1)} %pad_add_fusion.refs_0_, f32[136,128]{1,0:T(8,128)S(1)} %collective-permute-done.refs_1_, f32[136,128]{1,0:T(8,128)S(1)} %collective-permute-done.2.refs_2_, f32[136,128]{1,0:T(8,128)S(1)} %collective-permute-done.4.refs_3_, ...), custom_call_target="tpu_custom_call" | custom-call | tf_op jit(solution)/shard_map/pallas_call | solution.py:312
  20.6 0.1 shard_map.71
  20.7 1.5 %collective-permute-start.10 = (f32[56,512]{1,0:T(8,128)S(1)}, f32[56,512]{1,0:T(8,128)S(1)}, u32[]{:S(2)}, u32[]{:S(2)}) collective-permute-start(f32[56,512]{1,0:T(8,128)S(1)} %get-tuple-element.13), channel_id=1, source_target_pairs={{0,8},{8,16},{16,24},{24,0},{1,9},{9,17},{17,25},{25,1},{2,10},{10... | collective-permute-start | bytes 344072 | tf_op jit(solution)/shard_map/ppermute | solution.py:295
  22.2 1.4 %collective-permute-start.11 = (f32[56,512]{1,0:T(8,128)S(1)}, f32[56,512]{1,0:T(8,128)S(1)}, u32[]{:S(2)}, u32[]{:S(2)}) collective-permute-start(f32[56,512]{1,0:T(8,128)S(1)} %get-tuple-element.14), channel_id=1, source_target_pairs={{0,24},{8,0},{16,8},{24,16},{1,25},{9,1},{17,9},{25,17},{2,26},{10... | collective-permute-start | bytes 344072 | tf_op jit(solution)/shard_map/ppermute | solution.py:295
  23.7 1.5 %collective-permute-start.12 = (f32[8,512]{1,0:T(8,128)S(1)}, f32[8,512]{1,0:T(8,128)S(1)}, u32[]{:S(2)}, u32[]{:S(2)}) collective-permute-start(f32[8,512]{1,0:T(8,128)S(1)} %get-tuple-element.12.refs_3_), channel_id=1, source_target_pairs={{0,16},{8,24},{16,0},{24,8},{1,17},{9,25},{17,1},{25,9},{2,18},{10... | collective-permute-start | bytes 49160 | tf_op jit(solution)/shard_map/ppermute | solution.py:295
  25.2 2.4 %collective-permute-done.12.refs_6_ = f32[8,512]{1,0:T(8,128)S(1)} collective-permute-done((f32[8,512]{1,0:T(8,128)S(1)}, f32[8,512]{1,0:T(8,128)S(1)}, u32[]{:S(2)}, u32[]{:S(2)}) %collective-permute-start.12) | collective-permute-done | bytes 16416 | tf_op jit(solution)/shard_map/ppermute | solution.py:295
  27.6 0.1 collective-permute-done.10.refs_4_
  27.6 1.6 %collective-permute-done.11.refs_5_ = f32[56,512]{1,0:T(8,128)S(1)} collective-permute-done((f32[56,512]{1,0:T(8,128)S(1)}, f32[56,512]{1,0:T(8,128)S(1)}, u32[]{:S(2)}, u32[]{:S(2)}) %collective-permute-start.11) | collective-permute-done | bytes 114720 | tf_op jit(solution)/shard_map/ppermute | solution.py:295
  29.3 2.3 %shard_map.72 = (f32[32,512]{1,0:T(8,128)}, f32[4,4,40,128]{3,2,1,0:T(8,128)S(1)}, f32[32,512]{1,0:T(8,128)S(1)}) custom-call(s32[2]{0:T(128)S(1)} %pad_add_fusion.refs_0_, f32[136,128]{1,0:T(8,128)S(1)} %collective-permute-done.refs_1_, f32[4,40,512]{2,1,0:T(8,128)S(1)} %shard_map.70.refs_0_.refs_2_, f32[8,512]{1,0:T(8,128)S(1)} %get-tuple-element.12.refs_3_, ...), custom_call_target="tpu_custom_call" | custom-call | tf_op jit(solution)/shard_map/pallas_call | solution.py:312
  31.6 1.3 %shard_map.73 = f32[32,512]{1,0:T(8,128)S(1)} custom-call(f32[136,128]{1,0:T(8,128)S(1)} %shard_map.68.refs_1_.entries, f32[4,4,40,128]{3,2,1,0:T(8,128)S(1)} %get-tuple-element.16.held), custom_call_target="tpu_custom_call" | custom-call | tf_op jit(solution)/shard_map/pallas_call | solution.py:312
  32.9 0.0 collective-permute-done.13
  32.9 0.6 %add_bitcast_fusion = f32[1,32,512]{2,1,0:T(8,128)} fusion(f32[32,512]{1,0:T(8,128)S(1)} %shard_map.73, f32[32,512]{1,0:T(8,128)S(1)} %collective-permute-done.13), kind=kLoop, calls=%fused_computation | loop fusion | flops 16384 | bytes 196608 | tf_op jit(solution)/shard_map/broadcast_in_dim | solution.py:377
  (14 shorter events, 0.0 us)
Async XLA Ops:
  0.6 0.7 %copy-start.2 = (f32[8,1]{0,1:T(1,128)S(1)}, f32[8,1]{0,1:T(1,128)}, u32[]{:S(2)}) copy-start(f32[8,1]{0,1:T(1,128)} %param.7) | copy-start | bytes 100
  0.6 0.7 %copy-start.3 = (s32[8,1]{0,1:T(1,128)S(1)}, s32[8,1]{0,1:T(1,128)}, u32[]{:S(2)}) copy-start(s32[8,1]{0,1:T(1,128)} %param.8) | copy-start | bytes 100
  0.7 0.7 %copy-start.4 = (s32[8,1]{0,1:T(1,128)S(1)}, s32[8,1]{0,1:T(1,128)}, u32[]{:S(2)}) copy-start(s32[8,1]{0,1:T(1,128)} %param.9) | copy-start | bytes 100
  1.3 0.8 %copy-start.1 = (f32[1,32,512]{2,1,0:T(8,128)S(1)}, f32[1,32,512]{2,1,0:T(8,128)}, u32[]{:S(2)}) copy-start(f32[1,32,512]{2,1,0:T(8,128)} %param.5) | copy-start | bytes 196612
  2.2 7.9 %copy-start = (f32[1,32,512]{2,1,0:T(8,128)S(1)}, f32[1,32,512]{2,1,0:T(8,128)}, u32[]{:S(2)}) copy-start(f32[1,32,512]{2,1,0:T(8,128)} %param.6) | copy-start | bytes 196612
  2.4 7.7 %collective-permute-start.5 = (f32[136,128]{1,0:T(8,128)S(1)}, f32[136,128]{1,0:T(8,128)S(1)}, u32[]{:S(2)}, u32[]{:S(2)}) collective-permute-start(f32[136,128]{1,0:T(8,128)S(1)} %shard_map.68.refs_1_.entries), channel_id=1, source_target_pairs={{0,6},{1,7},{2,4},{3,5},{4,2},{5,3},{6,0},{7,1},{8,14},{9,15},{10,... | collective-permute-start | bytes 208904 | tf_op jit(solution)/shard_map/ppermute | solution.py:290
  7.5 2.6 %collective-permute-start = (f32[136,128]{1,0:T(8,128)S(1)}, f32[136,128]{1,0:T(8,128)S(1)}, u32[]{:S(2)}, u32[]{:S(2)}) collective-permute-start(f32[136,128]{1,0:T(8,128)S(1)} %shard_map.68.refs_1_.entries), channel_id=1, source_target_pairs={{0,1},{1,0},{2,3},{3,2},{4,5},{5,4},{6,7},{7,6},{8,9},{9,8},{10,11... | collective-permute-start | bytes 208904 | tf_op jit(solution)/shard_map/ppermute | solution.py:290
  7.5 7.0 %collective-permute-start.3 = (f32[136,128]{1,0:T(8,128)S(1)}, f32[136,128]{1,0:T(8,128)S(1)}, u32[]{:S(2)}, u32[]{:S(2)}) collective-permute-start(f32[136,128]{1,0:T(8,128)S(1)} %shard_map.68.refs_1_.entries), channel_id=1, source_target_pairs={{0,4},{1,5},{2,6},{3,7},{4,0},{5,1},{6,2},{7,3},{8,12},{9,13},{10,... | collective-permute-start | bytes 208904 | tf_op jit(solution)/shard_map/ppermute | solution.py:290
  7.5 7.7 %collective-permute-start.1 = (f32[136,128]{1,0:T(8,128)S(1)}, f32[136,128]{1,0:T(8,128)S(1)}, u32[]{:S(2)}, u32[]{:S(2)}) collective-permute-start(f32[136,128]{1,0:T(8,128)S(1)} %shard_map.68.refs_1_.entries), channel_id=1, source_target_pairs={{0,2},{1,3},{2,0},{3,1},{4,6},{5,7},{6,4},{7,5},{8,10},{9,11},{10,... | collective-permute-start | bytes 208904 | tf_op jit(solution)/shard_map/ppermute | solution.py:290
  10.1 5.1 %collective-permute-start.6 = (f32[136,128]{1,0:T(8,128)S(1)}, f32[136,128]{1,0:T(8,128)S(1)}, u32[]{:S(2)}, u32[]{:S(2)}) collective-permute-start(f32[136,128]{1,0:T(8,128)S(1)} %collective-permute-done.5.refs_4_), channel_id=1, source_target_pairs={{0,1},{1,0},{2,3},{3,2},{4,5},{5,4},{6,7},{7,6},{8,9},{9,8},{10,11... | collective-permute-start | bytes 208904 | tf_op jit(solution)/shard_map/ppermute | solution.py:290
  10.1 10.5 %collective-permute-start.9 = (f32[32,512]{1,0:T(8,128)S(1)}, f32[32,512]{1,0:T(8,128)S(1)}, u32[]{:S(2)}, u32[]{:S(2)}) collective-permute-start(f32[32,512]{1,0:T(8,128)S(1)} %bitcast.11), channel_id=1, source_target_pairs={{0,6},{1,7},{2,4},{3,5},{4,2},{5,3},{6,0},{7,1},{8,14},{9,15},{10,... | collective-permute-start | bytes 196616 | tf_op jit(solution)/shard_map/ppermute | solution.py:290
  14.5 6.1 %collective-permute-start.8 = (f32[32,512]{1,0:T(8,128)S(1)}, f32[32,512]{1,0:T(8,128)S(1)}, u32[]{:S(2)}, u32[]{:S(2)}) collective-permute-start(f32[32,512]{1,0:T(8,128)S(1)} %bitcast.12), channel_id=1, source_target_pairs={{0,4},{1,5},{2,6},{3,7},{4,0},{5,1},{6,2},{7,3},{8,12},{9,13},{10,... | collective-permute-start | bytes 196616 | tf_op jit(solution)/shard_map/ppermute | solution.py:290
  14.5 6.1 %collective-permute-start.7 = (f32[32,512]{1,0:T(8,128)S(1)}, f32[32,512]{1,0:T(8,128)S(1)}, u32[]{:S(2)}, u32[]{:S(2)}) collective-permute-start(f32[32,512]{1,0:T(8,128)S(1)} %bitcast.13), channel_id=1, source_target_pairs={{0,2},{1,3},{2,0},{3,1},{4,6},{5,7},{6,4},{7,5},{8,10},{9,11},{10,... | collective-permute-start | bytes 196616 | tf_op jit(solution)/shard_map/ppermute | solution.py:290
  15.2 3.0 %collective-permute-start.4 = (f32[136,128]{1,0:T(8,128)S(1)}, f32[136,128]{1,0:T(8,128)S(1)}, u32[]{:S(2)}, u32[]{:S(2)}) collective-permute-start(f32[136,128]{1,0:T(8,128)S(1)} %collective-permute-done.3.refs_3_), channel_id=1, source_target_pairs={{0,1},{1,0},{2,3},{3,2},{4,5},{5,4},{6,7},{7,6},{8,9},{9,8},{10,11... | collective-permute-start | bytes 208904 | tf_op jit(solution)/shard_map/ppermute | solution.py:290
  15.2 3.0 %collective-permute-start.2 = (f32[136,128]{1,0:T(8,128)S(1)}, f32[136,128]{1,0:T(8,128)S(1)}, u32[]{:S(2)}, u32[]{:S(2)}) collective-permute-start(f32[136,128]{1,0:T(8,128)S(1)} %collective-permute-done.1.refs_2_), channel_id=1, source_target_pairs={{0,1},{1,0},{2,3},{3,2},{4,5},{5,4},{6,7},{7,6},{8,9},{9,8},{10,11... | collective-permute-start | bytes 208904 | tf_op jit(solution)/shard_map/ppermute | solution.py:290
  20.7 6.9 %collective-permute-start.10 = (f32[56,512]{1,0:T(8,128)S(1)}, f32[56,512]{1,0:T(8,128)S(1)}, u32[]{:S(2)}, u32[]{:S(2)}) collective-permute-start(f32[56,512]{1,0:T(8,128)S(1)} %get-tuple-element.13), channel_id=1, source_target_pairs={{0,8},{8,16},{16,24},{24,0},{1,9},{9,17},{17,25},{25,1},{2,10},{10... | collective-permute-start | bytes 344072 | tf_op jit(solution)/shard_map/ppermute | solution.py:295
  22.2 7.0 %collective-permute-start.11 = (f32[56,512]{1,0:T(8,128)S(1)}, f32[56,512]{1,0:T(8,128)S(1)}, u32[]{:S(2)}, u32[]{:S(2)}) collective-permute-start(f32[56,512]{1,0:T(8,128)S(1)} %get-tuple-element.14), channel_id=1, source_target_pairs={{0,24},{8,0},{16,8},{24,16},{1,25},{9,1},{17,9},{25,17},{2,26},{10... | collective-permute-start | bytes 344072 | tf_op jit(solution)/shard_map/ppermute | solution.py:295
  23.7 3.9 %collective-permute-start.12 = (f32[8,512]{1,0:T(8,128)S(1)}, f32[8,512]{1,0:T(8,128)S(1)}, u32[]{:S(2)}, u32[]{:S(2)}) collective-permute-start(f32[8,512]{1,0:T(8,128)S(1)} %get-tuple-element.12.refs_3_), channel_id=1, source_target_pairs={{0,16},{8,24},{16,0},{24,8},{1,17},{9,25},{17,1},{25,9},{2,18},{10... | collective-permute-start | bytes 49160 | tf_op jit(solution)/shard_map/ppermute | solution.py:295
  31.6 1.3 %collective-permute-start.13 = (f32[32,512]{1,0:T(8,128)S(1)}, f32[32,512]{1,0:T(8,128)S(1)}, u32[]{:S(2)}, u32[]{:S(2)}) collective-permute-start(f32[32,512]{1,0:T(8,128)S(1)} %get-tuple-element.17), channel_id=1, source_target_pairs={{0,1},{1,0},{2,3},{3,2},{4,5},{5,4},{6,7},{7,6},{8,9},{9,8},{10,11... | collective-permute-start | bytes 196616 | tf_op jit(solution)/shard_map/ppermute | solution.py:290

commit v3 on v2

--- a/solution.py
+++ b/solution.py
@@ -44,8 +44,13 @@
     return ((place >= HALO) | (slab > 0)) & ((place < HALO + depth) | (slab < slabs - 1))
 
 
-def pack_kernel(depth, width, volume, magnification, shift_y, shift_z, place, packed, sem):
+def pack_kernel(depth, width, volume, *refs):
+    small, place, packed, held, sem = refs[:3], refs[3], refs[4], refs[5:8], refs[8]
+    magnification, shift_y, shift_z = held
     tiles = width // LANES
+    small_copies = [pltpu.make_async_copy(x, y, sem.at[tiles + i]) for i, (x, y) in enumerate(zip(small, held))]
+    for copy in small_copies:
+        copy.start()
     copies = [
         pltpu.make_async_copy(
             volume.at[:, pl.ds(tile * LANES, LANES)], packed.at[pl.ds(tile * depth, depth)], sem.at[tile]
@@ -54,6 +59,8 @@
     ]
     for copy in copies:
         copy.start()
+    for copy in small_copies:
+        copy.wait()
     mag = magnification[...]
     n = mag.shape[1]
     offset = (width - 1) / 2.0 + shift_y[...].astype(jnp.float32)
@@ -323,9 +330,18 @@
     packed = on_core(
         functools.partial(pack_kernel, depth, width),
         [(tiles * depth + 8, LANES)],
-        [volume[0]] + [x.reshape(1, n) for x in (magnification, shift_y, shift_z)] + [place],
-        [pltpu.SemaphoreType.DMA((tiles,))],
-        {0: pl.BlockSpec(memory_space=pl.ANY)},
+        [
+            pltpu.with_memory_space_constraint(x, pltpu.HBM)
+            for x in (volume[0], magnification.reshape(1, n), shift_y.reshape(1, n), shift_z.reshape(1, n))
+        ]
+        + [place],
+        [
+            pltpu.VMEM((1, n), f32),
+            pltpu.VMEM((1, n), jnp.int32),
+            pltpu.VMEM((1, n), jnp.int32),
+            pltpu.SemaphoreType.DMA((tiles + 3,)),
+        ],
+        {i: pl.BlockSpec(memory_space=pl.ANY) for i in range(4)},
     )
     far_first = range(half - 1, 0, -1)
     moved = {k: swapped(packed, 2 * k) for k in far_first}

time: 33.8 us -> 33 us (0.976)
  local copies, waits for them, and re-layouts: 1.51 us -> 0.01 us
  Pallas kernels: 8.66 us -> 9.4 us
    unnamed x10 -> x2, local copies, waits for them, and re-layouts: 1.51 us -> 0.01 us
    pallas_call x6, Pallas kernels: 8.66 us -> 9.4 us  [on_core(): pl.pallas_call(body, out_shape=[jax.ShapeDtypeStruct(shape, f32) for shap...]
  transfers between devices with their start and end apart: 14 -> 14, of which waited for: 4 -> 4; matrix products, arithmetic and copies ran while one was open for 0% -> 0% of each run, Pallas kernels for 18% -> 19%
where the time goes in v3:
time: 33 us; the launch traced here: 32.8 us
  starting transfers between devices  15.9 us (48%)
  Pallas kernels  9.4 us (28%)
  waiting for transfers between devices  5.98 us (18%)
  between operations  0.74 us (2%)
  other arithmetic  0.72 us (2%)
    ppermute x11, starting transfers between devices, swapped(): return lax.ppermute(x, 'xband', [(i, i ^ by) for i in range(n)])  11.4 us
    pallas_call x6, Pallas kernels, on_core(): pl.pallas_call(body, out_shape=[jax.ShapeDtypeStruct(shape, f32) for shap...  9.4 us
    ppermute x3, starting transfers between devices, from_slab(): return lax.ppermute(x, 'zslab', [(i, (i + by) % n) for i in range(n)])  4.49 us
    ppermute x3, waiting for transfers between devices, from_slab(): return lax.ppermute(x, 'zslab', [(i, (i + by) % n) for i in range(n)])  4.08 us
    ppermute x11, waiting for transfers between devices, swapped(): return lax.ppermute(x, 'xband', [(i, i ^ by) for i in range(n)])  1.89 us
  transfers between devices with their start and end apart: 14, of which 4 were waited for; matrix products, arithmetic and copies ran while one was open for 0% of the time, Pallas kernels for 19%

profile of v3, /device:TPU:0, one launch (start us, length us, event | category | flops | bytes accessed | tf_op | source)
XLA Modules:
  0.0 32.8 jit_solution(8382816838286101780)
XLA Ops:
  0.6 0.9 %shard_map.68.refs_1_.entries = f32[136,128]{1,0:T(8,128)S(1)} custom-call(f32[32,512]{1,0:T(8,128)} %bitcast.16, f32[1,8]{1,0:T(1,128)} %bitcast.17, s32[1,8]{1,0:T(1,128)} %bitcast.18, s32[1,8]{1,0:T(1,128)} %bitcast.19, s32[1,1]{1,0:T(1,128)} %bitcast.7.refs_3_), custom_call_target="tpu_custom_call" | custom-call | tf_op jit(solution)/shard_map/pallas_call | solution.py:319
  1.6 5.1 %collective-permute-start.5 = (f32[136,128]{1,0:T(8,128)S(1)}, f32[136,128]{1,0:T(8,128)S(1)}, u32[]{:S(2)}, u32[]{:S(2)}) collective-permute-start(f32[136,128]{1,0:T(8,128)S(1)} %shard_map.68.refs_1_.entries), channel_id=1, source_target_pairs={{0,6},{1,7},{2,4},{3,5},{4,2},{5,3},{6,0},{7,1},{8,14},{9,15},{10,... | collective-permute-start | bytes 208904 | tf_op jit(solution)/shard_map/ppermute | solution.py:297
  6.7 0.0 collective-permute-start
  6.7 0.0 collective-permute-start.3
  6.7 0.7 %collective-permute-start.1 = (f32[136,128]{1,0:T(8,128)S(1)}, f32[136,128]{1,0:T(8,128)S(1)}, u32[]{:S(2)}, u32[]{:S(2)}) collective-permute-start(f32[136,128]{1,0:T(8,128)S(1)} %shard_map.68.refs_1_.entries), channel_id=1, source_target_pairs={{0,2},{1,3},{2,0},{3,1},{4,6},{5,7},{6,4},{7,5},{8,10},{9,11},{10,... | collective-permute-start | bytes 208904 | tf_op jit(solution)/shard_map/ppermute | solution.py:297
  7.4 1.9 %collective-permute-done.5.refs_4_ = f32[136,128]{1,0:T(8,128)S(1)} collective-permute-done((f32[136,128]{1,0:T(8,128)S(1)}, f32[136,128]{1,0:T(8,128)S(1)}, u32[]{:S(2)}, u32[]{:S(2)}) %collective-permute-start.5) | collective-permute-done | bytes 69664 | tf_op jit(solution)/shard_map/ppermute | solution.py:297
  9.3 0.0 collective-permute-start.6
  9.3 0.0 collective-permute-done.refs_1_
  9.3 4.4 %collective-permute-start.9 = (f32[32,512]{1,0:T(8,128)S(1)}, f32[32,512]{1,0:T(8,128)S(1)}, u32[]{:S(2)}, u32[]{:S(2)}) collective-permute-start(f32[32,512]{1,0:T(8,128)S(1)} %bitcast.11), channel_id=1, source_target_pairs={{0,6},{1,7},{2,4},{3,5},{4,2},{5,3},{6,0},{7,1},{8,14},{9,15},{10,... | collective-permute-start | bytes 196616 | tf_op jit(solution)/shard_map/ppermute | solution.py:297
  13.7 0.0 collective-permute-start.8
  13.7 0.0 collective-permute-done.3.refs_3_
  13.7 0.6 %collective-permute-start.7 = (f32[32,512]{1,0:T(8,128)S(1)}, f32[32,512]{1,0:T(8,128)S(1)}, u32[]{:S(2)}, u32[]{:S(2)}) collective-permute-start(f32[32,512]{1,0:T(8,128)S(1)} %bitcast.13), channel_id=1, source_target_pairs={{0,2},{1,3},{2,0},{3,1},{4,6},{5,7},{6,4},{7,5},{8,10},{9,11},{10,... | collective-permute-start | bytes 196616 | tf_op jit(solution)/shard_map/ppermute | solution.py:297
  14.4 0.0 collective-permute-done.6.refs_4_
  14.4 0.5 %collective-permute-start.2 = (f32[136,128]{1,0:T(8,128)S(1)}, f32[136,128]{1,0:T(8,128)S(1)}, u32[]{:S(2)}, u32[]{:S(2)}) collective-permute-start(f32[136,128]{1,0:T(8,128)S(1)} %collective-permute-done.1.refs_2_), channel_id=1, source_target_pairs={{0,1},{1,0},{2,3},{3,2},{4,5},{5,4},{6,7},{7,6},{8,9},{9,8},{10,11... | collective-permute-start | bytes 208904 | tf_op jit(solution)/shard_map/ppermute | solution.py:297
  14.9 0.1 pad_add_fusion.refs_0_
  15.0 2.4 %shard_map.69.refs_5_ = f32[4,40,512]{2,1,0:T(8,128)S(1)} custom-call(s32[2]{0:T(128)S(1)} %pad_add_fusion.refs_0_, f32[136,128]{1,0:T(8,128)S(1)} %shard_map.68.refs_1_.entries, f32[136,128]{1,0:T(8,128)S(1)} %collective-permute-done.1.refs_2_, f32[136,128]{1,0:T(8,128)S(1)} %collective-permute-done.3.refs_3_, f32[136,128]{1,0:T(8,128)S(1)} %collective-permute-done.5.refs_4_), custom_call_target="tpu_custom_call" | custom-call | tf_op jit(solution)/shard_map/pallas_call | solution.py:319
  17.4 0.0 collective-permute-done.4.refs_3_
  17.4 0.0 collective-permute-done.2.refs_2_
  17.4 2.4 %shard_map.70.refs_0_.refs_2_ = f32[4,40,512]{2,1,0:T(8,128)S(1)} custom-call(s32[2]{0:T(128)S(1)} %pad_add_fusion.refs_0_, f32[136,128]{1,0:T(8,128)S(1)} %collective-permute-done.refs_1_, f32[136,128]{1,0:T(8,128)S(1)} %collective-permute-done.2.refs_2_, f32[136,128]{1,0:T(8,128)S(1)} %collective-permute-done.4.refs_3_, ...), custom_call_target="tpu_custom_call" | custom-call | tf_op jit(solution)/shard_map/pallas_call | solution.py:319
  19.8 0.0 collective-permute-done.8.refs_3_.refs_9_
  19.8 0.0 collective-permute-done.7.refs_2_.refs_8_
  19.8 0.1 shard_map.71
  19.9 1.5 %collective-permute-start.10 = (f32[56,512]{1,0:T(8,128)S(1)}, f32[56,512]{1,0:T(8,128)S(1)}, u32[]{:S(2)}, u32[]{:S(2)}) collective-permute-start(f32[56,512]{1,0:T(8,128)S(1)} %get-tuple-element.13), channel_id=1, source_target_pairs={{0,8},{8,16},{16,24},{24,0},{1,9},{9,17},{17,25},{25,1},{2,10},{10... | collective-permute-start | bytes 344072 | tf_op jit(solution)/shard_map/ppermute | solution.py:302
  21.5 1.4 %collective-permute-start.11 = (f32[56,512]{1,0:T(8,128)S(1)}, f32[56,512]{1,0:T(8,128)S(1)}, u32[]{:S(2)}, u32[]{:S(2)}) collective-permute-start(f32[56,512]{1,0:T(8,128)S(1)} %get-tuple-element.14), channel_id=1, source_target_pairs={{0,24},{8,0},{16,8},{24,16},{1,25},{9,1},{17,9},{25,17},{2,26},{10... | collective-permute-start | bytes 344072 | tf_op jit(solution)/shard_map/ppermute | solution.py:302
  22.9 1.5 %collective-permute-start.12 = (f32[8,512]{1,0:T(8,128)S(1)}, f32[8,512]{1,0:T(8,128)S(1)}, u32[]{:S(2)}, u32[]{:S(2)}) collective-permute-start(f32[8,512]{1,0:T(8,128)S(1)} %get-tuple-element.12.refs_3_), channel_id=1, source_target_pairs={{0,16},{8,24},{16,0},{24,8},{1,17},{9,25},{17,1},{25,9},{2,18},{10... | collective-permute-start | bytes 49160 | tf_op jit(solution)/shard_map/ppermute | solution.py:302
  24.4 2.4 %collective-permute-done.12.refs_6_ = f32[8,512]{1,0:T(8,128)S(1)} collective-permute-done((f32[8,512]{1,0:T(8,128)S(1)}, f32[8,512]{1,0:T(8,128)S(1)}, u32[]{:S(2)}, u32[]{:S(2)}) %collective-permute-start.12) | collective-permute-done | bytes 16416 | tf_op jit(solution)/shard_map/ppermute | solution.py:302
  26.8 0.1 collective-permute-done.10.refs_4_
  26.9 1.6 %collective-permute-done.11.refs_5_ = f32[56,512]{1,0:T(8,128)S(1)} collective-permute-done((f32[56,512]{1,0:T(8,128)S(1)}, f32[56,512]{1,0:T(8,128)S(1)}, u32[]{:S(2)}, u32[]{:S(2)}) %collective-permute-start.11) | collective-permute-done | bytes 114720 | tf_op jit(solution)/shard_map/ppermute | solution.py:302
  28.5 2.3 %shard_map.72 = (f32[32,512]{1,0:T(8,128)}, f32[4,4,40,128]{3,2,1,0:T(8,128)S(1)}, f32[32,512]{1,0:T(8,128)S(1)}) custom-call(s32[2]{0:T(128)S(1)} %pad_add_fusion.refs_0_, f32[136,128]{1,0:T(8,128)S(1)} %collective-permute-done.refs_1_, f32[4,40,512]{2,1,0:T(8,128)S(1)} %shard_map.70.refs_0_.refs_2_, f32[8,512]{1,0:T(8,128)S(1)} %get-tuple-element.12.refs_3_, ...), custom_call_target="tpu_custom_call" | custom-call | tf_op jit(solution)/shard_map/pallas_call | solution.py:319
  30.8 1.3 %shard_map.73 = f32[32,512]{1,0:T(8,128)S(1)} custom-call(f32[136,128]{1,0:T(8,128)S(1)} %shard_map.68.refs_1_.entries, f32[4,4,40,128]{3,2,1,0:T(8,128)S(1)} %get-tuple-element.16.held), custom_call_target="tpu_custom_call" | custom-call | tf_op jit(solution)/shard_map/pallas_call | solution.py:319
  32.1 0.0 collective-permute-done.13
  32.1 0.6 %add_bitcast_fusion = f32[1,32,512]{2,1,0:T(8,128)} fusion(f32[32,512]{1,0:T(8,128)S(1)} %shard_map.73, f32[32,512]{1,0:T(8,128)S(1)} %collective-permute-done.13), kind=kLoop, calls=%fused_computation | loop fusion | flops 16384 | bytes 196608 | tf_op jit(solution)/shard_map/broadcast_in_dim | solution.py:393
  (6 shorter events, 0.0 us)
Async XLA Ops:
  0.6 8.6 %copy-start = (f32[1,32,512]{2,1,0:T(8,128)S(1)}, f32[1,32,512]{2,1,0:T(8,128)}, u32[]{:S(2)}) copy-start(f32[1,32,512]{2,1,0:T(8,128)} %param.6) | copy-start | bytes 196612
  1.6 7.7 %collective-permute-start.5 = (f32[136,128]{1,0:T(8,128)S(1)}, f32[136,128]{1,0:T(8,128)S(1)}, u32[]{:S(2)}, u32[]{:S(2)}) collective-permute-start(f32[136,128]{1,0:T(8,128)S(1)} %shard_map.68.refs_1_.entries), channel_id=1, source_target_pairs={{0,6},{1,7},{2,4},{3,5},{4,2},{5,3},{6,0},{7,1},{8,14},{9,15},{10,... | collective-permute-start | bytes 208904 | tf_op jit(solution)/shard_map/ppermute | solution.py:297
  6.7 2.6 %collective-permute-start = (f32[136,128]{1,0:T(8,128)S(1)}, f32[136,128]{1,0:T(8,128)S(1)}, u32[]{:S(2)}, u32[]{:S(2)}) collective-permute-start(f32[136,128]{1,0:T(8,128)S(1)} %shard_map.68.refs_1_.entries), channel_id=1, source_target_pairs={{0,1},{1,0},{2,3},{3,2},{4,5},{5,4},{6,7},{7,6},{8,9},{9,8},{10,11... | collective-permute-start | bytes 208904 | tf_op jit(solution)/shard_map/ppermute | solution.py:297
  6.7 7.0 %collective-permute-start.3 = (f32[136,128]{1,0:T(8,128)S(1)}, f32[136,128]{1,0:T(8,128)S(1)}, u32[]{:S(2)}, u32[]{:S(2)}) collective-permute-start(f32[136,128]{1,0:T(8,128)S(1)} %shard_map.68.refs_1_.entries), channel_id=1, source_target_pairs={{0,4},{1,5},{2,6},{3,7},{4,0},{5,1},{6,2},{7,3},{8,12},{9,13},{10,... | collective-permute-start | bytes 208904 | tf_op jit(solution)/shard_map/ppermute | solution.py:297
  6.7 7.7 %collective-permute-start.1 = (f32[136,128]{1,0:T(8,128)S(1)}, f32[136,128]{1,0:T(8,128)S(1)}, u32[]{:S(2)}, u32[]{:S(2)}) collective-permute-start(f32[136,128]{1,0:T(8,128)S(1)} %shard_map.68.refs_1_.entries), channel_id=1, source_target_pairs={{0,2},{1,3},{2,0},{3,1},{4,6},{5,7},{6,4},{7,5},{8,10},{9,11},{10,... | collective-permute-start | bytes 208904 | tf_op jit(solution)/shard_map/ppermute | solution.py:297
  9.3 5.1 %collective-permute-start.6 = (f32[136,128]{1,0:T(8,128)S(1)}, f32[136,128]{1,0:T(8,128)S(1)}, u32[]{:S(2)}, u32[]{:S(2)}) collective-permute-start(f32[136,128]{1,0:T(8,128)S(1)} %collective-permute-done.5.refs_4_), channel_id=1, source_target_pairs={{0,1},{1,0},{2,3},{3,2},{4,5},{5,4},{6,7},{7,6},{8,9},{9,8},{10,11... | collective-permute-start | bytes 208904 | tf_op jit(solution)/shard_map/ppermute | solution.py:297
  9.3 10.5 %collective-permute-start.9 = (f32[32,512]{1,0:T(8,128)S(1)}, f32[32,512]{1,0:T(8,128)S(1)}, u32[]{:S(2)}, u32[]{:S(2)}) collective-permute-start(f32[32,512]{1,0:T(8,128)S(1)} %bitcast.11), channel_id=1, source_target_pairs={{0,6},{1,7},{2,4},{3,5},{4,2},{5,3},{6,0},{7,1},{8,14},{9,15},{10,... | collective-permute-start | bytes 196616 | tf_op jit(solution)/shard_map/ppermute | solution.py:297
  13.7 6.1 %collective-permute-start.8 = (f32[32,512]{1,0:T(8,128)S(1)}, f32[32,512]{1,0:T(8,128)S(1)}, u32[]{:S(2)}, u32[]{:S(2)}) collective-permute-start(f32[32,512]{1,0:T(8,128)S(1)} %bitcast.12), channel_id=1, source_target_pairs={{0,4},{1,5},{2,6},{3,7},{4,0},{5,1},{6,2},{7,3},{8,12},{9,13},{10,... | collective-permute-start | bytes 196616 | tf_op jit(solution)/shard_map/ppermute | solution.py:297
  13.7 6.1 %collective-permute-start.7 = (f32[32,512]{1,0:T(8,128)S(1)}, f32[32,512]{1,0:T(8,128)S(1)}, u32[]{:S(2)}, u32[]{:S(2)}) collective-permute-start(f32[32,512]{1,0:T(8,128)S(1)} %bitcast.13), channel_id=1, source_target_pairs={{0,2},{1,3},{2,0},{3,1},{4,6},{5,7},{6,4},{7,5},{8,10},{9,11},{10,... | collective-permute-start | bytes 196616 | tf_op jit(solution)/shard_map/ppermute | solution.py:297
  14.4 3.0 %collective-permute-start.4 = (f32[136,128]{1,0:T(8,128)S(1)}, f32[136,128]{1,0:T(8,128)S(1)}, u32[]{:S(2)}, u32[]{:S(2)}) collective-permute-start(f32[136,128]{1,0:T(8,128)S(1)} %collective-permute-done.3.refs_3_), channel_id=1, source_target_pairs={{0,1},{1,0},{2,3},{3,2},{4,5},{5,4},{6,7},{7,6},{8,9},{9,8},{10,11... | collective-permute-start | bytes 208904 | tf_op jit(solution)/shard_map/ppermute | solution.py:297
  14.4 3.0 %collective-permute-start.2 = (f32[136,128]{1,0:T(8,128)S(1)}, f32[136,128]{1,0:T(8,128)S(1)}, u32[]{:S(2)}, u32[]{:S(2)}) collective-permute-start(f32[136,128]{1,0:T(8,128)S(1)} %collective-permute-done.1.refs_2_), channel_id=1, source_target_pairs={{0,1},{1,0},{2,3},{3,2},{4,5},{5,4},{6,7},{7,6},{8,9},{9,8},{10,11... | collective-permute-start | bytes 208904 | tf_op jit(solution)/shard_map/ppermute | solution.py:297
  19.9 7.0 %collective-permute-start.10 = (f32[56,512]{1,0:T(8,128)S(1)}, f32[56,512]{1,0:T(8,128)S(1)}, u32[]{:S(2)}, u32[]{:S(2)}) collective-permute-start(f32[56,512]{1,0:T(8,128)S(1)} %get-tuple-element.13), channel_id=1, source_target_pairs={{0,8},{8,16},{16,24},{24,0},{1,9},{9,17},{17,25},{25,1},{2,10},{10... | collective-permute-start | bytes 344072 | tf_op jit(solution)/shard_map/ppermute | solution.py:302
  21.5 7.0 %collective-permute-start.11 = (f32[56,512]{1,0:T(8,128)S(1)}, f32[56,512]{1,0:T(8,128)S(1)}, u32[]{:S(2)}, u32[]{:S(2)}) collective-permute-start(f32[56,512]{1,0:T(8,128)S(1)} %get-tuple-element.14), channel_id=1, source_target_pairs={{0,24},{8,0},{16,8},{24,16},{1,25},{9,1},{17,9},{25,17},{2,26},{10... | collective-permute-start | bytes 344072 | tf_op jit(solution)/shard_map/ppermute | solution.py:302
  22.9 3.9 %collective-permute-start.12 = (f32[8,512]{1,0:T(8,128)S(1)}, f32[8,512]{1,0:T(8,128)S(1)}, u32[]{:S(2)}, u32[]{:S(2)}) collective-permute-start(f32[8,512]{1,0:T(8,128)S(1)} %get-tuple-element.12.refs_3_), channel_id=1, source_target_pairs={{0,16},{8,24},{16,0},{24,8},{1,17},{9,25},{17,1},{25,9},{2,18},{10... | collective-permute-start | bytes 49160 | tf_op jit(solution)/shard_map/ppermute | solution.py:302
  30.8 1.3 %collective-permute-start.13 = (f32[32,512]{1,0:T(8,128)S(1)}, f32[32,512]{1,0:T(8,128)S(1)}, u32[]{:S(2)}, u32[]{:S(2)}) collective-permute-start(f32[32,512]{1,0:T(8,128)S(1)} %get-tuple-element.17), channel_id=1, source_target_pairs={{0,1},{1,0},{2,3},{3,2},{4,5},{5,4},{6,7},{7,6},{8,9},{9,8},{10,11... | collective-permute-start | bytes 196616 | tf_op jit(solution)/shard_map/ppermute | solution.py:297

commit v4 on v3

--- a/solution.py
+++ b/solution.py
@@ -103,7 +103,6 @@
     per = LANES // depth
     groups = bands // per
     rows = depth + 2 * HALO
-    slab = info[1]
     for g in range(groups):
         for tile in range(tiles):
             part = slice(tile * depth, (tile + 1) * depth)
@@ -114,7 +113,7 @@
     step = lax.broadcasted_iota(jnp.int32, (8, LANES), 0).astype(jnp.float32)
     place = lax.broadcasted_iota(jnp.int32, (rows, LANES), 0)
     wide_lane = lax.broadcasted_iota(jnp.int32, (rows, LANES), 1)
-    keep = inside((rows, LANES), depth, slab, slabs)
+    keep = info[...] > 0.0
     together = images.shape[0]
 
     def gather(i, g, inverse, stride, start):
@@ -257,14 +256,14 @@
 def residual_kernel(half, depth, width, slabs, *refs):
     info, entries, proj, sums, from_below, from_above = refs[:6]
     others, measured = refs[6 : 6 + slabs - 3], refs[6 + slabs - 3 : 6 + slabs - 3 + half]
-    residual, held, other, stack, turned, images = refs[6 + slabs - 3 + half :]
+    residual, held, other, stack, turned, images, result, sem = refs[6 + slabs - 3 + half :]
     rows = depth + 2 * HALO
     tiles = width // LANES
     edge = (8 + HALO) * half
     column = sums[...] + from_below[edge:, :] + from_above[edge:, :]
     for ref in others:
         column += ref[...]
-    keep = inside((rows, LANES), depth, info[1], slabs)
+    keep = info[...] > 0.0
     for j in range(half):
         at = 8 * half + HALO * j
         for tile in range(tiles):
@@ -283,9 +282,13 @@
             gain = column[half + j : half + j + 1, part] / column[j : j + 1, part]
             value = jnp.where(keep, (wanted - gain * image) * (1.0 / (2 * half)), 0.0)
             if j == 0:
-                residual[:, part] = value[HALO : HALO + depth, :]
+                result[:, part] = value[HALO : HALO + depth, :]
             held[j, tile] = value
+        if j == 0:
+            copy = pltpu.make_async_copy(result, residual, sem)
+            copy.start()
     project_back(half, depth, width, 1, entries, held, other, stack, turned, images)
+    copy.wait()
 
 
 def own_kernel(half, depth, width, entries, held, out, stack, turned, images):
@@ -309,24 +312,23 @@
     rows = depth + 2 * HALO
     tiles = width // LANES
     f32, bf16 = jnp.float32, jnp.bfloat16
-    info = jnp.stack([lax.axis_index("xband"), lax.axis_index("zslab")]).astype(jnp.int32)
-
-    smem = pl.BlockSpec(memory_space=pltpu.SMEM)
+    place = jnp.full((1, 1), lax.axis_index("xband"), jnp.int32)
+    info = jnp.where(inside((rows, LANES), depth, lax.axis_index("zslab"), slabs), 1.0, 0.0).astype(f32)
+
     vmem = pl.BlockSpec(memory_space=pltpu.VMEM)
     params = pltpu.CompilerParams(vmem_limit_bytes=VMEM_LIMIT)
 
-    def on_core(body, shapes, operands, scratch=(), spaces={}):
+    def on_core(body, shapes, operands, scratch=(), spaces={}, out_spaces={}):
         out = pl.pallas_call(
             body,
             out_shape=[jax.ShapeDtypeStruct(shape, f32) for shape in shapes],
-            in_specs=[spaces.get(i, smem if x is info else vmem) for i, x in enumerate(operands)],
-            out_specs=[vmem] * len(shapes),
+            in_specs=[spaces.get(i, vmem) for i in range(len(operands))],
+            out_specs=[out_spaces.get(i, vmem) for i in range(len(shapes))],
             scratch_shapes=scratch,
             compiler_params=params,
         )(*operands)
         return out if len(shapes) > 1 else out[0]
 
-    place = jnp.full((1, 1), lax.axis_index("xband"), jnp.int32)
     packed = on_core(
         functools.partial(pack_kernel, depth, width),
         [(tiles * depth + 8, LANES)],
@@ -384,7 +386,8 @@
         functools.partial(residual_kernel, half, depth, width, slabs),
         [(depth, width), (half, tiles, rows, LANES), (depth, width)],
         [info, theirs[0], proj, sums, below, above] + others + views,
-        scratch,
+        scratch + [pltpu.VMEM((depth, width), f32), pltpu.SemaphoreType.DMA],
+        out_spaces={0: pl.BlockSpec(memory_space=pl.ANY)},
     )
     from_other = swapped(other, 1)
     own = on_core(

time: 33 us -> 31.2 us (0.945)
  Pallas kernels: 9.4 us -> 7.34 us
    pallas_call x6, Pallas kernels: 9.4 us -> 7.34 us  [on_core(): pl.pallas_call(body, out_shape=[jax.ShapeDtypeStruct(shape, f32) for shap...]
    ppermute x11, waiting for transfers between devices: 1.89 us -> 2.57 us  [swapped(): return lax.ppermute(x, 'xband', [(i, i ^ by) for i in range(n)])]
    ppermute x3, waiting for transfers between devices: 4.08 us -> 3.67 us  [from_slab(): return lax.ppermute(x, 'zslab', [(i, (i + by) % n) for i in range(n)])]
  transfers between devices with their start and end apart: 14 -> 14, of which waited for: 4 -> 5; matrix products, arithmetic and copies ran while one was open for 0% -> 0% of each run, Pallas kernels for 19% -> 16%
where the time goes in v4:
time: 31.2 us; the launch traced here: 31 us
  starting transfers between devices  16 us (51%)
  Pallas kernels  7.34 us (24%)
  waiting for transfers between devices  6.24 us (20%)
  between operations  0.73 us (2%)
  other arithmetic  0.65 us (2%)
    ppermute x11, starting transfers between devices, swapped(): return lax.ppermute(x, 'xband', [(i, i ^ by) for i in range(n)])  11.5 us
    pallas_call x6, Pallas kernels, on_core(): pl.pallas_call(body, out_shape=[jax.ShapeDtypeStruct(shape, f32) for shap...  7.34 us
    ppermute x3, starting transfers between devices, from_slab(): return lax.ppermute(x, 'zslab', [(i, (i + by) % n) for i in range(n)])  4.49 us
    ppermute x3, waiting for transfers between devices, from_slab(): return lax.ppermute(x, 'zslab', [(i, (i + by) % n) for i in range(n)])  3.67 us
    ppermute x11, waiting for transfers between devices, swapped(): return lax.ppermute(x, 'xband', [(i, i ^ by) for i in range(n)])  2.57 us
    broadcast_in_dim x1, other arithmetic, shards(): return (residual[None], (own + from_other)[None])  0.64 us
  transfers between devices with their start and end apart: 14, of which 5 were waited for; matrix products, arithmetic and copies ran while one was open for 0% of the time, Pallas kernels for 16%

profile of v4, /device:TPU:0, one launch (start us, length us, event | category | flops | bytes accessed | tf_op | source)
XLA Modules:
  0.0 31.0 jit_solution(16005769234602141501)
XLA Ops:
  0.6 0.9 %shard_map.68.refs_1_.entries = f32[136,128]{1,0:T(8,128)S(1)} custom-call(f32[32,512]{1,0:T(8,128)} %bitcast.14, f32[1,8]{1,0:T(1,128)} %bitcast.15, s32[1,8]{1,0:T(1,128)} %bitcast.16, s32[1,8]{1,0:T(1,128)} %bitcast.17, s32[1,1]{1,0:T(1,128)} %bitcast.5.refs_3_), custom_call_target="tpu_custom_call" | custom-call | tf_op jit(solution)/shard_map/pallas_call | solution.py:322
  1.6 5.1 %collective-permute-start.5 = (f32[136,128]{1,0:T(8,128)S(1)}, f32[136,128]{1,0:T(8,128)S(1)}, u32[]{:S(2)}, u32[]{:S(2)}) collective-permute-start(f32[136,128]{1,0:T(8,128)S(1)} %shard_map.68.refs_1_.entries), channel_id=1, source_target_pairs={{0,6},{1,7},{2,4},{3,5},{4,2},{5,3},{6,0},{7,1},{8,14},{9,15},{10,... | collective-permute-start | bytes 208904 | tf_op jit(solution)/shard_map/ppermute | solution.py:300
  6.7 0.0 collective-permute-start
  6.7 0.0 collective-permute-start.3
  6.7 0.7 %collective-permute-start.1 = (f32[136,128]{1,0:T(8,128)S(1)}, f32[136,128]{1,0:T(8,128)S(1)}, u32[]{:S(2)}, u32[]{:S(2)}) collective-permute-start(f32[136,128]{1,0:T(8,128)S(1)} %shard_map.68.refs_1_.entries), channel_id=1, source_target_pairs={{0,2},{1,3},{2,0},{3,1},{4,6},{5,7},{6,4},{7,5},{8,10},{9,11},{10,... | collective-permute-start | bytes 208904 | tf_op jit(solution)/shard_map/ppermute | solution.py:300
  7.4 1.9 %collective-permute-done.5.refs_4_ = f32[136,128]{1,0:T(8,128)S(1)} collective-permute-done((f32[136,128]{1,0:T(8,128)S(1)}, f32[136,128]{1,0:T(8,128)S(1)}, u32[]{:S(2)}, u32[]{:S(2)}) %collective-permute-start.5) | collective-permute-done | bytes 69664 | tf_op jit(solution)/shard_map/ppermute | solution.py:300
  9.3 0.0 collective-permute-start.6
  9.3 0.0 collective-permute-done.refs_1_
  9.3 4.4 %collective-permute-start.9 = (f32[32,512]{1,0:T(8,128)S(1)}, f32[32,512]{1,0:T(8,128)S(1)}, u32[]{:S(2)}, u32[]{:S(2)}) collective-permute-start(f32[32,512]{1,0:T(8,128)S(1)} %bitcast.9), channel_id=1, source_target_pairs={{0,6},{1,7},{2,4},{3,5},{4,2},{5,3},{6,0},{7,1},{8,14},{9,15},{10,... | collective-permute-start | bytes 196616 | tf_op jit(solution)/shard_map/ppermute | solution.py:300
  13.7 0.0 collective-permute-done.3.refs_3_
  13.7 0.6 %collective-permute-start.7 = (f32[32,512]{1,0:T(8,128)S(1)}, f32[32,512]{1,0:T(8,128)S(1)}, u32[]{:S(2)}, u32[]{:S(2)}) collective-permute-start(f32[32,512]{1,0:T(8,128)S(1)} %bitcast.11), channel_id=1, source_target_pairs={{0,2},{1,3},{2,0},{3,1},{4,6},{5,7},{6,4},{7,5},{8,10},{9,11},{10,... | collective-permute-start | bytes 196616 | tf_op jit(solution)/shard_map/ppermute | solution.py:300
  14.4 0.0 collective-permute-done.6.refs_4_
  14.4 0.5 %collective-permute-start.2 = (f32[136,128]{1,0:T(8,128)S(1)}, f32[136,128]{1,0:T(8,128)S(1)}, u32[]{:S(2)}, u32[]{:S(2)}) collective-permute-start(f32[136,128]{1,0:T(8,128)S(1)} %collective-permute-done.1.refs_2_), channel_id=1, source_target_pairs={{0,1},{1,0},{2,3},{3,2},{4,5},{5,4},{6,7},{7,6},{8,9},{9,8},{10,11... | collective-permute-start | bytes 208904 | tf_op jit(solution)/shard_map/ppermute | solution.py:300
  14.9 0.1 iota.10.refs_0_
  15.0 1.8 %shard_map.69.refs_5_ = f32[4,40,512]{2,1,0:T(8,128)S(1)} custom-call(f32[40,128]{1,0:T(8,128)S(1)} %iota.10.refs_0_, f32[136,128]{1,0:T(8,128)S(1)} %shard_map.68.refs_1_.entries, f32[136,128]{1,0:T(8,128)S(1)} %collective-permute-done.1.refs_2_, f32[136,128]{1,0:T(8,128)S(1)} %collective-permute-done.3.refs_3_, f32[136,128]{1,0:T(8,128)S(1)} %collective-permute-done.5.refs_4_), custom_call_target="tpu_custom_call" | custom-call | tf_op jit(solution)/shard_map/pallas_call | solution.py:322
  16.8 0.0 collective-permute-done.4.refs_3_
  16.8 0.0 collective-permute-done.2.refs_2_
  16.8 1.9 %shard_map.70.refs_0_.refs_2_ = f32[4,40,512]{2,1,0:T(8,128)S(1)} custom-call(f32[40,128]{1,0:T(8,128)S(1)} %iota.10.refs_0_, f32[136,128]{1,0:T(8,128)S(1)} %collective-permute-done.refs_1_, f32[136,128]{1,0:T(8,128)S(1)} %collective-permute-done.2.refs_2_, f32[136,128]{1,0:T(8,128)S(1)} %collective-permute-done.4.refs_3_, ...), custom_call_target="tpu_custom_call" | custom-call | tf_op jit(solution)/shard_map/pallas_call | solution.py:322
  18.7 0.6 %collective-permute-done.8.refs_3_.refs_9_ = f32[32,512]{1,0:T(8,128)S(1)} collective-permute-done((f32[32,512]{1,0:T(8,128)S(1)}, f32[32,512]{1,0:T(8,128)S(1)}, u32[]{:S(2)}, u32[]{:S(2)}) %collective-permute-start.8) | collective-permute-done | bytes 65568 | tf_op jit(solution)/shard_map/ppermute | solution.py:300
  19.3 0.1 collective-permute-done.7.refs_2_.refs_8_
  19.4 0.1 shard_map.71
  19.5 1.5 %collective-permute-start.10 = (f32[56,512]{1,0:T(8,128)S(1)}, f32[56,512]{1,0:T(8,128)S(1)}, u32[]{:S(2)}, u32[]{:S(2)}) collective-permute-start(f32[56,512]{1,0:T(8,128)S(1)} %get-tuple-element.13), channel_id=1, source_target_pairs={{0,8},{8,16},{16,24},{24,0},{1,9},{9,17},{17,25},{25,1},{2,10},{10... | collective-permute-start | bytes 344072 | tf_op jit(solution)/shard_map/ppermute | solution.py:305
  21.0 1.4 %collective-permute-start.11 = (f32[56,512]{1,0:T(8,128)S(1)}, f32[56,512]{1,0:T(8,128)S(1)}, u32[]{:S(2)}, u32[]{:S(2)}) collective-permute-start(f32[56,512]{1,0:T(8,128)S(1)} %get-tuple-element.14), channel_id=1, source_target_pairs={{0,24},{8,0},{16,8},{24,16},{1,25},{9,1},{17,9},{25,17},{2,26},{10... | collective-permute-start | bytes 344072 | tf_op jit(solution)/shard_map/ppermute | solution.py:305
  22.5 1.5 %collective-permute-start.12 = (f32[8,512]{1,0:T(8,128)S(1)}, f32[8,512]{1,0:T(8,128)S(1)}, u32[]{:S(2)}, u32[]{:S(2)}) collective-permute-start(f32[8,512]{1,0:T(8,128)S(1)} %get-tuple-element.12.refs_3_), channel_id=1, source_target_pairs={{0,16},{8,24},{16,0},{24,8},{1,17},{9,25},{17,1},{25,9},{2,18},{10... | collective-permute-start | bytes 49160 | tf_op jit(solution)/shard_map/ppermute | solution.py:305
  24.0 2.4 %collective-permute-done.12.refs_6_ = f32[8,512]{1,0:T(8,128)S(1)} collective-permute-done((f32[8,512]{1,0:T(8,128)S(1)}, f32[8,512]{1,0:T(8,128)S(1)}, u32[]{:S(2)}, u32[]{:S(2)}) %collective-permute-start.12) | collective-permute-done | bytes 16416 | tf_op jit(solution)/shard_map/ppermute | solution.py:305
  26.4 0.0 collective-permute-done.10.refs_4_
  26.4 1.2 %collective-permute-done.11.refs_5_ = f32[56,512]{1,0:T(8,128)S(1)} collective-permute-done((f32[56,512]{1,0:T(8,128)S(1)}, f32[56,512]{1,0:T(8,128)S(1)}, u32[]{:S(2)}, u32[]{:S(2)}) %collective-permute-start.11) | collective-permute-done | bytes 114720 | tf_op jit(solution)/shard_map/ppermute | solution.py:305
  27.6 1.3 %shard_map.72 = (f32[32,512]{1,0:T(8,128)}, f32[4,4,40,128]{3,2,1,0:T(8,128)S(1)}, f32[32,512]{1,0:T(8,128)S(1)}) custom-call(f32[40,128]{1,0:T(8,128)S(1)} %iota.10.refs_0_, f32[136,128]{1,0:T(8,128)S(1)} %collective-permute-done.refs_1_, f32[4,40,512]{2,1,0:T(8,128)S(1)} %shard_map.70.refs_0_.refs_2_, f32[8,512]{1,0:T(8,128)S(1)} %get-tuple-element.12.refs_3_, ...), custom_call_target="tpu_custom_call" | custom-call | tf_op jit(solution)/shard_map/pallas_call | solution.py:322
  29.0 0.1 collective-permute-start.13
  29.1 1.3 %shard_map.73 = f32[32,512]{1,0:T(8,128)S(1)} custom-call(f32[136,128]{1,0:T(8,128)S(1)} %shard_map.68.refs_1_.entries, f32[4,4,40,128]{3,2,1,0:T(8,128)S(1)} %get-tuple-element.16.held), custom_call_target="tpu_custom_call" | custom-call | tf_op jit(solution)/shard_map/pallas_call | solution.py:322
  30.4 0.0 collective-permute-done.13
  30.4 0.6 %add_bitcast_fusion = f32[1,32,512]{2,1,0:T(8,128)} fusion(f32[32,512]{1,0:T(8,128)S(1)} %shard_map.73, f32[32,512]{1,0:T(8,128)S(1)} %collective-permute-done.13), kind=kLoop, calls=%fused_computation | loop fusion | flops 16384 | bytes 196608 | tf_op jit(solution)/shard_map/broadcast_in_dim | solution.py:396
  (7 shorter events, 0.0 us)
Async XLA Ops:
  0.6 8.6 %copy-start = (f32[1,32,512]{2,1,0:T(8,128)S(1)}, f32[1,32,512]{2,1,0:T(8,128)}, u32[]{:S(2)}) copy-start(f32[1,32,512]{2,1,0:T(8,128)} %param.6) | copy-start | bytes 196612
  1.6 7.7 %collective-permute-start.5 = (f32[136,128]{1,0:T(8,128)S(1)}, f32[136,128]{1,0:T(8,128)S(1)}, u32[]{:S(2)}, u32[]{:S(2)}) collective-permute-start(f32[136,128]{1,0:T(8,128)S(1)} %shard_map.68.refs_1_.entries), channel_id=1, source_target_pairs={{0,6},{1,7},{2,4},{3,5},{4,2},{5,3},{6,0},{7,1},{8,14},{9,15},{10,... | collective-permute-start | bytes 208904 | tf_op jit(solution)/shard_map/ppermute | solution.py:300
  6.7 2.6 %collective-permute-start = (f32[136,128]{1,0:T(8,128)S(1)}, f32[136,128]{1,0:T(8,128)S(1)}, u32[]{:S(2)}, u32[]{:S(2)}) collective-permute-start(f32[136,128]{1,0:T(8,128)S(1)} %shard_map.68.refs_1_.entries), channel_id=1, source_target_pairs={{0,1},{1,0},{2,3},{3,2},{4,5},{5,4},{6,7},{7,6},{8,9},{9,8},{10,11... | collective-permute-start | bytes 208904 | tf_op jit(solution)/shard_map/ppermute | solution.py:300
  6.7 7.0 %collective-permute-start.3 = (f32[136,128]{1,0:T(8,128)S(1)}, f32[136,128]{1,0:T(8,128)S(1)}, u32[]{:S(2)}, u32[]{:S(2)}) collective-permute-start(f32[136,128]{1,0:T(8,128)S(1)} %shard_map.68.refs_1_.entries), channel_id=1, source_target_pairs={{0,4},{1,5},{2,6},{3,7},{4,0},{5,1},{6,2},{7,3},{8,12},{9,13},{10,... | collective-permute-start | bytes 208904 | tf_op jit(solution)/shard_map/ppermute | solution.py:300
  6.7 7.7 %collective-permute-start.1 = (f32[136,128]{1,0:T(8,128)S(1)}, f32[136,128]{1,0:T(8,128)S(1)}, u32[]{:S(2)}, u32[]{:S(2)}) collective-permute-start(f32[136,128]{1,0:T(8,128)S(1)} %shard_map.68.refs_1_.entries), channel_id=1, source_target_pairs={{0,2},{1,3},{2,0},{3,1},{4,6},{5,7},{6,4},{7,5},{8,10},{9,11},{10,... | collective-permute-start | bytes 208904 | tf_op jit(solution)/shard_map/ppermute | solution.py:300
  9.3 5.1 %collective-permute-start.6 = (f32[136,128]{1,0:T(8,128)S(1)}, f32[136,128]{1,0:T(8,128)S(1)}, u32[]{:S(2)}, u32[]{:S(2)}) collective-permute-start(f32[136,128]{1,0:T(8,128)S(1)} %collective-permute-done.5.refs_4_), channel_id=1, source_target_pairs={{0,1},{1,0},{2,3},{3,2},{4,5},{5,4},{6,7},{7,6},{8,9},{9,8},{10,11... | collective-permute-start | bytes 208904 | tf_op jit(solution)/shard_map/ppermute | solution.py:300
  9.3 9.4 %collective-permute-start.9 = (f32[32,512]{1,0:T(8,128)S(1)}, f32[32,512]{1,0:T(8,128)S(1)}, u32[]{:S(2)}, u32[]{:S(2)}) collective-permute-start(f32[32,512]{1,0:T(8,128)S(1)} %bitcast.9), channel_id=1, source_target_pairs={{0,6},{1,7},{2,4},{3,5},{4,2},{5,3},{6,0},{7,1},{8,14},{9,15},{10,... | collective-permute-start | bytes 196616 | tf_op jit(solution)/shard_map/ppermute | solution.py:300
  13.7 5.6 %collective-permute-start.8 = (f32[32,512]{1,0:T(8,128)S(1)}, f32[32,512]{1,0:T(8,128)S(1)}, u32[]{:S(2)}, u32[]{:S(2)}) collective-permute-start(f32[32,512]{1,0:T(8,128)S(1)} %bitcast.10), channel_id=1, source_target_pairs={{0,4},{1,5},{2,6},{3,7},{4,0},{5,1},{6,2},{7,3},{8,12},{9,13},{10,... | collective-permute-start | bytes 196616 | tf_op jit(solution)/shard_map/ppermute | solution.py:300
  13.7 5.7 %collective-permute-start.7 = (f32[32,512]{1,0:T(8,128)S(1)}, f32[32,512]{1,0:T(8,128)S(1)}, u32[]{:S(2)}, u32[]{:S(2)}) collective-permute-start(f32[32,512]{1,0:T(8,128)S(1)} %bitcast.11), channel_id=1, source_target_pairs={{0,2},{1,3},{2,0},{3,1},{4,6},{5,7},{6,4},{7,5},{8,10},{9,11},{10,... | collective-permute-start | bytes 196616 | tf_op jit(solution)/shard_map/ppermute | solution.py:300
  14.4 2.4 %collective-permute-start.4 = (f32[136,128]{1,0:T(8,128)S(1)}, f32[136,128]{1,0:T(8,128)S(1)}, u32[]{:S(2)}, u32[]{:S(2)}) collective-permute-start(f32[136,128]{1,0:T(8,128)S(1)} %collective-permute-done.3.refs_3_), channel_id=1, source_target_pairs={{0,1},{1,0},{2,3},{3,2},{4,5},{5,4},{6,7},{7,6},{8,9},{9,8},{10,11... | collective-permute-start | bytes 208904 | tf_op jit(solution)/shard_map/ppermute | solution.py:300
  14.4 2.4 %collective-permute-start.2 = (f32[136,128]{1,0:T(8,128)S(1)}, f32[136,128]{1,0:T(8,128)S(1)}, u32[]{:S(2)}, u32[]{:S(2)}) collective-permute-start(f32[136,128]{1,0:T(8,128)S(1)} %collective-permute-done.1.refs_2_), channel_id=1, source_target_pairs={{0,1},{1,0},{2,3},{3,2},{4,5},{5,4},{6,7},{7,6},{8,9},{9,8},{10,11... | collective-permute-start | bytes 208904 | tf_op jit(solution)/shard_map/ppermute | solution.py:300
  19.5 6.9 %collective-permute-start.10 = (f32[56,512]{1,0:T(8,128)S(1)}, f32[56,512]{1,0:T(8,128)S(1)}, u32[]{:S(2)}, u32[]{:S(2)}) collective-permute-start(f32[56,512]{1,0:T(8,128)S(1)} %get-tuple-element.13), channel_id=1, source_target_pairs={{0,8},{8,16},{16,24},{24,0},{1,9},{9,17},{17,25},{25,1},{2,10},{10... | collective-permute-start | bytes 344072 | tf_op jit(solution)/shard_map/ppermute | solution.py:305
  21.0 6.6 %collective-permute-start.11 = (f32[56,512]{1,0:T(8,128)S(1)}, f32[56,512]{1,0:T(8,128)S(1)}, u32[]{:S(2)}, u32[]{:S(2)}) collective-permute-start(f32[56,512]{1,0:T(8,128)S(1)} %get-tuple-element.14), channel_id=1, source_target_pairs={{0,24},{8,0},{16,8},{24,16},{1,25},{9,1},{17,9},{25,17},{2,26},{10... | collective-permute-start | bytes 344072 | tf_op jit(solution)/shard_map/ppermute | solution.py:305
  22.5 3.9 %collective-permute-start.12 = (f32[8,512]{1,0:T(8,128)S(1)}, f32[8,512]{1,0:T(8,128)S(1)}, u32[]{:S(2)}, u32[]{:S(2)}) collective-permute-start(f32[8,512]{1,0:T(8,128)S(1)} %get-tuple-element.12.refs_3_), channel_id=1, source_target_pairs={{0,16},{8,24},{16,0},{24,8},{1,17},{9,25},{17,1},{25,9},{2,18},{10... | collective-permute-start | bytes 49160 | tf_op jit(solution)/shard_map/ppermute | solution.py:305
  29.0 1.4 %collective-permute-start.13 = (f32[32,512]{1,0:T(8,128)S(1)}, f32[32,512]{1,0:T(8,128)S(1)}, u32[]{:S(2)}, u32[]{:S(2)}) collective-permute-start(f32[32,512]{1,0:T(8,128)S(1)} %get-tuple-element.17), channel_id=1, source_target_pairs={{0,1},{1,0},{2,3},{3,2},{4,5},{5,4},{6,7},{7,6},{8,9},{9,8},{10,11... | collective-permute-start | bytes 196616 | tf_op jit(solution)/shard_map/ppermute | solution.py:300

commit v5 on v4

--- a/solution.py
+++ b/solution.py
@@ -10,12 +10,16 @@
 
 HALO = 4
 LANES = 128
-PAD = 24
+SHIFT_MOST = 32
 Y_BITS = 21
 U_BITS = 20
 INVERSE, SHIFT, Y_STRIDE, Y_MIDDLE, U_STRIDE, U_MIDDLE, MAGNIFICATION = range(7)
 VMEM_LIMIT = 48 * 1024 * 1024
 NT = (((1,), (1,)), ((), ()))
+
+
+def padding(width):
+    return width // 2 + 2 * SHIFT_MOST + 8
 
 
 def rows_at(tile, index):
@@ -194,8 +198,9 @@
     wide_lane = lax.broadcasted_iota(jnp.int32, (depth, LANES), 1)
     select = jnp.where(place == (wide_lane & (depth - 1)), 1.0, 0.0).astype(jnp.bfloat16)
     select = jnp.concatenate([select, select], axis=1)
-    turned[:PAD, :] = jnp.zeros((PAD, LANES), jnp.float32)
-    turned[PAD + width :, :] = jnp.zeros((PAD, LANES), jnp.float32)
+    pad = padding(width)
+    turned[:pad, :] = jnp.zeros((pad, LANES), jnp.float32)
+    turned[pad + width :, :] = jnp.zeros((pad, LANES), jnp.float32)
     table = entries[tiles * depth :, :]
     numbers = table.astype(jnp.int32)
     ahead = pltpu.roll(numbers, U_MIDDLE - U_STRIDE, 0)
@@ -212,30 +217,36 @@
         for tile in range(tiles):
             for q in range(per):
                 stack[tile, q * depth : (q + 1) * depth, :] = held[g * per + q, tile, pl.ds(shift[q], depth), :]
-            turned[PAD + tile * LANES : PAD + (tile + 1) * LANES, :] = stack[tile].T
+            turned[pad + tile * LANES : pad + (tile + 1) * LANES, :] = stack[tile].T
         inverse_l = by_lane(lane, depth, value(table, INVERSE, g))
+        beside_l, beyond_l = 1.0 - inverse_l, 1.0 - 2.0 * inverse_l
         fine = step * by_lane(lane, depth, value(table, MAGNIFICATION, g))
         stride_l = by_lane(lane, depth, stride)
         start_l = by_lane(lane, depth, start)
 
         def eight(point, point_l):
-            base = [jnp.clip((p >> U_BITS) - 1, -PAD, width) + PAD for p in point]
-            windows = [turned[pl.ds(base[0] + 8 * r, 8), :] for r in range(3)]
+            base = [p >> U_BITS for p in point]
+            starts = (pad - 1, pad + 7, pad + 1, pad + 9)
+            windows = [turned[pl.ds(base[0] + r, 8), :] for r in starts]
             for q in range(1, per):
                 here = lane >= q * depth
-                windows = [jnp.where(here, turned[pl.ds(base[q] + 8 * r, 8), :], windows[r]) for r in range(3)]
+                windows = [jnp.where(here, turned[pl.ds(base[q] + r, 8), :], w) for r, w in zip(starts, windows)]
             target = (point_l & (2**U_BITS - 1)).astype(jnp.float32) * 2.0**-U_BITS + fine
             lower = target.astype(jnp.int32)
             frac = (target - lower.astype(jnp.float32)) * inverse_l
-            out = jnp.zeros((8, LANES), jnp.float32)
-            for tap in range(4):
-                index = lower + tap
+            weights = [
+                jnp.maximum(0.0, beside_l - frac),
+                1.0 - frac,
+                beside_l + frac,
+                jnp.maximum(0.0, beyond_l + frac),
+            ]
+            out = None
+            for tap, weight in enumerate(weights):
+                index = lower + tap % 2
                 within = index & 7
-                value = jnp.where(index < 8, rows_at(windows[0], within), rows_at(windows[1], within))
-                if tap >= 2:
-                    value = jnp.where(index < 16, value, rows_at(windows[2], within))
-                weight = jnp.maximum(0.0, 1.0 - jnp.abs(frac + (1.0 - tap) * inverse_l))
-                out += weight * value
+                pair = windows[tap // 2 * 2 : tap // 2 * 2 + 2]
+                value = jnp.where(index < 8, rows_at(pair[0], within), rows_at(pair[1], within))
+                out = weight * value if out is None else out + weight * value
             return out
 
         def sixteen(i, carry):
@@ -248,7 +259,7 @@
             images[at, :LANES], images[at, LANES:] = two_parts(pair)
             return point, point_l
 
-        lax.fori_loop(0, width // 16, sixteen, (start, start_l), unroll=4)
+        lax.fori_loop(0, width // 16, sixteen, (start, start_l), unroll=8)
         total += lax.dot_general(select, images[...], NT, preferred_element_type=jnp.float32)
     out[...] = total * (1.0 / math.sqrt(2 * half))
 
@@ -379,7 +390,7 @@
 
     scratch = [
         pltpu.VMEM((tiles, LANES, LANES), f32),
-        pltpu.VMEM((width + 2 * PAD, LANES), f32),
+        pltpu.VMEM((width + 2 * padding(width), LANES), f32),
         pltpu.VMEM((width, 2 * LANES), bf16),
     ]
     residual, held, other = on_core(

time: 31.2 us -> 30.8 us (0.987)
  Pallas kernels: 7.34 us -> 6.81 us
    pallas_call x6, Pallas kernels: 7.34 us -> 6.81 us  [on_core(): pl.pallas_call(body, out_shape=[jax.ShapeDtypeStruct(shape, f32) for shap...]
  transfers between devices with their start and end apart: 14 -> 14, of which waited for: 5 -> 6; matrix products, arithmetic and copies ran while one was open for 0% -> 0% of each run, Pallas kernels for 16% -> 15%
where the time goes in v5:
time: 30.8 us; the launch traced here: 30.7 us
  starting transfers between devices  16 us (52%)
  Pallas kernels  6.81 us (22%)
  waiting for transfers between devices  6.43 us (21%)
  between operations  0.72 us (2%)
  other arithmetic  0.65 us (2%)
    ppermute x11, starting transfers between devices, swapped(): return lax.ppermute(x, 'xband', [(i, i ^ by) for i in range(n)])  11.5 us
    pallas_call x6, Pallas kernels, on_core(): pl.pallas_call(body, out_shape=[jax.ShapeDtypeStruct(shape, f32) for shap...  6.81 us
    ppermute x3, starting transfers between devices, from_slab(): return lax.ppermute(x, 'zslab', [(i, (i + by) % n) for i in range(n)])  4.49 us
    ppermute x3, waiting for transfers between devices, from_slab(): return lax.ppermute(x, 'zslab', [(i, (i + by) % n) for i in range(n)])  3.67 us
    ppermute x11, waiting for transfers between devices, swapped(): return lax.ppermute(x, 'xband', [(i, i ^ by) for i in range(n)])  2.76 us
    broadcast_in_dim x1, other arithmetic, shards(): return (residual[None], (own + from_other)[None])  0.64 us
  transfers between devices with their start and end apart: 14, of which 6 were waited for; matrix products, arithmetic and copies ran while one was open for 0% of the time, Pallas kernels for 15%

profile of v5, /device:TPU:0, one launch (start us, length us, event | category | flops | bytes accessed | tf_op | source)
XLA Modules:
  0.0 30.7 jit_solution(964376361114934018)
XLA Ops:
  0.6 0.9 %shard_map.68.refs_1_.entries = f32[136,128]{1,0:T(8,128)S(1)} custom-call(f32[32,512]{1,0:T(8,128)} %bitcast.14, f32[1,8]{1,0:T(1,128)} %bitcast.15, s32[1,8]{1,0:T(1,128)} %bitcast.16, s32[1,8]{1,0:T(1,128)} %bitcast.17, s32[1,1]{1,0:T(1,128)} %bitcast.5.refs_3_), custom_call_target="tpu_custom_call" | custom-call | tf_op jit(solution)/shard_map/pallas_call | solution.py:333
  1.6 5.1 %collective-permute-start.5 = (f32[136,128]{1,0:T(8,128)S(1)}, f32[136,128]{1,0:T(8,128)S(1)}, u32[]{:S(2)}, u32[]{:S(2)}) collective-permute-start(f32[136,128]{1,0:T(8,128)S(1)} %shard_map.68.refs_1_.entries), channel_id=1, source_target_pairs={{0,6},{1,7},{2,4},{3,5},{4,2},{5,3},{6,0},{7,1},{8,14},{9,15},{10,... | collective-permute-start | bytes 208904 | tf_op jit(solution)/shard_map/ppermute | solution.py:311
  6.7 0.0 collective-permute-start
  6.7 0.0 collective-permute-start.3
  6.7 0.7 %collective-permute-start.1 = (f32[136,128]{1,0:T(8,128)S(1)}, f32[136,128]{1,0:T(8,128)S(1)}, u32[]{:S(2)}, u32[]{:S(2)}) collective-permute-start(f32[136,128]{1,0:T(8,128)S(1)} %shard_map.68.refs_1_.entries), channel_id=1, source_target_pairs={{0,2},{1,3},{2,0},{3,1},{4,6},{5,7},{6,4},{7,5},{8,10},{9,11},{10,... | collective-permute-start | bytes 208904 | tf_op jit(solution)/shard_map/ppermute | solution.py:311
  7.4 1.9 %collective-permute-done.5.refs_4_ = f32[136,128]{1,0:T(8,128)S(1)} collective-permute-done((f32[136,128]{1,0:T(8,128)S(1)}, f32[136,128]{1,0:T(8,128)S(1)}, u32[]{:S(2)}, u32[]{:S(2)}) %collective-permute-start.5) | collective-permute-done | bytes 69664 | tf_op jit(solution)/shard_map/ppermute | solution.py:311
  9.3 0.0 collective-permute-start.6
  9.3 0.0 collective-permute-done.refs_1_
  9.3 4.4 %collective-permute-start.9 = (f32[32,512]{1,0:T(8,128)S(1)}, f32[32,512]{1,0:T(8,128)S(1)}, u32[]{:S(2)}, u32[]{:S(2)}) collective-permute-start(f32[32,512]{1,0:T(8,128)S(1)} %bitcast.9), channel_id=1, source_target_pairs={{0,6},{1,7},{2,4},{3,5},{4,2},{5,3},{6,0},{7,1},{8,14},{9,15},{10,... | collective-permute-start | bytes 196616 | tf_op jit(solution)/shard_map/ppermute | solution.py:311
  13.7 0.6 %collective-permute-start.7 = (f32[32,512]{1,0:T(8,128)S(1)}, f32[32,512]{1,0:T(8,128)S(1)}, u32[]{:S(2)}, u32[]{:S(2)}) collective-permute-start(f32[32,512]{1,0:T(8,128)S(1)} %bitcast.11), channel_id=1, source_target_pairs={{0,2},{1,3},{2,0},{3,1},{4,6},{5,7},{6,4},{7,5},{8,10},{9,11},{10,... | collective-permute-start | bytes 196616 | tf_op jit(solution)/shard_map/ppermute | solution.py:311
  14.4 0.0 collective-permute-done.1.refs_2_
  14.4 0.5 %collective-permute-start.2 = (f32[136,128]{1,0:T(8,128)S(1)}, f32[136,128]{1,0:T(8,128)S(1)}, u32[]{:S(2)}, u32[]{:S(2)}) collective-permute-start(f32[136,128]{1,0:T(8,128)S(1)} %collective-permute-done.1.refs_2_), channel_id=1, source_target_pairs={{0,1},{1,0},{2,3},{3,2},{4,5},{5,4},{6,7},{7,6},{8,9},{9,8},{10,11... | collective-permute-start | bytes 208904 | tf_op jit(solution)/shard_map/ppermute | solution.py:311
  14.9 0.1 iota.10.refs_0_
  15.0 1.8 %shard_map.69.refs_5_ = f32[4,40,512]{2,1,0:T(8,128)S(1)} custom-call(f32[40,128]{1,0:T(8,128)S(1)} %iota.10.refs_0_, f32[136,128]{1,0:T(8,128)S(1)} %shard_map.68.refs_1_.entries, f32[136,128]{1,0:T(8,128)S(1)} %collective-permute-done.1.refs_2_, f32[136,128]{1,0:T(8,128)S(1)} %collective-permute-done.3.refs_3_, f32[136,128]{1,0:T(8,128)S(1)} %collective-permute-done.5.refs_4_), custom_call_target="tpu_custom_call" | custom-call | tf_op jit(solution)/shard_map/pallas_call | solution.py:333
  16.8 0.0 collective-permute-done.4.refs_3_
  16.8 0.0 collective-permute-done.2.refs_2_
  16.8 1.9 %shard_map.70.refs_0_.refs_2_ = f32[4,40,512]{2,1,0:T(8,128)S(1)} custom-call(f32[40,128]{1,0:T(8,128)S(1)} %iota.10.refs_0_, f32[136,128]{1,0:T(8,128)S(1)} %collective-permute-done.refs_1_, f32[136,128]{1,0:T(8,128)S(1)} %collective-permute-done.2.refs_2_, f32[136,128]{1,0:T(8,128)S(1)} %collective-permute-done.4.refs_3_, ...), custom_call_target="tpu_custom_call" | custom-call | tf_op jit(solution)/shard_map/pallas_call | solution.py:333
  18.7 0.0 collective-permute-done.9.refs_4_.refs_10_
  18.7 0.6 %collective-permute-done.8.refs_3_.refs_9_ = f32[32,512]{1,0:T(8,128)S(1)} collective-permute-done((f32[32,512]{1,0:T(8,128)S(1)}, f32[32,512]{1,0:T(8,128)S(1)}, u32[]{:S(2)}, u32[]{:S(2)}) %collective-permute-start.8) | collective-permute-done | bytes 65568 | tf_op jit(solution)/shard_map/ppermute | solution.py:311
  19.3 0.1 collective-permute-done.7.refs_2_.refs_8_
  19.4 0.1 shard_map.71
  19.5 1.5 %collective-permute-start.10 = (f32[56,512]{1,0:T(8,128)S(1)}, f32[56,512]{1,0:T(8,128)S(1)}, u32[]{:S(2)}, u32[]{:S(2)}) collective-permute-start(f32[56,512]{1,0:T(8,128)S(1)} %get-tuple-element.13), channel_id=1, source_target_pairs={{0,8},{8,16},{16,24},{24,0},{1,9},{9,17},{17,25},{25,1},{2,10},{10... | collective-permute-start | bytes 344072 | tf_op jit(solution)/shard_map/ppermute | solution.py:316
  21.0 1.4 %collective-permute-start.11 = (f32[56,512]{1,0:T(8,128)S(1)}, f32[56,512]{1,0:T(8,128)S(1)}, u32[]{:S(2)}, u32[]{:S(2)}) collective-permute-start(f32[56,512]{1,0:T(8,128)S(1)} %get-tuple-element.14), channel_id=1, source_target_pairs={{0,24},{8,0},{16,8},{24,16},{1,25},{9,1},{17,9},{25,17},{2,26},{10... | collective-permute-start | bytes 344072 | tf_op jit(solution)/shard_map/ppermute | solution.py:316
  22.5 1.5 %collective-permute-start.12 = (f32[8,512]{1,0:T(8,128)S(1)}, f32[8,512]{1,0:T(8,128)S(1)}, u32[]{:S(2)}, u32[]{:S(2)}) collective-permute-start(f32[8,512]{1,0:T(8,128)S(1)} %get-tuple-element.12.refs_3_), channel_id=1, source_target_pairs={{0,16},{8,24},{16,0},{24,8},{1,17},{9,25},{17,1},{25,9},{2,18},{10... | collective-permute-start | bytes 49160 | tf_op jit(solution)/shard_map/ppermute | solution.py:316
  24.0 2.4 %collective-permute-done.12.refs_6_ = f32[8,512]{1,0:T(8,128)S(1)} collective-permute-done((f32[8,512]{1,0:T(8,128)S(1)}, f32[8,512]{1,0:T(8,128)S(1)}, u32[]{:S(2)}, u32[]{:S(2)}) %collective-permute-start.12) | collective-permute-done | bytes 16416 | tf_op jit(solution)/shard_map/ppermute | solution.py:316
  26.4 0.0 collective-permute-done.10.refs_4_
  26.4 1.2 %collective-permute-done.11.refs_5_ = f32[56,512]{1,0:T(8,128)S(1)} collective-permute-done((f32[56,512]{1,0:T(8,128)S(1)}, f32[56,512]{1,0:T(8,128)S(1)}, u32[]{:S(2)}, u32[]{:S(2)}) %collective-permute-start.11) | collective-permute-done | bytes 114720 | tf_op jit(solution)/shard_map/ppermute | solution.py:316
  27.6 1.1 %shard_map.72 = (f32[32,512]{1,0:T(8,128)}, f32[4,4,40,128]{3,2,1,0:T(8,128)S(1)}, f32[32,512]{1,0:T(8,128)S(1)}) custom-call(f32[40,128]{1,0:T(8,128)S(1)} %iota.10.refs_0_, f32[136,128]{1,0:T(8,128)S(1)} %collective-permute-done.refs_1_, f32[4,40,512]{2,1,0:T(8,128)S(1)} %shard_map.70.refs_0_.refs_2_, f32[8,512]{1,0:T(8,128)S(1)} %get-tuple-element.12.refs_3_, ...), custom_call_target="tpu_custom_call" | custom-call | tf_op jit(solution)/shard_map/pallas_call | solution.py:333
  28.7 0.1 collective-permute-start.13
  28.8 1.0 %shard_map.73 = f32[32,512]{1,0:T(8,128)S(1)} custom-call(f32[136,128]{1,0:T(8,128)S(1)} %shard_map.68.refs_1_.entries, f32[4,4,40,128]{3,2,1,0:T(8,128)S(1)} %get-tuple-element.16.held), custom_call_target="tpu_custom_call" | custom-call | tf_op jit(solution)/shard_map/pallas_call | solution.py:333
  29.8 0.2 collective-permute-done.13
  30.0 0.6 %add_bitcast_fusion = f32[1,32,512]{2,1,0:T(8,128)} fusion(f32[32,512]{1,0:T(8,128)S(1)} %shard_map.73, f32[32,512]{1,0:T(8,128)S(1)} %collective-permute-done.13), kind=kLoop, calls=%fused_computation | loop fusion | flops 16384 | bytes 196608 | tf_op jit(solution)/shard_map/broadcast_in_dim | solution.py:407
  (7 shorter events, 0.0 us)
Async XLA Ops:
  0.6 8.6 %copy-start = (f32[1,32,512]{2,1,0:T(8,128)S(1)}, f32[1,32,512]{2,1,0:T(8,128)}, u32[]{:S(2)}) copy-start(f32[1,32,512]{2,1,0:T(8,128)} %param.6) | copy-start | bytes 196612
  1.6 7.7 %collective-permute-start.5 = (f32[136,128]{1,0:T(8,128)S(1)}, f32[136,128]{1,0:T(8,128)S(1)}, u32[]{:S(2)}, u32[]{:S(2)}) collective-permute-start(f32[136,128]{1,0:T(8,128)S(1)} %shard_map.68.refs_1_.entries), channel_id=1, source_target_pairs={{0,6},{1,7},{2,4},{3,5},{4,2},{5,3},{6,0},{7,1},{8,14},{9,15},{10,... | collective-permute-start | bytes 208904 | tf_op jit(solution)/shard_map/ppermute | solution.py:311
  6.7 2.6 %collective-permute-start = (f32[136,128]{1,0:T(8,128)S(1)}, f32[136,128]{1,0:T(8,128)S(1)}, u32[]{:S(2)}, u32[]{:S(2)}) collective-permute-start(f32[136,128]{1,0:T(8,128)S(1)} %shard_map.68.refs_1_.entries), channel_id=1, source_target_pairs={{0,1},{1,0},{2,3},{3,2},{4,5},{5,4},{6,7},{7,6},{8,9},{9,8},{10,11... | collective-permute-start | bytes 208904 | tf_op jit(solution)/shard_map/ppermute | solution.py:311
  6.7 7.0 %collective-permute-start.3 = (f32[136,128]{1,0:T(8,128)S(1)}, f32[136,128]{1,0:T(8,128)S(1)}, u32[]{:S(2)}, u32[]{:S(2)}) collective-permute-start(f32[136,128]{1,0:T(8,128)S(1)} %shard_map.68.refs_1_.entries), channel_id=1, source_target_pairs={{0,4},{1,5},{2,6},{3,7},{4,0},{5,1},{6,2},{7,3},{8,12},{9,13},{10,... | collective-permute-start | bytes 208904 | tf_op jit(solution)/shard_map/ppermute | solution.py:311
  6.7 7.7 %collective-permute-start.1 = (f32[136,128]{1,0:T(8,128)S(1)}, f32[136,128]{1,0:T(8,128)S(1)}, u32[]{:S(2)}, u32[]{:S(2)}) collective-permute-start(f32[136,128]{1,0:T(8,128)S(1)} %shard_map.68.refs_1_.entries), channel_id=1, source_target_pairs={{0,2},{1,3},{2,0},{3,1},{4,6},{5,7},{6,4},{7,5},{8,10},{9,11},{10,... | collective-permute-start | bytes 208904 | tf_op jit(solution)/shard_map/ppermute | solution.py:311
  9.3 5.1 %collective-permute-start.6 = (f32[136,128]{1,0:T(8,128)S(1)}, f32[136,128]{1,0:T(8,128)S(1)}, u32[]{:S(2)}, u32[]{:S(2)}) collective-permute-start(f32[136,128]{1,0:T(8,128)S(1)} %collective-permute-done.5.refs_4_), channel_id=1, source_target_pairs={{0,1},{1,0},{2,3},{3,2},{4,5},{5,4},{6,7},{7,6},{8,9},{9,8},{10,11... | collective-permute-start | bytes 208904 | tf_op jit(solution)/shard_map/ppermute | solution.py:311
  9.3 9.4 %collective-permute-start.9 = (f32[32,512]{1,0:T(8,128)S(1)}, f32[32,512]{1,0:T(8,128)S(1)}, u32[]{:S(2)}, u32[]{:S(2)}) collective-permute-start(f32[32,512]{1,0:T(8,128)S(1)} %bitcast.9), channel_id=1, source_target_pairs={{0,6},{1,7},{2,4},{3,5},{4,2},{5,3},{6,0},{7,1},{8,14},{9,15},{10,... | collective-permute-start | bytes 196616 | tf_op jit(solution)/shard_map/ppermute | solution.py:311
  13.7 5.6 %collective-permute-start.8 = (f32[32,512]{1,0:T(8,128)S(1)}, f32[32,512]{1,0:T(8,128)S(1)}, u32[]{:S(2)}, u32[]{:S(2)}) collective-permute-start(f32[32,512]{1,0:T(8,128)S(1)} %bitcast.10), channel_id=1, source_target_pairs={{0,4},{1,5},{2,6},{3,7},{4,0},{5,1},{6,2},{7,3},{8,12},{9,13},{10,... | collective-permute-start | bytes 196616 | tf_op jit(solution)/shard_map/ppermute | solution.py:311
  13.7 5.7 %collective-permute-start.7 = (f32[32,512]{1,0:T(8,128)S(1)}, f32[32,512]{1,0:T(8,128)S(1)}, u32[]{:S(2)}, u32[]{:S(2)}) collective-permute-start(f32[32,512]{1,0:T(8,128)S(1)} %bitcast.11), channel_id=1, source_target_pairs={{0,2},{1,3},{2,0},{3,1},{4,6},{5,7},{6,4},{7,5},{8,10},{9,11},{10,... | collective-permute-start | bytes 196616 | tf_op jit(solution)/shard_map/ppermute | solution.py:311
  14.4 2.4 %collective-permute-start.4 = (f32[136,128]{1,0:T(8,128)S(1)}, f32[136,128]{1,0:T(8,128)S(1)}, u32[]{:S(2)}, u32[]{:S(2)}) collective-permute-start(f32[136,128]{1,0:T(8,128)S(1)} %collective-permute-done.3.refs_3_), channel_id=1, source_target_pairs={{0,1},{1,0},{2,3},{3,2},{4,5},{5,4},{6,7},{7,6},{8,9},{9,8},{10,11... | collective-permute-start | bytes 208904 | tf_op jit(solution)/shard_map/ppermute | solution.py:311
  14.4 2.4 %collective-permute-start.2 = (f32[136,128]{1,0:T(8,128)S(1)}, f32[136,128]{1,0:T(8,128)S(1)}, u32[]{:S(2)}, u32[]{:S(2)}) collective-permute-start(f32[136,128]{1,0:T(8,128)S(1)} %collective-permute-done.1.refs_2_), channel_id=1, source_target_pairs={{0,1},{1,0},{2,3},{3,2},{4,5},{5,4},{6,7},{7,6},{8,9},{9,8},{10,11... | collective-permute-start | bytes 208904 | tf_op jit(solution)/shard_map/ppermute | solution.py:311
  19.5 6.9 %collective-permute-start.10 = (f32[56,512]{1,0:T(8,128)S(1)}, f32[56,512]{1,0:T(8,128)S(1)}, u32[]{:S(2)}, u32[]{:S(2)}) collective-permute-start(f32[56,512]{1,0:T(8,128)S(1)} %get-tuple-element.13), channel_id=1, source_target_pairs={{0,8},{8,16},{16,24},{24,0},{1,9},{9,17},{17,25},{25,1},{2,10},{10... | collective-permute-start | bytes 344072 | tf_op jit(solution)/shard_map/ppermute | solution.py:316
  21.0 6.6 %collective-permute-start.11 = (f32[56,512]{1,0:T(8,128)S(1)}, f32[56,512]{1,0:T(8,128)S(1)}, u32[]{:S(2)}, u32[]{:S(2)}) collective-permute-start(f32[56,512]{1,0:T(8,128)S(1)} %get-tuple-element.14), channel_id=1, source_target_pairs={{0,24},{8,0},{16,8},{24,16},{1,25},{9,1},{17,9},{25,17},{2,26},{10... | collective-permute-start | bytes 344072 | tf_op jit(solution)/shard_map/ppermute | solution.py:316
  22.5 3.9 %collective-permute-start.12 = (f32[8,512]{1,0:T(8,128)S(1)}, f32[8,512]{1,0:T(8,128)S(1)}, u32[]{:S(2)}, u32[]{:S(2)}) collective-permute-start(f32[8,512]{1,0:T(8,128)S(1)} %get-tuple-element.12.refs_3_), channel_id=1, source_target_pairs={{0,16},{8,24},{16,0},{24,8},{1,17},{9,25},{17,1},{25,9},{2,18},{10... | collective-permute-start | bytes 49160 | tf_op jit(solution)/shard_map/ppermute | solution.py:316
  28.7 1.3 %collective-permute-start.13 = (f32[32,512]{1,0:T(8,128)S(1)}, f32[32,512]{1,0:T(8,128)S(1)}, u32[]{:S(2)}, u32[]{:S(2)}) collective-permute-start(f32[32,512]{1,0:T(8,128)S(1)} %get-tuple-element.17), channel_id=1, source_target_pairs={{0,1},{1,0},{2,3},{3,2},{4,5},{5,4},{6,7},{7,6},{8,9},{9,8},{10,11... | collective-permute-start | bytes 196616 | tf_op jit(solution)/shard_map/ppermute | solution.py:311

commit v6 on v5

--- a/solution.py
+++ b/solution.py
@@ -84,19 +84,30 @@
         copy.wait()
 
 
-def edges_kernel(half, depth, *refs):
-    proj, measured, (up, down, sums) = refs[0], refs[1 : 1 + half], refs[1 + half :]
+def image_edges_kernel(half, depth, info, proj, first, second, sums):
+    width = proj.shape[2]
+    odd = jnp.broadcast_to(info[:1, :1] >= 2.0, (8, width))
     for j in range(half):
-        up[8 * j : 8 * j + 8, :] = proj[j, depth : depth + 8, :]
-        down[8 * j : 8 * j + 8, :] = proj[j, :8, :]
-        at = 8 * half + HALO * j
-        up[at : at + HALO, :] = measured[j][depth - HALO :, :]
-        down[at : at + HALO, :] = measured[j][:HALO, :]
+        up, down = proj[j, depth : depth + 8, :], proj[j, :8, :]
+        first[8 * j : 8 * j + 8, :] = jnp.where(odd, down, up)
+        second[8 * j : 8 * j + 8, :] = jnp.where(odd, up, down)
         sums[j : j + 1, :] = jnp.sum(proj[j], axis=0, keepdims=True)
+    first[8 * half :, :] = sums[...]
+    second[8 * half :, :] = sums[...]
+
+
+def measured_edges_kernel(half, depth, info, image_sums, *refs):
+    measured, (first, second, sums) = refs[:half], refs[half:]
+    width = sums.shape[1]
+    odd = jnp.broadcast_to(info[:1, :1] >= 2.0, (HALO, width))
+    sums[:half, :] = image_sums[...]
+    for j in range(half):
+        up, down = measured[j][depth - HALO :, :], measured[j][:HALO, :]
+        first[HALO * j : HALO * j + HALO, :] = jnp.where(odd, down, up)
+        second[HALO * j : HALO * j + HALO, :] = jnp.where(odd, up, down)
         sums[half + j : half + j + 1, :] = jnp.sum(measured[j][...], axis=0, keepdims=True)
-    at = (8 + HALO) * half
-    up[at:, :] = sums[...]
-    down[at:, :] = sums[...]
+    first[HALO * half :, :] = sums[half:, :]
+    second[HALO * half :, :] = sums[half:, :]
 
 
 def forward_kernel(half, depth, width, slabs, bands, swap, added, *refs):
@@ -117,7 +128,7 @@
     step = lax.broadcasted_iota(jnp.int32, (8, LANES), 0).astype(jnp.float32)
     place = lax.broadcasted_iota(jnp.int32, (rows, LANES), 0)
     wide_lane = lax.broadcasted_iota(jnp.int32, (rows, LANES), 1)
-    keep = info[...] > 0.0
+    keep = (info[...] == 1.0) | (info[...] == 3.0)
     together = images.shape[0]
 
     def gather(i, g, inverse, stride, start):
@@ -145,7 +156,7 @@
             images[i, g, at, :LANES], images[i, g, at, LANES:] = two_parts(pair)
             return point, point_l
 
-        lax.fori_loop(0, width // 16, sixteen, (start, start_l), unroll=8)
+        lax.fori_loop(0, width // 16, sixteen, (start, start_l), unroll=True)
 
     def some_angles(first, carry):
         tables, whole = [], []
@@ -188,7 +199,7 @@
         lax.fori_loop(0, half // together, some_angles, 0)
 
 
-def project_back(half, depth, width, swap, entries, held, out, stack, turned, images):
+def project_back(half, depth, width, swap, unroll, entries, held, out, stack, turned, images):
     tiles = width // LANES
     per = LANES // depth
     groups = half // per
@@ -259,38 +270,38 @@
             images[at, :LANES], images[at, LANES:] = two_parts(pair)
             return point, point_l
 
-        lax.fori_loop(0, width // 16, sixteen, (start, start_l), unroll=8)
+        lax.fori_loop(0, width // 16, sixteen, (start, start_l), unroll=unroll)
         total += lax.dot_general(select, images[...], NT, preferred_element_type=jnp.float32)
     out[...] = total * (1.0 / math.sqrt(2 * half))
 
 
 def residual_kernel(half, depth, width, slabs, *refs):
-    info, entries, proj, sums, from_below, from_above = refs[:6]
+    info, entries, proj, sums, first, second, first_m, second_m = refs[:8]
+    refs = refs[2:]
     others, measured = refs[6 : 6 + slabs - 3], refs[6 + slabs - 3 : 6 + slabs - 3 + half]
     residual, held, other, stack, turned, images, result, sem = refs[6 + slabs - 3 + half :]
     rows = depth + 2 * HALO
     tiles = width // LANES
-    edge = (8 + HALO) * half
-    column = sums[...] + from_below[edge:, :] + from_above[edge:, :]
+    image_sum = sums[:half, :] + first[8 * half :, :] + second[8 * half :, :]
+    measured_sum = sums[half:, :] + first_m[HALO * half :, :] + second_m[HALO * half :, :]
+    odd = jnp.broadcast_to(info[:1, :1] >= 2.0, (8, LANES))
     for ref in others:
-        column += ref[...]
-    keep = info[...] > 0.0
+        image_sum += ref[:half, :]
+        measured_sum += ref[half:, :]
+    keep = (info[...] == 1.0) | (info[...] == 3.0)
     for j in range(half):
-        at = 8 * half + HALO * j
+        at = HALO * j
         for tile in range(tiles):
             part = slice(tile * LANES, (tile + 1) * LANES)
+            one, two = first[8 * j : 8 * j + 8, part], second[8 * j : 8 * j + 8, part]
+            below, above = jnp.where(odd, one, two), jnp.where(odd, two, one)
             image = jnp.concatenate(
-                [
-                    proj[j, :8, part] + from_below[8 * j : 8 * j + 8, part],
-                    proj[j, 8:depth, part],
-                    proj[j, depth:, part] + from_above[8 * j : 8 * j + 8, part],
-                ],
-                axis=0,
+                [proj[j, :8, part] + below, proj[j, 8:depth, part], proj[j, depth:, part] + above], axis=0
             )
-            wanted = jnp.concatenate(
-                [from_below[at : at + HALO, part], measured[j][:, part], from_above[at : at + HALO, part]], axis=0
-            )
-            gain = column[half + j : half + j + 1, part] / column[j : j + 1, part]
+            one, two = first_m[at : at + HALO, part], second_m[at : at + HALO, part]
+            below, above = jnp.where(odd[:HALO], one, two), jnp.where(odd[:HALO], two, one)
+            wanted = jnp.concatenate([below, measured[j][:, part], above], axis=0)
+            gain = measured_sum[j : j + 1, part] / image_sum[j : j + 1, part]
             value = jnp.where(keep, (wanted - gain * image) * (1.0 / (2 * half)), 0.0)
             if j == 0:
                 result[:, part] = value[HALO : HALO + depth, :]
@@ -298,12 +309,12 @@
         if j == 0:
             copy = pltpu.make_async_copy(result, residual, sem)
             copy.start()
-    project_back(half, depth, width, 1, entries, held, other, stack, turned, images)
+    project_back(half, depth, width, 1, 8, entries, held, other, stack, turned, images)
     copy.wait()
 
 
 def own_kernel(half, depth, width, entries, held, out, stack, turned, images):
-    project_back(half, depth, width, 0, entries, held, out, stack, turned, images)
+    project_back(half, depth, width, 0, width // 16, entries, held, out, stack, turned, images)
 
 
 def swapped(x, by):
@@ -314,6 +325,11 @@
 def from_slab(x, by):
     n = lax.axis_size("zslab")
     return lax.ppermute(x, "zslab", [(i, (i + by) % n) for i in range(n)])
+
+
+def between(x, odd):
+    n = lax.axis_size("zslab")
+    return lax.ppermute(x, "zslab", [(i, (i + (1 if i % 2 == odd else -1)) % n) for i in range(n)])
 
 
 def shards(volume, measured, magnification, shift_y, shift_z):
@@ -324,7 +340,8 @@
     tiles = width // LANES
     f32, bf16 = jnp.float32, jnp.bfloat16
     place = jnp.full((1, 1), lax.axis_index("xband"), jnp.int32)
-    info = jnp.where(inside((rows, LANES), depth, lax.axis_index("zslab"), slabs), 1.0, 0.0).astype(f32)
+    slab = lax.axis_index("zslab")
+    info = jnp.where(inside((rows, LANES), depth, slab, slabs), 1.0, 0.0).astype(f32) + 2.0 * ((slab + 1) % 2).astype(f32)
 
     vmem = pl.BlockSpec(memory_space=pltpu.VMEM)
     params = pltpu.CompilerParams(vmem_limit_bytes=VMEM_LIMIT)
@@ -379,13 +396,16 @@
         )
 
     proj = forward(theirs, 1, [forward(mine, 0, [])])
-    edge_rows = (8 + HALO + 2) * half
-    up, down, sums = on_core(
-        functools.partial(edges_kernel, half, depth),
-        [(edge_rows, width), (edge_rows, width), (2 * half, width)],
-        [proj] + views,
-    )
-    below, above = from_slab(up, 1), from_slab(down, -1)
+    first, second, image_sums = on_core(
+        functools.partial(image_edges_kernel, half, depth), [(9 * half, width)] * 2 + [(half, width)], [info, proj]
+    )
+    first, second = between(first, 1), between(second, 0)
+    first_m, second_m, sums = on_core(
+        functools.partial(measured_edges_kernel, half, depth),
+        [((HALO + 1) * half, width)] * 2 + [(2 * half, width)],
+        [info, image_sums] + views,
+    )
+    first_m, second_m = between(first_m, 1), between(second_m, 0)
     others = [from_slab(sums, k) for k in range(2, slabs - 1)]
 
     scratch = [
@@ -396,7 +416,7 @@
     residual, held, other = on_core(
         functools.partial(residual_kernel, half, depth, width, slabs),
         [(depth, width), (half, tiles, rows, LANES), (depth, width)],
-        [info, theirs[0], proj, sums, below, above] + others + views,
+        [info, theirs[0], proj, sums, first, second, first_m, second_m] + others + views,
         scratch + [pltpu.VMEM((depth, width), f32), pltpu.SemaphoreType.DMA],
         out_spaces={0: pl.BlockSpec(memory_space=pl.ANY)},
     )

time: 30.8 us -> 30.6 us (level)
  starting transfers between devices: 16 us -> 18.1 us
  waiting for transfers between devices: 6.43 us -> 4.84 us
  Pallas kernels: 6.81 us -> 6.01 us
    ppermute x0 -> x4, starting transfers between devices: none -> 5.08 us  [between(): lax.ppermute(x, 'zslab', [(i, (i + (1 if i % 2 == odd else -1)) % n) for...]
    ppermute x3 -> x1, starting transfers between devices: 4.49 us -> 1.52 us  [from_slab(): return lax.ppermute(x, 'zslab', [(i, (i + by) % n) for i in range(n)])]
    ppermute x3 -> x1, waiting for transfers between devices: 3.67 us -> 2.24 us  [from_slab(): return lax.ppermute(x, 'zslab', [(i, (i + by) % n) for i in range(n)])]
    pallas_call x6 -> x7, Pallas kernels: 6.81 us -> 6.01 us  [on_core(): pl.pallas_call(body, out_shape=[jax.ShapeDtypeStruct(shape, f32) for shap...]
    ppermute x11, waiting for transfers between devices: 2.76 us -> 2.19 us  [swapped(): return lax.ppermute(x, 'xband', [(i, i ^ by) for i in range(n)])]
    ppermute x0 -> x4, waiting for transfers between devices: none -> 0.41 us  [between(): lax.ppermute(x, 'zslab', [(i, (i + (1 if i % 2 == odd else -1)) % n) for...]
  transfers between devices with their start and end apart: 14 -> 16, of which waited for: 6 -> 4; matrix products, arithmetic and copies ran while one was open for 0% -> 0% of each run, Pallas kernels for 15% -> 13%
where the time goes in v6:
time: 30.6 us; the launch traced here: 30.4 us
  starting transfers between devices  18.1 us (59%)
  Pallas kernels  6.01 us (20%)
  waiting for transfers between devices  4.84 us (16%)
  between operations  0.72 us (2%)
  other arithmetic  0.65 us (2%)
    ppermute x11, starting transfers between devices, swapped(): return lax.ppermute(x, 'xband', [(i, i ^ by) for i in range(n)])  11.5 us
    pallas_call x7, Pallas kernels, on_core(): pl.pallas_call(body, out_shape=[jax.ShapeDtypeStruct(shape, f32) for shap...  6.01 us
    ppermute x4, starting transfers between devices, between(): lax.ppermute(x, 'zslab', [(i, (i + (1 if i % 2 == odd else -1)) % n) for...  5.08 us
    ppermute x1, waiting for transfers between devices, from_slab(): return lax.ppermute(x, 'zslab', [(i, (i + by) % n) for i in range(n)])  2.24 us
    ppermute x11, waiting for transfers between devices, swapped(): return lax.ppermute(x, 'xband', [(i, i ^ by) for i in range(n)])  2.19 us
    ppermute x1, starting transfers between devices, from_slab(): return lax.ppermute(x, 'zslab', [(i, (i + by) % n) for i in range(n)])  1.52 us
    broadcast_in_dim x1, other arithmetic, shards(): return (residual[None], (own + from_other)[None])  0.64 us
  transfers between devices with their start and end apart: 16, of which 4 were waited for; matrix products, arithmetic and copies ran while one was open for 0% of the time, Pallas kernels for 13%

profile of v6, /device:TPU:0, one launch (start us, length us, event | category | flops | bytes accessed | tf_op | source)
XLA Modules:
  0.0 30.4 jit_solution(16108088234847759839)
XLA Ops:
  0.6 0.9 %shard_map.68.refs_1_.entries = f32[136,128]{1,0:T(8,128)S(1)} custom-call(f32[32,512]{1,0:T(8,128)} %bitcast.14, f32[1,8]{1,0:T(1,128)} %bitcast.15, s32[1,8]{1,0:T(1,128)} %bitcast.16, s32[1,8]{1,0:T(1,128)} %bitcast.17, s32[1,1]{1,0:T(1,128)} %bitcast.5.refs_3_), custom_call_target="tpu_custom_call" | custom-call | tf_op jit(solution)/shard_map/pallas_call | solution.py:350
  1.6 5.1 %collective-permute-start.5 = (f32[136,128]{1,0:T(8,128)S(1)}, f32[136,128]{1,0:T(8,128)S(1)}, u32[]{:S(2)}, u32[]{:S(2)}) collective-permute-start(f32[136,128]{1,0:T(8,128)S(1)} %shard_map.68.refs_1_.entries), channel_id=1, source_target_pairs={{0,6},{1,7},{2,4},{3,5},{4,2},{5,3},{6,0},{7,1},{8,14},{9,15},{10,... | collective-permute-start | bytes 208904 | tf_op jit(solution)/shard_map/ppermute | solution.py:322
  6.7 0.7 %collective-permute-start.1 = (f32[136,128]{1,0:T(8,128)S(1)}, f32[136,128]{1,0:T(8,128)S(1)}, u32[]{:S(2)}, u32[]{:S(2)}) collective-permute-start(f32[136,128]{1,0:T(8,128)S(1)} %shard_map.68.refs_1_.entries), channel_id=1, source_target_pairs={{0,2},{1,3},{2,0},{3,1},{4,6},{5,7},{6,4},{7,5},{8,10},{9,11},{10,... | collective-permute-start | bytes 208904 | tf_op jit(solution)/shard_map/ppermute | solution.py:322
  7.4 1.9 %collective-permute-done.5.refs_4_ = f32[136,128]{1,0:T(8,128)S(1)} collective-permute-done((f32[136,128]{1,0:T(8,128)S(1)}, f32[136,128]{1,0:T(8,128)S(1)}, u32[]{:S(2)}, u32[]{:S(2)}) %collective-permute-start.5) | collective-permute-done | bytes 69664 | tf_op jit(solution)/shard_map/ppermute | solution.py:322
  9.3 4.4 %collective-permute-start.9 = (f32[32,512]{1,0:T(8,128)S(1)}, f32[32,512]{1,0:T(8,128)S(1)}, u32[]{:S(2)}, u32[]{:S(2)}) collective-permute-start(f32[32,512]{1,0:T(8,128)S(1)} %bitcast.9), channel_id=1, source_target_pairs={{0,6},{1,7},{2,4},{3,5},{4,2},{5,3},{6,0},{7,1},{8,14},{9,15},{10,... | collective-permute-start | bytes 196616 | tf_op jit(solution)/shard_map/ppermute | solution.py:322
  13.7 0.0 collective-permute-done.3.refs_3_
  13.7 0.6 %collective-permute-start.7 = (f32[32,512]{1,0:T(8,128)S(1)}, f32[32,512]{1,0:T(8,128)S(1)}, u32[]{:S(2)}, u32[]{:S(2)}) collective-permute-start(f32[32,512]{1,0:T(8,128)S(1)} %bitcast.11), channel_id=1, source_target_pairs={{0,2},{1,3},{2,0},{3,1},{4,6},{5,7},{6,4},{7,5},{8,10},{9,11},{10,... | collective-permute-start | bytes 196616 | tf_op jit(solution)/shard_map/ppermute | solution.py:322
  14.4 0.0 collective-permute-done.6.refs_4_
  14.4 0.5 %collective-permute-start.2 = (f32[136,128]{1,0:T(8,128)S(1)}, f32[136,128]{1,0:T(8,128)S(1)}, u32[]{:S(2)}, u32[]{:S(2)}) collective-permute-start(f32[136,128]{1,0:T(8,128)S(1)} %collective-permute-done.1.refs_2_), channel_id=1, source_target_pairs={{0,1},{1,0},{2,3},{3,2},{4,5},{5,4},{6,7},{7,6},{8,9},{9,8},{10,11... | collective-permute-start | bytes 208904 | tf_op jit(solution)/shard_map/ppermute | solution.py:322
  14.9 0.1 iota.10.refs_0_.info
  15.0 1.5 %shard_map.69.refs_5_ = f32[4,40,512]{2,1,0:T(8,128)S(1)} custom-call(f32[40,128]{1,0:T(8,128)S(1)} %iota.10.refs_0_.info, f32[136,128]{1,0:T(8,128)S(1)} %shard_map.68.refs_1_.entries, f32[136,128]{1,0:T(8,128)S(1)} %collective-permute-done.1.refs_2_, f32[136,128]{1,0:T(8,128)S(1)} %collective-permute-done.3.refs_3_, ...), custom_call_target="tpu_custom_call" | custom-call | tf_op jit(solution)/shard_map/pallas_call | solution.py:350
  16.5 0.0 collective-permute-done.4.refs_3_
  16.5 0.0 collective-permute-done.2.refs_2_
  16.5 1.5 %shard_map.70.proj.refs_2_ = f32[4,40,512]{2,1,0:T(8,128)S(1)} custom-call(f32[40,128]{1,0:T(8,128)S(1)} %iota.10.refs_0_.info, f32[136,128]{1,0:T(8,128)S(1)} %collective-permute-done.refs_1_, f32[136,128]{1,0:T(8,128)S(1)} %collective-permute-done.2.refs_2_, f32[136,128]{1,0:T(8,128)S(1)} %collective-permute-done.4.refs_3_, ...), custom_call_target="tpu_custom_call" | custom-call | tf_op jit(solution)/shard_map/pallas_call | solution.py:350
  17.9 0.1 shard_map.71
  18.0 2.5 %collective-permute-start.10 = (f32[36,512]{1,0:T(8,128)S(1)}, f32[36,512]{1,0:T(8,128)S(1)}, u32[]{:S(2)}, u32[]{:S(2)}) collective-permute-start(f32[36,512]{1,0:T(8,128)S(1)} %get-tuple-element.17), channel_id=1, source_target_pairs={{0,24},{8,16},{16,8},{24,0},{1,25},{9,17},{17,9},{25,1},{2,26},{10... | collective-permute-start | bytes 221192 | tf_op jit(solution)/shard_map/ppermute | solution.py:332
  20.5 0.5 %collective-permute-start.11 = (f32[36,512]{1,0:T(8,128)S(1)}, f32[36,512]{1,0:T(8,128)S(1)}, u32[]{:S(2)}, u32[]{:S(2)}) collective-permute-start(f32[36,512]{1,0:T(8,128)S(1)} %get-tuple-element.18), channel_id=1, source_target_pairs={{0,8},{8,0},{16,24},{24,16},{1,9},{9,1},{17,25},{25,17},{2,10},{10... | collective-permute-start | bytes 221192 | tf_op jit(solution)/shard_map/ppermute | solution.py:332
  21.1 0.0 collective-permute-done.9.refs_3_.refs_12_
  21.1 0.0 collective-permute-done.8.refs_2_.refs_11_
  21.1 0.1 shard_map.72
  21.1 1.5 %collective-permute-start.12 = (f32[20,512]{1,0:T(8,128)S(1)}, f32[20,512]{1,0:T(8,128)S(1)}, u32[]{:S(2)}, u32[]{:S(2)}) collective-permute-start(f32[20,512]{1,0:T(8,128)S(1)} %get-tuple-element.19), channel_id=1, source_target_pairs={{0,24},{8,16},{16,8},{24,0},{1,25},{9,17},{17,9},{25,1},{2,26},{10... | collective-permute-start | bytes 122888 | tf_op jit(solution)/shard_map/ppermute | solution.py:332
  22.6 0.5 %collective-permute-start.13 = (f32[20,512]{1,0:T(8,128)S(1)}, f32[20,512]{1,0:T(8,128)S(1)}, u32[]{:S(2)}, u32[]{:S(2)}) collective-permute-start(f32[20,512]{1,0:T(8,128)S(1)} %get-tuple-element.20), channel_id=1, source_target_pairs={{0,8},{8,0},{16,24},{24,16},{1,9},{9,1},{17,25},{25,17},{2,10},{10... | collective-permute-start | bytes 122888 | tf_op jit(solution)/shard_map/ppermute | solution.py:332
  23.2 1.5 %collective-permute-start.14 = (f32[8,512]{1,0:T(8,128)S(1)}, f32[8,512]{1,0:T(8,128)S(1)}, u32[]{:S(2)}, u32[]{:S(2)}) collective-permute-start(f32[8,512]{1,0:T(8,128)S(1)} %get-tuple-element.16.refs_3_), channel_id=1, source_target_pairs={{0,16},{8,24},{16,0},{24,8},{1,17},{9,25},{17,1},{25,9},{2,18},{10... | collective-permute-start | bytes 49160 | tf_op jit(solution)/shard_map/ppermute | solution.py:327
  24.7 2.2 %collective-permute-done.14.refs_8_ = f32[8,512]{1,0:T(8,128)S(1)} collective-permute-done((f32[8,512]{1,0:T(8,128)S(1)}, f32[8,512]{1,0:T(8,128)S(1)}, u32[]{:S(2)}, u32[]{:S(2)}) %collective-permute-start.14) | collective-permute-done | bytes 16416 | tf_op jit(solution)/shard_map/ppermute | solution.py:327
  26.9 0.0 collective-permute-done.12.refs_6_
  26.9 0.4 %collective-permute-done.13.refs_7_ = f32[20,512]{1,0:T(8,128)S(1)} collective-permute-done((f32[20,512]{1,0:T(8,128)S(1)}, f32[20,512]{1,0:T(8,128)S(1)}, u32[]{:S(2)}, u32[]{:S(2)}) %collective-permute-start.13) | collective-permute-done | bytes 40992 | tf_op jit(solution)/shard_map/ppermute | solution.py:332
  27.3 0.0 collective-permute-done.10.refs_4_
  27.3 1.1 %shard_map.73 = (f32[32,512]{1,0:T(8,128)}, f32[4,4,40,128]{3,2,1,0:T(8,128)S(1)}, f32[32,512]{1,0:T(8,128)S(1)}) custom-call(f32[40,128]{1,0:T(8,128)S(1)} %iota.10.refs_0_.info, f32[136,128]{1,0:T(8,128)S(1)} %collective-permute-done.refs_1_, f32[4,40,512]{2,1,0:T(8,128)S(1)} %shard_map.70.proj.refs_2_, f32[8,512]{1,0:T(8,128)S(1)} %get-tuple-element.16.refs_3_, ...), custom_call_target="tpu_custom_call" | custom-call | tf_op jit(solution)/shard_map/pallas_call | solution.py:350
  28.4 0.1 collective-permute-start.15
  28.5 0.9 %shard_map.74 = f32[32,512]{1,0:T(8,128)S(1)} custom-call(f32[136,128]{1,0:T(8,128)S(1)} %shard_map.68.refs_1_.entries, f32[4,4,40,128]{3,2,1,0:T(8,128)S(1)} %get-tuple-element.22.held), custom_call_target="tpu_custom_call" | custom-call | tf_op jit(solution)/shard_map/pallas_call | solution.py:350
  29.4 0.3 %collective-permute-done.15 = f32[32,512]{1,0:T(8,128)S(1)} collective-permute-done((f32[32,512]{1,0:T(8,128)S(1)}, f32[32,512]{1,0:T(8,128)S(1)}, u32[]{:S(2)}, u32[]{:S(2)}) %collective-permute-start.15) | collective-permute-done | bytes 65568 | tf_op jit(solution)/shard_map/ppermute | solution.py:322
  29.8 0.6 %add_bitcast_fusion = f32[1,32,512]{2,1,0:T(8,128)} fusion(f32[32,512]{1,0:T(8,128)S(1)} %shard_map.74, f32[32,512]{1,0:T(8,128)S(1)} %collective-permute-done.15), kind=kLoop, calls=%fused_computation | loop fusion | flops 16384 | bytes 196608 | tf_op jit(solution)/shard_map/broadcast_in_dim | solution.py:427
  (12 shorter events, 0.0 us)
Async XLA Ops:
  0.6 8.6 %copy-start = (f32[1,32,512]{2,1,0:T(8,128)S(1)}, f32[1,32,512]{2,1,0:T(8,128)}, u32[]{:S(2)}) copy-start(f32[1,32,512]{2,1,0:T(8,128)} %param.6) | copy-start | bytes 196612
  1.6 7.7 %collective-permute-start.5 = (f32[136,128]{1,0:T(8,128)S(1)}, f32[136,128]{1,0:T(8,128)S(1)}, u32[]{:S(2)}, u32[]{:S(2)}) collective-permute-start(f32[136,128]{1,0:T(8,128)S(1)} %shard_map.68.refs_1_.entries), channel_id=1, source_target_pairs={{0,6},{1,7},{2,4},{3,5},{4,2},{5,3},{6,0},{7,1},{8,14},{9,15},{10,... | collective-permute-start | bytes 208904 | tf_op jit(solution)/shard_map/ppermute | solution.py:322
  6.7 2.6 %collective-permute-start = (f32[136,128]{1,0:T(8,128)S(1)}, f32[136,128]{1,0:T(8,128)S(1)}, u32[]{:S(2)}, u32[]{:S(2)}) collective-permute-start(f32[136,128]{1,0:T(8,128)S(1)} %shard_map.68.refs_1_.entries), channel_id=1, source_target_pairs={{0,1},{1,0},{2,3},{3,2},{4,5},{5,4},{6,7},{7,6},{8,9},{9,8},{10,11... | collective-permute-start | bytes 208904 | tf_op jit(solution)/shard_map/ppermute | solution.py:322
  6.7 7.0 %collective-permute-start.3 = (f32[136,128]{1,0:T(8,128)S(1)}, f32[136,128]{1,0:T(8,128)S(1)}, u32[]{:S(2)}, u32[]{:S(2)}) collective-permute-start(f32[136,128]{1,0:T(8,128)S(1)} %shard_map.68.refs_1_.entries), channel_id=1, source_target_pairs={{0,4},{1,5},{2,6},{3,7},{4,0},{5,1},{6,2},{7,3},{8,12},{9,13},{10,... | collective-permute-start | bytes 208904 | tf_op jit(solution)/shard_map/ppermute | solution.py:322
  6.7 7.7 %collective-permute-start.1 = (f32[136,128]{1,0:T(8,128)S(1)}, f32[136,128]{1,0:T(8,128)S(1)}, u32[]{:S(2)}, u32[]{:S(2)}) collective-permute-start(f32[136,128]{1,0:T(8,128)S(1)} %shard_map.68.refs_1_.entries), channel_id=1, source_target_pairs={{0,2},{1,3},{2,0},{3,1},{4,6},{5,7},{6,4},{7,5},{8,10},{9,11},{10,... | collective-permute-start | bytes 208904 | tf_op jit(solution)/shard_map/ppermute | solution.py:322
  9.3 5.1 %collective-permute-start.6 = (f32[136,128]{1,0:T(8,128)S(1)}, f32[136,128]{1,0:T(8,128)S(1)}, u32[]{:S(2)}, u32[]{:S(2)}) collective-permute-start(f32[136,128]{1,0:T(8,128)S(1)} %collective-permute-done.5.refs_4_), channel_id=1, source_target_pairs={{0,1},{1,0},{2,3},{3,2},{4,5},{5,4},{6,7},{7,6},{8,9},{9,8},{10,11... | collective-permute-start | bytes 208904 | tf_op jit(solution)/shard_map/ppermute | solution.py:322
  9.3 11.8 %collective-permute-start.9 = (f32[32,512]{1,0:T(8,128)S(1)}, f32[32,512]{1,0:T(8,128)S(1)}, u32[]{:S(2)}, u32[]{:S(2)}) collective-permute-start(f32[32,512]{1,0:T(8,128)S(1)} %bitcast.9), channel_id=1, source_target_pairs={{0,6},{1,7},{2,4},{3,5},{4,2},{5,3},{6,0},{7,1},{8,14},{9,15},{10,... | collective-permute-start | bytes 196616 | tf_op jit(solution)/shard_map/ppermute | solution.py:322
  13.7 7.3 %collective-permute-start.8 = (f32[32,512]{1,0:T(8,128)S(1)}, f32[32,512]{1,0:T(8,128)S(1)}, u32[]{:S(2)}, u32[]{:S(2)}) collective-permute-start(f32[32,512]{1,0:T(8,128)S(1)} %bitcast.10), channel_id=1, source_target_pairs={{0,4},{1,5},{2,6},{3,7},{4,0},{5,1},{6,2},{7,3},{8,12},{9,13},{10,... | collective-permute-start | bytes 196616 | tf_op jit(solution)/shard_map/ppermute | solution.py:322
  13.7 7.3 %collective-permute-start.7 = (f32[32,512]{1,0:T(8,128)S(1)}, f32[32,512]{1,0:T(8,128)S(1)}, u32[]{:S(2)}, u32[]{:S(2)}) collective-permute-start(f32[32,512]{1,0:T(8,128)S(1)} %bitcast.11), channel_id=1, source_target_pairs={{0,2},{1,3},{2,0},{3,1},{4,6},{5,7},{6,4},{7,5},{8,10},{9,11},{10,... | collective-permute-start | bytes 196616 | tf_op jit(solution)/shard_map/ppermute | solution.py:322
  14.4 2.1 %collective-permute-start.4 = (f32[136,128]{1,0:T(8,128)S(1)}, f32[136,128]{1,0:T(8,128)S(1)}, u32[]{:S(2)}, u32[]{:S(2)}) collective-permute-start(f32[136,128]{1,0:T(8,128)S(1)} %collective-permute-done.3.refs_3_), channel_id=1, source_target_pairs={{0,1},{1,0},{2,3},{3,2},{4,5},{5,4},{6,7},{7,6},{8,9},{9,8},{10,11... | collective-permute-start | bytes 208904 | tf_op jit(solution)/shard_map/ppermute | solution.py:322
  14.4 2.1 %collective-permute-start.2 = (f32[136,128]{1,0:T(8,128)S(1)}, f32[136,128]{1,0:T(8,128)S(1)}, u32[]{:S(2)}, u32[]{:S(2)}) collective-permute-start(f32[136,128]{1,0:T(8,128)S(1)} %collective-permute-done.1.refs_2_), channel_id=1, source_target_pairs={{0,1},{1,0},{2,3},{3,2},{4,5},{5,4},{6,7},{7,6},{8,9},{9,8},{10,11... | collective-permute-start | bytes 208904 | tf_op jit(solution)/shard_map/ppermute | solution.py:322
  18.0 9.3 %collective-permute-start.10 = (f32[36,512]{1,0:T(8,128)S(1)}, f32[36,512]{1,0:T(8,128)S(1)}, u32[]{:S(2)}, u32[]{:S(2)}) collective-permute-start(f32[36,512]{1,0:T(8,128)S(1)} %get-tuple-element.17), channel_id=1, source_target_pairs={{0,24},{8,16},{16,8},{24,0},{1,25},{9,17},{17,9},{25,1},{2,26},{10... | collective-permute-start | bytes 221192 | tf_op jit(solution)/shard_map/ppermute | solution.py:332
  20.5 6.8 %collective-permute-start.11 = (f32[36,512]{1,0:T(8,128)S(1)}, f32[36,512]{1,0:T(8,128)S(1)}, u32[]{:S(2)}, u32[]{:S(2)}) collective-permute-start(f32[36,512]{1,0:T(8,128)S(1)} %get-tuple-element.18), channel_id=1, source_target_pairs={{0,8},{8,0},{16,24},{24,16},{1,9},{9,1},{17,25},{25,17},{2,10},{10... | collective-permute-start | bytes 221192 | tf_op jit(solution)/shard_map/ppermute | solution.py:332
  21.1 5.8 %collective-permute-start.12 = (f32[20,512]{1,0:T(8,128)S(1)}, f32[20,512]{1,0:T(8,128)S(1)}, u32[]{:S(2)}, u32[]{:S(2)}) collective-permute-start(f32[20,512]{1,0:T(8,128)S(1)} %get-tuple-element.19), channel_id=1, source_target_pairs={{0,24},{8,16},{16,8},{24,0},{1,25},{9,17},{17,9},{25,1},{2,26},{10... | collective-permute-start | bytes 122888 | tf_op jit(solution)/shard_map/ppermute | solution.py:332
  22.6 4.7 %collective-permute-start.13 = (f32[20,512]{1,0:T(8,128)S(1)}, f32[20,512]{1,0:T(8,128)S(1)}, u32[]{:S(2)}, u32[]{:S(2)}) collective-permute-start(f32[20,512]{1,0:T(8,128)S(1)} %get-tuple-element.20), channel_id=1, source_target_pairs={{0,8},{8,0},{16,24},{24,16},{1,9},{9,1},{17,25},{25,17},{2,10},{10... | collective-permute-start | bytes 122888 | tf_op jit(solution)/shard_map/ppermute | solution.py:332
  23.2 3.8 %collective-permute-start.14 = (f32[8,512]{1,0:T(8,128)S(1)}, f32[8,512]{1,0:T(8,128)S(1)}, u32[]{:S(2)}, u32[]{:S(2)}) collective-permute-start(f32[8,512]{1,0:T(8,128)S(1)} %get-tuple-element.16.refs_3_), channel_id=1, source_target_pairs={{0,16},{8,24},{16,0},{24,8},{1,17},{9,25},{17,1},{25,9},{2,18},{10... | collective-permute-start | bytes 49160 | tf_op jit(solution)/shard_map/ppermute | solution.py:327
  28.4 1.3 %collective-permute-start.15 = (f32[32,512]{1,0:T(8,128)S(1)}, f32[32,512]{1,0:T(8,128)S(1)}, u32[]{:S(2)}, u32[]{:S(2)}) collective-permute-start(f32[32,512]{1,0:T(8,128)S(1)} %get-tuple-element.23), channel_id=1, source_target_pairs={{0,1},{1,0},{2,3},{3,2},{4,5},{5,4},{6,7},{7,6},{8,9},{9,8},{10,11... | collective-permute-start | bytes 196616 | tf_op jit(solution)/shard_map/ppermute | solution.py:322
